TPU v7x, 128 devices: a whole 4x4x4 slice. The times are simulated.
128 devices in a mesh: row: 8 (over y, z_lo), col: 16 (over x, z_hi, core).
Axes of the slice: x: 4, y: 4, z: 4 (z_hi: 2, z_lo: 2; z = z_hi * 2 + z_lo), core: 2. Of those that a mesh axis runs over, the one named last changes fastest.
Arguments:
- vectors: bfloat16 [16384, 256], P(('row', 'col')), may hold values from -6 to 6
- blocks: bfloat16 [8, 16, 256, 128, 128], P('row', 'col'), may hold values from -0.03125 to 0.03125
- block_rows: int32 [8, 16, 256], P('row', 'col'), may hold values from 0 to 15
- block_cols: int32 [8, 16, 256], P('row', 'col'), may hold values from 0 to 7
- counts: int32 [8, 16], P('row', 'col'), may hold values from 1 to 256, as said below
Outputs:
- filtered: bfloat16 [16384, 256], P(('row', 'col'))
- gram: float32 [256, 256], P(('row', 'col'))
Inputs may be any that keep to these rules, and one draw needn't show every extreme that they name: Entries of a tile at positions counts[r, c] and beyond are padding; some tile stores exactly 256 blocks.
All inputs are finite; a program needn't handle non-finite values.
Results may differ from a plain program's by a relative error of at most 0.017.
Values may be sent and summed in bfloat16 or wider, within the bound.
No kernel may reach another device: no remote copies, remote signals or barrier semaphores. Data moves between devices by JAX's collectives and lax.ppermute only.
A program may use at most 64 MiB of HBM per device.

v0:
```python
import math

import jax
import jax.numpy as jnp
from jax import lax
from jax.sharding import PartitionSpec as P

BLOCK = 128
BR = 16
MAXB = 256
DEG = 3


def per_device(vectors, blocks, block_rows, block_cols, counts):
    col_count = lax.axis_size("col")
    shard_rows, vec_width = vectors.shape
    run_count = shard_rows // (8 * col_count)
    tile_blocks = blocks[0, 0]
    tile_rows = block_rows[0, 0]
    tile_cols = block_cols[0, 0]
    stored = counts[0, 0]
    entry_group = math.gcd(64, MAXB)

    def recurrence(summed, previous, degree):
        if degree == 0:
            return summed.astype(jnp.bfloat16)
        return (2.0 * summed - previous.astype(jnp.float32)).astype(jnp.bfloat16)

    previous = vectors
    current = vectors
    for degree in range(DEG):
        dealt_panel = lax.all_to_all(
            current.reshape(run_count, col_count, 8, vec_width),
            "col",
            split_axis=1,
            concat_axis=0,
            tiled=True,
        )
        dealt_panel = dealt_panel.reshape(shard_rows, vec_width)
        gathered = lax.all_gather(dealt_panel, "row", axis=0, tiled=True)
        column_blocks = gathered.reshape(-1, BLOCK, vec_width)

        def add_group(group_index, accumulated):
            offset = group_index * entry_group
            part_blocks = lax.dynamic_slice_in_dim(tile_blocks, offset, entry_group, 0)
            part_rows = lax.dynamic_slice_in_dim(tile_rows, offset, entry_group, 0)
            part_cols = lax.dynamic_slice_in_dim(tile_cols, offset, entry_group, 0)
            pieces = jnp.take(column_blocks, part_cols, axis=0)
            products = jnp.einsum(
                "eab,ebk->eak", part_blocks, pieces, preferred_element_type=jnp.float32
            )
            active_entries = offset + jnp.arange(entry_group, dtype=jnp.int32) < stored
            products = jnp.where(active_entries[:, None, None], products, 0.0)
            return accumulated.at[part_rows].add(products)

        loop_turns = (stored + entry_group - 1) // entry_group
        initial = jnp.zeros((BR, BLOCK, vec_width), jnp.float32)
        tile_summed = lax.fori_loop(0, loop_turns, add_group, initial)
        summed = lax.psum_scatter(
            tile_summed.reshape(BR * BLOCK, vec_width).astype(jnp.bfloat16),
            "col",
            scatter_dimension=0,
            tiled=True,
        ).astype(jnp.float32)
        updated = recurrence(summed, previous, degree)
        previous, current = (current, updated)
    local_gram = jnp.dot(current.T, current, preferred_element_type=jnp.float32)
    gram = lax.psum_scatter(local_gram, ("row", "col"), scatter_dimension=0, tiled=True) / (
        BR * BLOCK // col_count
    )
    return (current, gram)


def solution(mesh):
    in_specs = (
        P(("row", "col"), None),
        P("row", "col", None, None, None),
        P("row", "col", None),
        P("row", "col", None),
        P("row", "col"),
    )
    out_specs = (P(("row", "col"), None), P(("row", "col"), None))
    return jax.shard_map(
        per_device, mesh=mesh, in_specs=in_specs, out_specs=out_specs, check_vma=False
    )
```

profile of v0, /device:TPU:1, one launch (start us, length us, event | category | flops | bytes accessed | tf_op | source)
XLA Modules:
  0.0 765.6 jit_solution(3692057470771155155)
XLA Ops:
  7.2 9.1 %all-to-all-start = ((bf16[1,16,8,256]{3,2,0,1:T(8,128)(2,1)}), bf16[1,16,8,256]{3,2,0,1:T(8,128)(2,1)S(1)}, u32[]{:S(2)}, u32[]{:S(2)}) async-start(bf16[1,16,8,256]{3,2,0,1:T(8,128)(2,1)} %bitcast.27), calls=%async_computation | async-start | bytes 131072 | tf_op jit(solution)/shard_map/all_to_all | solution.py:32
  17.0 6.7 all-to-all-done
  23.7 23.4 %all_gather.9 = bf16[1024,256]{1,0:T(8,128)(2,1)S(1)} all-gather(bf16[128,256]{1,0:T(8,128)(2,1)S(1)} %bitcast.29), channel_id=1, replica_groups=mesh['row'=8,'col'=16] {'row'}, dimensions={0}, use_global_device_ids=true | all-gather | bytes 589824 | tf_op jit(solution)/shard_map/all_gather | solution.py:40
  47.3 96.5 %while.30 = (s32[]{:T(128)}, f32[16,128,256]{2,1,0:T(8,128)S(1)}, s32[]{:T(128)}, s32[256]{0:T(256)}, s32[]{:T(128)}, /*index=5*/bf16[256,128,128]{2,1,0:T(8,128...) while((s32[]{:T(128)}, f32[16,128,256]{2,1,0:T(8,128)S(1)}, ...), condition=%wide.region_2.4_spmd, body=%wide.region_0.3_spmd.sunk | while | flops 543164096 | bytes 48244944 | solution.py:58
  47.3 1.4 compare_and_fusion.6
  48.7 2.8 gather_fusion
  51.5 7.4 broadcast_select_fusion.6
  59.0 12.4 %scatter_fusion = f32[16,128,256]{2,1,0:T(8,128)S(1)} fusion(f32[16,128,256]{2,1,0:T(8,128)S(1)} %get-tuple-element.373, s32[64]{0:T(128)S(1)} %compare_select_fusion.12, f32[64,128,256]{2,1,0:T(8,128)} %broadcast_select_fusion.6), kind=kCustom, calls=%fused_computation.3.clone.1 | custom fusion | flops 2097152 | bytes 25166080 | tf_op jit(solution)/shard_map/while/body/scatter-add | solution.py:54
  71.4 1.4 compare_and_fusion.6
  72.8 2.8 gather_fusion
  75.6 7.4 broadcast_select_fusion.6
  83.1 12.4 %scatter_fusion = f32[16,128,256]{2,1,0:T(8,128)S(1)} fusion(f32[16,128,256]{2,1,0:T(8,128)S(1)} %get-tuple-element.373, s32[64]{0:T(128)S(1)} %compare_select_fusion.12, f32[64,128,256]{2,1,0:T(8,128)} %broadcast_select_fusion.6), kind=kCustom, calls=%fused_computation.3.clone.1 | custom fusion | flops 2097152 | bytes 25166080 | tf_op jit(solution)/shard_map/while/body/scatter-add | solution.py:54
  95.5 1.4 compare_and_fusion.6
  97.0 2.8 gather_fusion
  99.7 7.4 broadcast_select_fusion.6
  107.2 12.4 %scatter_fusion = f32[16,128,256]{2,1,0:T(8,128)S(1)} fusion(f32[16,128,256]{2,1,0:T(8,128)S(1)} %get-tuple-element.373, s32[64]{0:T(128)S(1)} %compare_select_fusion.12, f32[64,128,256]{2,1,0:T(8,128)} %broadcast_select_fusion.6), kind=kCustom, calls=%fused_computation.3.clone.1 | custom fusion | flops 2097152 | bytes 25166080 | tf_op jit(solution)/shard_map/while/body/scatter-add | solution.py:54
  119.7 1.4 compare_and_fusion.6
  121.1 2.8 gather_fusion
  123.9 7.4 broadcast_select_fusion.6
  131.3 12.4 %scatter_fusion = f32[16,128,256]{2,1,0:T(8,128)S(1)} fusion(f32[16,128,256]{2,1,0:T(8,128)S(1)} %get-tuple-element.373, s32[64]{0:T(128)S(1)} %compare_select_fusion.12, f32[64,128,256]{2,1,0:T(8,128)} %broadcast_select_fusion.6), kind=kCustom, calls=%fused_computation.3.clone.1 | custom fusion | flops 2097152 | bytes 25166080 | tf_op jit(solution)/shard_map/while/body/scatter-add | solution.py:54
  143.8 1.1 convert_element_type.38
  144.9 66.4 %reduce-scatter.4.cloned.1.call-done = bf16[128,256]{1,0:T(8,128)(2,1)} async-done(((bf16[2048,256]{1,0:T(8,128)(2,1)}), bf16[128,256]{1,0:T(8,128)(2,1)}) %reduce-scatter.4.cloned.1.call-update) | async-done | bytes 65552 | tf_op jit(solution)/shard_map/reduce_scatter | solution.py:59
  211.3 7.2 all-to-all-start.1
  218.6 7.3 all-to-all-done.1
  225.9 23.1 %all_gather.10 = bf16[1024,256]{1,0:T(8,128)(2,1)S(1)} all-gather(bf16[128,256]{1,0:T(8,128)(2,1)S(1)} %bitcast.31), channel_id=1, replica_groups=mesh['row'=8,'col'=16] {'row'}, dimensions={0}, use_global_device_ids=true | all-gather | bytes 589824 | tf_op jit(solution)/shard_map/all_gather | solution.py:40
  249.2 93.7 %while.31 = (s32[]{:T(128)}, f32[16,128,256]{2,1,0:T(8,128)S(1)}, s32[]{:T(128)}, s32[256]{0:T(256)S(1)}, s32[]{:T(128)}, /*index=5*/bf16[256,128,128]{2,1,0:T(8...) while((s32[]{:T(128)}, f32[16,128,256]{2,1,0:T(8,128)S(1)}, ...), condition=%wide.region_6.8_spmd, body=%wide.region_4.7_spmd.sunk | while | flops 543164096 | bytes 48240824 | solution.py:58
  249.2 0.7 compare_and_fusion.7
  249.9 2.8 gather_fusion.1
  252.7 7.4 broadcast_select_fusion.7
  260.2 12.4 %scatter_fusion.1 = f32[16,128,256]{2,1,0:T(8,128)S(1)} fusion(f32[16,128,256]{2,1,0:T(8,128)S(1)} %get-tuple-element.409, s32[64]{0:T(128)S(1)} %compare_select_fusion.13, f32[64,128,256]{2,1,0:T(8,128)} %broadcast_select_fusion.7), kind=kCustom, calls=%fused_computation.4.clone.1 | custom fusion | flops 2097152 | bytes 25166080 | tf_op jit(solution)/shard_map/while/body/scatter-add | solution.py:54
  273.4 2.8 gather_fusion.1
  276.1 7.4 broadcast_select_fusion.7
  283.6 12.4 %scatter_fusion.1 = f32[16,128,256]{2,1,0:T(8,128)S(1)} fusion(f32[16,128,256]{2,1,0:T(8,128)S(1)} %get-tuple-element.409, s32[64]{0:T(128)S(1)} %compare_select_fusion.13, f32[64,128,256]{2,1,0:T(8,128)} %broadcast_select_fusion.7), kind=kCustom, calls=%fused_computation.4.clone.1 | custom fusion | flops 2097152 | bytes 25166080 | tf_op jit(solution)/shard_map/while/body/scatter-add | solution.py:54
  296.8 2.8 gather_fusion.1
  299.6 7.4 broadcast_select_fusion.7
  307.0 12.4 %scatter_fusion.1 = f32[16,128,256]{2,1,0:T(8,128)S(1)} fusion(f32[16,128,256]{2,1,0:T(8,128)S(1)} %get-tuple-element.409, s32[64]{0:T(128)S(1)} %compare_select_fusion.13, f32[64,128,256]{2,1,0:T(8,128)} %broadcast_select_fusion.7), kind=kCustom, calls=%fused_computation.4.clone.1 | custom fusion | flops 2097152 | bytes 25166080 | tf_op jit(solution)/shard_map/while/body/scatter-add | solution.py:54
  320.2 2.8 gather_fusion.1
  323.0 7.4 broadcast_select_fusion.7
  330.4 12.4 %scatter_fusion.1 = f32[16,128,256]{2,1,0:T(8,128)S(1)} fusion(f32[16,128,256]{2,1,0:T(8,128)S(1)} %get-tuple-element.409, s32[64]{0:T(128)S(1)} %compare_select_fusion.13, f32[64,128,256]{2,1,0:T(8,128)} %broadcast_select_fusion.7), kind=kCustom, calls=%fused_computation.4.clone.1 | custom fusion | flops 2097152 | bytes 25166080 | tf_op jit(solution)/shard_map/while/body/scatter-add | solution.py:54
  342.9 1.1 convert_element_type.40
  344.0 65.9 %reduce-scatter.6.cloned.1.call-done = bf16[128,256]{1,0:T(8,128)(2,1)} async-done(((bf16[2048,256]{1,0:T(8,128)(2,1)}), bf16[128,256]{1,0:T(8,128)(2,1)}) %reduce-scatter.6.cloned.1.call-update) | async-done | bytes 65552 | tf_op jit(solution)/shard_map/reduce_scatter | solution.py:59
  409.9 1.5 fusion.27
  411.4 7.2 all-to-all-start.2
  418.6 7.3 all-to-all-done.2
  426.0 23.0 %all_gather.11 = bf16[1024,256]{1,0:T(8,128)(2,1)S(1)} all-gather(bf16[128,256]{1,0:T(8,128)(2,1)S(1)} %bitcast.30), channel_id=1, replica_groups=mesh['row'=8,'col'=16] {'row'}, dimensions={0}, use_global_device_ids=true | all-gather | bytes 589824 | tf_op jit(solution)/shard_map/all_gather | solution.py:40
  449.2 93.7 %while.32 = (s32[]{:T(128)}, f32[16,128,256]{2,1,0:T(8,128)S(1)}, s32[]{:T(128)}, s32[256]{0:T(256)S(1)}, s32[]{:T(128)}, /*index=5*/bf16[256,128,128]{2,1,0:T(8...) while((s32[]{:T(128)}, f32[16,128,256]{2,1,0:T(8,128)S(1)}, ...), condition=%wide.region_10.12_spmd, body=%wide.region_8.11_spmd.sunk | while | flops 543164096 | bytes 48240824 | solution.py:58
  449.9 2.8 gather_fusion.2
  452.7 7.4 broadcast_select_fusion.8
  460.2 12.4 %scatter_fusion.2 = f32[16,128,256]{2,1,0:T(8,128)S(1)} fusion(f32[16,128,256]{2,1,0:T(8,128)S(1)} %get-tuple-element.445, s32[64]{0:T(128)S(1)} %compare_select_fusion.14, f32[64,128,256]{2,1,0:T(8,128)} %broadcast_select_fusion.8), kind=kCustom, calls=%fused_computation.5.clone.1 | custom fusion | flops 2097152 | bytes 25166080 | tf_op jit(solution)/shard_map/while/body/scatter-add | solution.py:54
  473.4 2.8 gather_fusion.2
  476.2 7.4 broadcast_select_fusion.8
  483.6 12.4 %scatter_fusion.2 = f32[16,128,256]{2,1,0:T(8,128)S(1)} fusion(f32[16,128,256]{2,1,0:T(8,128)S(1)} %get-tuple-element.445, s32[64]{0:T(128)S(1)} %compare_select_fusion.14, f32[64,128,256]{2,1,0:T(8,128)} %broadcast_select_fusion.8), kind=kCustom, calls=%fused_computation.5.clone.1 | custom fusion | flops 2097152 | bytes 25166080 | tf_op jit(solution)/shard_map/while/body/scatter-add | solution.py:54
  496.8 2.8 gather_fusion.2
  499.6 7.4 broadcast_select_fusion.8
  507.0 12.4 %scatter_fusion.2 = f32[16,128,256]{2,1,0:T(8,128)S(1)} fusion(f32[16,128,256]{2,1,0:T(8,128)S(1)} %get-tuple-element.445, s32[64]{0:T(128)S(1)} %compare_select_fusion.14, f32[64,128,256]{2,1,0:T(8,128)} %broadcast_select_fusion.8), kind=kCustom, calls=%fused_computation.5.clone.1 | custom fusion | flops 2097152 | bytes 25166080 | tf_op jit(solution)/shard_map/while/body/scatter-add | solution.py:54
  520.2 2.8 gather_fusion.2
  523.0 7.4 broadcast_select_fusion.8
  530.5 12.4 %scatter_fusion.2 = f32[16,128,256]{2,1,0:T(8,128)S(1)} fusion(f32[16,128,256]{2,1,0:T(8,128)S(1)} %get-tuple-element.445, s32[64]{0:T(128)S(1)} %compare_select_fusion.14, f32[64,128,256]{2,1,0:T(8,128)} %broadcast_select_fusion.8), kind=kCustom, calls=%fused_computation.5.clone.1 | custom fusion | flops 2097152 | bytes 25166080 | tf_op jit(solution)/shard_map/while/body/scatter-add | solution.py:54
  542.9 1.1 convert_element_type.45
  544.1 65.9 %reduce-scatter.8.cloned.1.call-done = bf16[128,256]{1,0:T(8,128)(2,1)} async-done(((bf16[2048,256]{1,0:T(8,128)(2,1)}), bf16[128,256]{1,0:T(8,128)(2,1)}) %reduce-scatter.8.cloned.1.call-update) | async-done | bytes 65552 | tf_op jit(solution)/shard_map/reduce_scatter | solution.py:59
  610.0 0.9 subtract_convert_fusion
  610.9 0.9 fusion.28
  611.8 146.0 %all-reduce.3.cloned.1.call-done = f32[256,256]{1,0:T(8,128)} async-done(((f32[256,256]{1,0:T(8,128)}), f32[256,256]{1,0:T(8,128)}) %all-reduce.3.cloned.1.call-update) | async-done | bytes 262160
  757.8 1.3 dynamic-slice_multiply_fusion
  (60 shorter events, 6.9 us)
Async XLA Ops:
  7.2 16.5 %all-to-all-start = ((bf16[1,16,8,256]{3,2,0,1:T(8,128)(2,1)}), bf16[1,16,8,256]{3,2,0,1:T(8,128)(2,1)S(1)}, u32[]{:S(2)}, u32[]{:S(2)}) async-start(bf16[1,16,8,256]{3,2,0,1:T(8,128)(2,1)} %bitcast.27), calls=%async_computation | async-start | bytes 131072 | tf_op jit(solution)/shard_map/all_to_all | solution.py:32
  16.3 195.0 %reduce-scatter.4.cloned.1.call-start = ((), (), s32[]{:S(2)}) async-start(), calls=%async_computation.6 | async-start | bytes 1114112 | tf_op jit(solution)/shard_map/reduce_scatter | solution.py:59
  51.5 7.4 copy-start.4
  75.6 7.4 copy-start.4
  99.7 7.4 copy-start.4
  123.9 7.4 copy-start.4
  143.8 105.4 %copy-start.3 = (s32[256]{0:T(256)S(1)}, s32[256]{0:T(256)}, u32[]{:S(2)}) copy-start(s32[256]{0:T(256)} %get-tuple-element.492) | copy-start | bytes 3076
  143.8 105.4 %copy-start.5 = (s32[256]{0:T(256)S(1)}, s32[256]{0:T(256)}, u32[]{:S(2)}) copy-start(s32[256]{0:T(256)} %get-tuple-element.495) | copy-start | bytes 3076
  211.3 14.5 %all-to-all-start.1 = ((bf16[1,16,8,256]{3,2,0,1:T(8,128)(2,1)}), bf16[1,16,8,256]{3,2,0,1:T(8,128)(2,1)S(1)}, u32[]{:S(2)}, u32[]{:S(2)}) async-start(bf16[1,16,8,256]{3,2,0,1:T(8,128)(2,1)} %bitcast.28), calls=%async_computation.2 | async-start | bytes 131072 | tf_op jit(solution)/shard_map/all_to_all | solution.py:32
  218.5 191.4 %reduce-scatter.6.cloned.1.call-start = ((), (), s32[]{:S(2)}) async-start(), calls=%async_computation.7 | async-start | bytes 1114112 | tf_op jit(solution)/shard_map/reduce_scatter | solution.py:59
  342.9 67.1 %copy-start.1 = (bf16[128,256]{1,0:T(8,128)(2,1)S(1)}, bf16[128,256]{1,0:T(8,128)(2,1)}, u32[]{:S(2)}) copy-start(bf16[128,256]{1,0:T(8,128)(2,1)} %param.13) | copy-start | bytes 196612
  411.4 14.5 %all-to-all-start.2 = ((bf16[1,16,8,256]{3,2,0,1:T(8,128)(2,1)}), bf16[1,16,8,256]{3,2,0,1:T(8,128)(2,1)S(1)}, u32[]{:S(2)}, u32[]{:S(2)}) async-start(bf16[1,16,8,256]{3,2,0,1:T(8,128)(2,1)} %fusion.27), calls=%async_computation.4 | async-start | bytes 131072 | tf_op jit(solution)/shard_map/all_to_all | solution.py:32
  418.6 191.4 %reduce-scatter.8.cloned.1.call-start = ((), (), s32[]{:S(2)}) async-start(), calls=%async_computation.8 | async-start | bytes 1114112 | tf_op jit(solution)/shard_map/reduce_scatter | solution.py:59
  542.9 67.1 %copy-start.2 = (bf16[128,256]{1,0:T(8,128)(2,1)S(1)}, bf16[128,256]{1,0:T(8,128)(2,1)}, u32[]{:S(2)}) copy-start(bf16[128,256]{1,0:T(8,128)(2,1)} %reduce-scatter.4.cloned.1.call-done) | copy-start | bytes 196612
  544.0 213.8 %all-reduce.3.cloned.1.call-start = ((), (), s32[]{:S(2)}) async-start(), calls=%async_computation.9 | async-start | bytes 524288
  610.9 148.2 %copy-start = (bf16[128,256]{1,0:T(8,128)(2,1)}, bf16[128,256]{1,0:T(8,128)(2,1)S(1)}, u32[]{:S(2)}) copy-start(bf16[128,256]{1,0:T(8,128)(2,1)S(1)} %subtract_convert_fusion) | copy-start | bytes 196612
Sparse Core Ops, SparseCore 0:
  145.0 66.2 reduce-scatter.3
  344.1 65.7 reduce-scatter.5
  544.1 65.8 reduce-scatter.7
  615.3 142.4 all-reduce.2
where the time goes:
time: 767 us; the launch traced here: 766 us
  waiting for transfers between devices  366 us (48%)
  other arithmetic  168 us (22%)
  matrix products  89.5 us (12%)
  blocking collectives  69.4 us (9%)
  local copies, waits for them, and re-layouts  34.1 us (4%)
  starting transfers between devices  23.6 us (3%)
  between operations  14.5 us (2%)
    reduce_scatter x3, waiting for transfers between devices, per_device(): lax.psum_scatter(tile_summed.reshape(BR * BLOCK, vec_width).astype(jnp.bf...  198 us
    scatter-add x12, other arithmetic, add_group(): return accumulated.at[part_rows].add(products)  149 us
    unnamed x5, waiting for transfers between devices  146 us
    dot_general x12, matrix products, add_group(): jnp.einsum('eab,ebk->eak', part_blocks, pieces, preferred_element_type=jn...  88.6 us
    all_gather x3, blocking collectives, per_device(): gathered = lax.all_gather(dealt_panel, 'row', axis=0, tiled=True)  69.4 us
    gather x12, local copies, waits for them, and re-layouts, add_group(): pieces = jnp.take(column_blocks, part_cols, axis=0)  33.4 us
    all_to_all x3, starting transfers between devices, per_device(): lax.all_to_all(current.reshape(run_count, col_count, 8, vec_width), 'col'...  23.5 us
    all_to_all x3, waiting for transfers between devices, per_device(): lax.all_to_all(current.reshape(run_count, col_count, 8, vec_width), 'col'...  21.3 us
  transfers between devices with their start and end apart: 7, of which 7 were waited for; matrix products, arithmetic and copies ran while one was open for 0% of the time, Pallas kernels for 0%

commit v1 on v0

v1 whole, which is shorter than its diff:
```python
import functools

import jax
import jax.numpy as jnp
from jax import lax
from jax.experimental import pallas as pl
from jax.experimental.pallas import tpu as pltpu
from jax.sharding import PartitionSpec as P

BLOCK = 128
BR = 16
COLBLK = 8
MAXB = 256
DEG = 3
RUN = 8
CHUNK = 16
UNROLL = 4
VMEM_LIMIT = 48 * 1024 * 1024


def merge_kernel(rows_ref, cols_ref, stored_ref, blocks_ref, out_ref, held, total, sems):
    stored = stored_ref[0]
    chunks = MAXB // CHUNK

    def copy(g):
        part = pl.ds(g * CHUNK, CHUNK)
        return pltpu.make_async_copy(blocks_ref.at[part], held.at[part], sems.at[g])

    for g in range(chunks):

        @pl.when(g * CHUNK < stored)
        def _():
            copy(g).start()

    @pl.loop(0, COLBLK)
    def _(j):
        total[j] = jnp.zeros(total.shape[1:], total.dtype)

    @pl.loop(0, (stored + CHUNK - 1) // CHUNK)
    def _(g):
        copy(g).wait()

        @pl.loop(0, CHUNK // UNROLL)
        def _(u):
            for k in range(UNROLL):
                e = g * CHUNK + u * UNROLL + k
                col = jnp.where(e < stored, cols_ref[e], COLBLK)
                part = pl.ds(pl.multiple_of(rows_ref[e] * RUN, RUN), RUN)
                block = held[e].astype(jnp.float32).reshape(BLOCK // RUN, RUN, BLOCK)
                total[col, :, part, :] = total[col, :, part, :] + block

    for j in range(COLBLK):
        out_ref[:, j * BLOCK : (j + 1) * BLOCK] = (
            total[j].reshape(BR * BLOCK, BLOCK).astype(out_ref.dtype)
        )


def merge(tile_rows, tile_cols, stored, tile_blocks):
    smem = pl.BlockSpec(memory_space=pltpu.SMEM)
    return pl.pallas_call(
        merge_kernel,
        out_shape=jax.ShapeDtypeStruct((BR * BLOCK, COLBLK * BLOCK), jnp.bfloat16),
        in_specs=[smem, smem, smem, pl.BlockSpec(memory_space=pl.ANY)],
        out_specs=pl.BlockSpec(memory_space=pltpu.VMEM),
        scratch_shapes=[
            pltpu.VMEM((MAXB, BLOCK, BLOCK), jnp.bfloat16),
            pltpu.VMEM((COLBLK + 1, BLOCK // RUN, BR * RUN, BLOCK), jnp.float32),
            pltpu.SemaphoreType.DMA((MAXB // CHUNK,)),
        ],
        compiler_params=pltpu.CompilerParams(vmem_limit_bytes=VMEM_LIMIT),
        cost_estimate=pl.CostEstimate(
            flops=MAXB * BLOCK * BLOCK,
            bytes_accessed=(MAXB + BR * COLBLK) * BLOCK * BLOCK * 2,
            transcendentals=0,
        ),
        name="merge_blocks",
    )(tile_rows, tile_cols, stored, tile_blocks)


def product_kernel(tile_ref, panel_ref, out_ref):
    step = 512

    @pl.loop(0, tile_ref.shape[0] // step)
    def _(m):
        part = pl.ds(pl.multiple_of(m * step, step), step)
        out_ref[part, :] = jnp.dot(
            tile_ref[part, :], panel_ref[...], preferred_element_type=jnp.float32
        ).astype(out_ref.dtype)


def last_product_kernel(col_ref, tile_ref, panel_ref, held_ref, out_ref, total):
    step = 512

    @pl.loop(0, tile_ref.shape[0] // step)
    def _(m):
        part = pl.ds(pl.multiple_of(m * step, step), step)
        total[part, :] = jnp.dot(
            tile_ref[part, :], panel_ref[...], preferred_element_type=jnp.float32
        )

    mine = pl.ds(pl.multiple_of(col_ref[0] * BLOCK, BLOCK), BLOCK)
    total[mine, :] = total[mine, :] - 0.5 * held_ref[...].astype(jnp.float32)

    @pl.loop(0, BR)
    def _(i):
        runs = [
            total[pl.ds(pl.multiple_of(j * BLOCK + i * RUN, RUN), RUN), :]
            for j in range(BLOCK // RUN)
        ]
        out_ref[pl.ds(pl.multiple_of(i * BLOCK, BLOCK), BLOCK), :] = jnp.concatenate(
            runs, axis=0
        ).astype(out_ref.dtype)


def product(tile, panel, col=None, held=None):
    vmem = pl.BlockSpec(memory_space=pltpu.VMEM)
    width = panel.shape[1]
    last = held is not None
    out_shape = (tile.shape[0], width)
    return pl.pallas_call(
        last_product_kernel if last else product_kernel,
        out_shape=jax.ShapeDtypeStruct(out_shape, jnp.bfloat16),
        in_specs=[pl.BlockSpec(memory_space=pltpu.SMEM), vmem, vmem, vmem] if last else [vmem, vmem],
        out_specs=vmem,
        scratch_shapes=[pltpu.VMEM(out_shape, jnp.float32)] if last else [],
        compiler_params=pltpu.CompilerParams(vmem_limit_bytes=VMEM_LIMIT),
        cost_estimate=pl.CostEstimate(
            flops=2 * tile.shape[0] * tile.shape[1] * width,
            bytes_accessed=2 * (tile.size + panel.size + tile.shape[0] * width),
            transcendentals=0,
        ),
        name="last_product" if last else "tile_product",
    )(*((col, tile, panel, held) if last else (tile, panel)))


def per_device(vectors, blocks, block_rows, block_cols, counts):
    col_count = lax.axis_size("col")
    row_count = lax.axis_size("row")
    shard_rows, width = vectors.shape
    col = lax.axis_index("col").astype(jnp.int32).reshape(1)

    def exchange(parts, axes):
        return lax.all_to_all(parts, axes, split_axis=0, concat_axis=0, tiled=True)

    def gather(own):
        copies = jnp.broadcast_to(own[None], (row_count,) + own.shape)
        return exchange(copies, "row").reshape(row_count * shard_rows, width)

    def reduce(terms):
        arrived = exchange(terms.reshape(col_count, shard_rows, width), "col")
        return jnp.sum(arrived.astype(jnp.float32), axis=0)

    with jax.named_scope("merge"):
        tile = merge(block_rows[0, 0], block_cols[0, 0], counts[0], blocks[0, 0])
    with jax.named_scope("deal"):
        runs = vectors.reshape(col_count, RUN, width)
        dealt = exchange(runs, "col").reshape(shard_rows, width)
    with jax.named_scope("gather0"):
        panel = gather(dealt)
    with jax.named_scope("step1"):
        first = reduce(product(tile, panel)).astype(jnp.bfloat16)
        panel = gather(first)
    with jax.named_scope("step2"):
        summed = reduce(product(tile, panel))
        second = (2.0 * summed - dealt.astype(jnp.float32)).astype(jnp.bfloat16)
        panel = gather(second)
    with jax.named_scope("step3"):
        filtered = (2.0 * reduce(product(tile, panel, col, first))).astype(jnp.bfloat16)
    with jax.named_scope("gram"):
        local = jnp.dot(filtered.T, filtered, preferred_element_type=jnp.float32)
        devices = row_count * col_count
        arrived = exchange(local.reshape(devices, width // devices, width), ("row", "col"))
        gram = jnp.sum(arrived, axis=0) / (BR * BLOCK // col_count)
    return filtered, gram


def solution(mesh):
    in_specs = (
        P(("row", "col"), None),
        P("row", "col", None, None, None),
        P("row", "col", None),
        P("row", "col", None),
        P("row", "col"),
    )
    out_specs = (P(("row", "col"), None), P(("row", "col"), None))
    return jax.shard_map(
        per_device, mesh=mesh, in_specs=in_specs, out_specs=out_specs, check_vma=False
    )
```

time: 767 us -> 153 us (0.20)
  waiting for transfers between devices: 366 us -> 9.34 us
  other arithmetic: 168 us -> 1.19 us
  matrix products: 89.5 us -> 0.2 us
  blocking collectives: 69.4 us -> 111 us
  local copies, waits for them, and re-layouts: 34.1 us -> 11.7 us
  starting transfers between devices: 23.6 us -> 8.14 us
  between operations: 14.5 us -> 1.4 us
  Pallas kernels: 0 us -> 9.6 us
    reduce_scatter x3 -> x0, waiting for transfers between devices: 198 us -> none  [per_device(): lax.psum_scatter(tile_summed.reshape(BR * BLOCK, vec_width).astype(jnp.bf...]
    scatter-add x12 -> x0, other arithmetic: 149 us -> none  [add_group(): return accumulated.at[part_rows].add(products)]
    unnamed x5 -> x0, waiting for transfers between devices: 146 us -> none
    all_to_all x0 -> x6, blocking collectives: none -> 111 us  [exchange(): return lax.all_to_all(parts, axes, split_axis=0, concat_axis=0, tiled=True)]
    dot_general x13 -> x1, matrix products: 89.5 us -> 0.2 us  [per_device(): local = jnp.dot(filtered.T, filtered, preferred_element_type=jnp.float32)]
    all_gather x3 -> x0, blocking collectives: 69.4 us -> none  [per_device(): gathered = lax.all_gather(dealt_panel, 'row', axis=0, tiled=True)]
    gather x12 -> x0, local copies, waits for them, and re-layouts: 33.4 us -> none  [add_group(): pieces = jnp.take(column_blocks, part_cols, axis=0)]
    all_to_all x3 -> x2, starting transfers between devices: 23.5 us -> 8.14 us  [exchange(): return lax.all_to_all(parts, axes, split_axis=0, concat_axis=0, tiled=True)]
  transfers between devices with their start and end apart: 7 -> 2, of which waited for: 7 -> 2; matrix products, arithmetic and copies ran while one was open for 0% -> 0% of each run, Pallas kernels for 0% -> 3%
where the time goes in v1:
time: 153 us
  blocking collectives  111 us (73%)
  local copies, waits for them, and re-layouts  11.7 us (8%)
  Pallas kernels  9.6 us (6%)
  waiting for transfers between devices  9.34 us (6%)
  starting transfers between devices  8.14 us (5%)
    all_to_all x6, blocking collectives, exchange(): return lax.all_to_all(parts, axes, split_axis=0, concat_axis=0, tiled=True)  111 us
    unnamed x14, local copies, waits for them, and re-layouts  9.84 us
    all_to_all x2, waiting for transfers between devices, exchange(): return lax.all_to_all(parts, axes, split_axis=0, concat_axis=0, tiled=True)  9.34 us
    all_to_all x2, starting transfers between devices, exchange(): return lax.all_to_all(parts, axes, split_axis=0, concat_axis=0, tiled=True)  8.14 us
    pallas_call x3, Pallas kernels, product(): pl.pallas_call(last_product_kernel if last else product_kernel, out_shape...  5.6 us
    pallas_call x1, Pallas kernels, merge(): pl.pallas_call(merge_kernel, out_shape=jax.ShapeDtypeStruct((BR * BLOCK,...  4 us
  transfers between devices with their start and end apart: 2, of which 2 were waited for; matrix products, arithmetic and copies ran while one was open for 0% of the time, Pallas kernels for 3%

profile of v1, /device:TPU:1, one launch (start us, length us, event | category | flops | bytes accessed | tf_op | source)
XLA Modules:
  0.0 152.6 jit_solution(13953042835596513416)
XLA Ops:
  0.6 16.5 %all_to_all.40 = bf16[16,8,256]{2,1,0:T(8,128)(2,1)S(1)} all-to-all(bf16[16,8,256]{2,1,0:T(8,128)(2,1)} %bitcast.27), channel_id=1, replica_groups=mesh['row'=8,'col'=16] {'col'}, dimensions={0} | all-to-all | bytes 131072 | tf_op jit(solution)/shard_map/deal/all_to_all | solution.py:143
  17.1 0.8 broadcast_in_dim.9
  18.0 4.6 %all-to-all-start.1 = ((bf16[8,128,256]{2,1,0:T(8,128)(2,1)}), bf16[8,128,256]{2,1,0:T(8,128)(2,1)S(1)}, u32[]{:S(2)}, u32[]{:S(2)}) async-start(bf16[8,128,256]{2,1,0:T(8,128)(2,1)} %broadcast_in_dim.9), calls=%async_computation.1 | async-start | bytes 1048576 | tf_op jit(solution)/shard_map/gather0/all_to_all | solution.py:143
  23.3 0.0 copy-start.4
  23.3 0.7 copy-done.4
  23.9 0.0 copy-start.5
  23.9 0.7 copy-done.5
  24.6 4.0 %merge_blocks.1.tile_ref = bf16[2048,1024]{1,0:T(8,128)(2,1)S(1)} custom-call(s32[256]{0:T(256)S(1)} %bitcast.23, s32[256]{0:T(256)S(1)} %bitcast.24, s32[1]{0:T(128)} %bitcast.16.stored_ref, bf16[256,128,128]{2,1,0:T(8,128)(2,1)} %bitcast.25), custom_call_target="tpu_custom_call" | custom-call | flops 4194304 | bytes 12582912 | tf_op jit(solution)/shard_map/merge/merge_blocks/pallas_call | solution.py:60
  28.6 0.0 copy-start
  28.6 1.9 %copy-done = bf16[2048,1024]{1,0:T(8,128)(2,1)} copy-done((bf16[2048,1024]{1,0:T(8,128)(2,1)}, bf16[2048,1024]{1,0:T(8,128)(2,1)S(1)}, u32[]{:S(2)}) %copy-start) | copy-done | bytes 4194328
  30.6 1.2 all-to-all-done.1
  31.8 0.0 copy-start.1
  31.8 2.2 %copy-done.1 = bf16[2048,1024]{1,0:T(8,128)(2,1)S(1)} copy-done((bf16[2048,1024]{1,0:T(8,128)(2,1)S(1)}, bf16[2048,1024]{1,0:T(8,128)(2,1)}, u32[]{:S(2)}) %copy-start.1) | copy-done | bytes 4194328
  34.0 1.7 %tile_product.2 = bf16[2048,256]{1,0:T(8,128)(2,1)S(1)} custom-call(bf16[2048,1024]{1,0:T(8,128)(2,1)S(1)} %copy-done.1, bf16[1024,256]{1,0:T(8,128)(2,1)S(1)} %bitcast.21), custom_call_target="tpu_custom_call" | custom-call | flops 1073741824 | bytes 5767168 | tf_op jit(solution)/shard_map/step1/tile_product/pallas_call | solution.py:120
  35.7 20.9 %all_to_all.41 = bf16[16,128,256]{2,1,0:T(8,128)(2,1)S(1)} all-to-all(bf16[16,128,256]{2,1,0:T(8,128)(2,1)S(1)} %bitcast.18), channel_id=1, replica_groups=mesh['row'=8,'col'=16] {'col'}, dimensions={0} | all-to-all | bytes 2097152 | tf_op jit(solution)/shard_map/step1/all_to_all | solution.py:143
  56.7 0.1 reduce_sum.39.held_ref
  56.9 12.7 %all_to_all.42 = bf16[8,128,256]{2,1,0:T(8,128)(2,1)S(1)} all-to-all(bf16[8,128,256]{2,1,0:T(8,128)(2,1)S(1)} %broadcast_in_dim.10), channel_id=1, replica_groups=mesh['row'=8,'col'=16] {'row'}, dimensions={0} | all-to-all | bytes 1048576 | tf_op jit(solution)/shard_map/step1/all_to_all | solution.py:143
  69.5 0.0 copy-start.2
  69.5 2.2 %copy-done.2 = bf16[2048,1024]{1,0:T(8,128)(2,1)S(1)} copy-done((bf16[2048,1024]{1,0:T(8,128)(2,1)S(1)}, bf16[2048,1024]{1,0:T(8,128)(2,1)}, u32[]{:S(2)}) %copy-start.2) | copy-done | bytes 4194328
  71.7 1.7 %tile_product.3 = bf16[2048,256]{1,0:T(8,128)(2,1)S(1)} custom-call(bf16[2048,1024]{1,0:T(8,128)(2,1)S(1)} %copy-done.2, bf16[1024,256]{1,0:T(8,128)(2,1)S(1)} %bitcast.22), custom_call_target="tpu_custom_call" | custom-call | flops 1073741824 | bytes 5767168 | tf_op jit(solution)/shard_map/step2/tile_product/pallas_call | solution.py:120
  73.5 23.2 %all_to_all.43 = bf16[16,128,256]{2,1,0:T(8,128)(2,1)S(1)} all-to-all(bf16[16,128,256]{2,1,0:T(8,128)(2,1)S(1)} %bitcast.19), channel_id=1, replica_groups=mesh['row'=8,'col'=16] {'col'}, dimensions={0} | all-to-all | bytes 2097152 | tf_op jit(solution)/shard_map/step2/all_to_all | solution.py:143
  96.7 0.1 convert_reduce_fusion.1
  96.9 0.8 broadcast_in_dim.22
  97.7 3.5 %all-to-all-start.5 = ((bf16[8,128,256]{2,1,0:T(8,128)(2,1)}), bf16[8,128,256]{2,1,0:T(8,128)(2,1)S(1)}, u32[]{:S(2)}, u32[]{:S(2)}) async-start(bf16[8,128,256]{2,1,0:T(8,128)(2,1)} %broadcast_in_dim.22), calls=%async_computation.5 | async-start | bytes 1048576 | tf_op jit(solution)/shard_map/step2/all_to_all | solution.py:143
  101.2 8.1 %all-to-all-done.5 = bf16[8,128,256]{2,1,0:T(8,128)(2,1)S(1)} async-done(((bf16[8,128,256]{2,1,0:T(8,128)(2,1)}), bf16[8,128,256]{2,1,0:T(8,128)(2,1)S(1)}, u32[]{:S(2)}, u32[]{:S(2)}) %all-to-all-start.5) | async-done | bytes 524320 | tf_op jit(solution)/shard_map/step2/all_to_all | solution.py:143
  109.3 0.0 copy-start.3
  109.3 2.2 %copy-done.3 = bf16[2048,1024]{1,0:T(8,128)(2,1)S(1)} copy-done((bf16[2048,1024]{1,0:T(8,128)(2,1)S(1)}, bf16[2048,1024]{1,0:T(8,128)(2,1)}, u32[]{:S(2)}) %copy-start.3) | copy-done | bytes 4194328
  111.5 2.1 %last_product.1 = bf16[2048,256]{1,0:T(8,128)(2,1)S(1)} custom-call(s32[1]{0:T(128)} %bitcast.col_ref, bf16[2048,1024]{1,0:T(8,128)(2,1)S(1)} %copy-done.3, bf16[1024,256]{1,0:T(8,128)(2,1)S(1)} %bitcast.20, bf16[128,256]{1,0:T(8,128)(2,1)S(1)} %reduce_sum.39.held_ref), custom_call_target="tpu_custom_call" | custom-call | flops 1073741824 | bytes 5767168 | tf_op jit(solution)/shard_map/step3/last_product/pallas_call | solution.py:120
  113.6 22.3 %all_to_all.44 = bf16[16,128,256]{2,1,0:T(8,128)(2,1)S(1)} all-to-all(bf16[16,128,256]{2,1,0:T(8,128)(2,1)S(1)} %bitcast.17), channel_id=1, replica_groups=mesh['row'=8,'col'=16] {'col'}, dimensions={0} | all-to-all | bytes 2097152 | tf_op jit(solution)/shard_map/step3/all_to_all | solution.py:143
  135.8 0.1 convert_reduce_fusion
  136.0 0.0 copy-start.6
  136.0 0.2 fusion
  136.2 0.1 reshape.53
  136.4 15.5 %all_to_all.45 = f32[128,2,256]{2,1,0:T(2,128)S(1)} all-to-all(f32[128,2,256]{2,1,0:T(2,128)S(1)} %reshape.53), channel_id=1, replica_groups=mesh['row'=8,'col'=16] {'row','col'}, dimensions={0} | all-to-all | bytes 524288 | tf_op jit(solution)/shard_map/gram/all_to_all | solution.py:143
  151.9 0.1 reduce_sum.42
  152.0 0.6 broadcast_multiply_fusion
  152.6 0.0 copy-done.6
  (3 shorter events, 0.1 us)
Async XLA Ops:
  18.0 13.8 %all-to-all-start.1 = ((bf16[8,128,256]{2,1,0:T(8,128)(2,1)}), bf16[8,128,256]{2,1,0:T(8,128)(2,1)S(1)}, u32[]{:S(2)}, u32[]{:S(2)}) async-start(bf16[8,128,256]{2,1,0:T(8,128)(2,1)} %broadcast_in_dim.9), calls=%async_computation.1 | async-start | bytes 1048576 | tf_op jit(solution)/shard_map/gather0/all_to_all | solution.py:143
  23.3 0.7 copy-start.4
  23.9 0.7 copy-start.5
  28.6 1.9 %copy-start = (bf16[2048,1024]{1,0:T(8,128)(2,1)}, bf16[2048,1024]{1,0:T(8,128)(2,1)S(1)}, u32[]{:S(2)}) copy-start(bf16[2048,1024]{1,0:T(8,128)(2,1)S(1)} %merge_blocks.1.tile_ref) | copy-start | bytes 12582916
  31.8 2.2 %copy-start.1 = (bf16[2048,1024]{1,0:T(8,128)(2,1)S(1)}, bf16[2048,1024]{1,0:T(8,128)(2,1)}, u32[]{:S(2)}) copy-start(bf16[2048,1024]{1,0:T(8,128)(2,1)} %copy-done) | copy-start | bytes 12582916
  69.5 2.2 %copy-start.2 = (bf16[2048,1024]{1,0:T(8,128)(2,1)S(1)}, bf16[2048,1024]{1,0:T(8,128)(2,1)}, u32[]{:S(2)}) copy-start(bf16[2048,1024]{1,0:T(8,128)(2,1)} %copy-done) | copy-start | bytes 12582916
  97.7 11.6 %all-to-all-start.5 = ((bf16[8,128,256]{2,1,0:T(8,128)(2,1)}), bf16[8,128,256]{2,1,0:T(8,128)(2,1)S(1)}, u32[]{:S(2)}, u32[]{:S(2)}) async-start(bf16[8,128,256]{2,1,0:T(8,128)(2,1)} %broadcast_in_dim.22), calls=%async_computation.5 | async-start | bytes 1048576 | tf_op jit(solution)/shard_map/step2/all_to_all | solution.py:143
  109.3 2.2 %copy-start.3 = (bf16[2048,1024]{1,0:T(8,128)(2,1)S(1)}, bf16[2048,1024]{1,0:T(8,128)(2,1)}, u32[]{:S(2)}) copy-start(bf16[2048,1024]{1,0:T(8,128)(2,1)} %copy-done) | copy-start | bytes 12582916
  136.0 16.6 %copy-start.6 = (bf16[128,256]{1,0:T(8,128)(2,1)}, bf16[128,256]{1,0:T(8,128)(2,1)S(1)}, u32[]{:S(2)}) copy-start(bf16[128,256]{1,0:T(8,128)(2,1)S(1)} %multiply_convert_fusion) | copy-start | bytes 196612

commit v2 on v0

v2 whole, which is shorter than its diff:
```python
import functools

import jax
import jax.numpy as jnp
from jax import lax
from jax.experimental import pallas as pl
from jax.experimental.pallas import tpu as pltpu
from jax.sharding import PartitionSpec as P

BLOCK = 128
BR = 16
COLBLK = 8
MAXB = 256
RUN = 8
HALF = 8
QUARTER = HALF * HALF * RUN
PAIR = 2 * BLOCK
CHUNK = 16
UNROLL = 4
MERGE_VMEM = 64 * 1024 * 1024 - 4096
SMALL_VMEM = 8 * 1024 * 1024
VMEM = pl.BlockSpec(memory_space=pltpu.VMEM)
HBM = pl.BlockSpec(memory_space=pltpu.HBM)
F32 = jnp.float32
BF16 = jnp.bfloat16


def small_call(kernel, name, out_shapes, operands, scratch=(), flops=0):
    outs = [jax.ShapeDtypeStruct(shape, BF16) for shape in out_shapes]
    sizes = sum(x.size for x in operands) + sum(x.size for x in outs)
    return pl.pallas_call(
        kernel,
        out_shape=outs,
        in_specs=[VMEM] * len(operands),
        out_specs=[VMEM] * len(outs),
        scratch_shapes=list(scratch),
        compiler_params=pltpu.CompilerParams(vmem_limit_bytes=SMALL_VMEM),
        cost_estimate=pl.CostEstimate(
            flops=flops, bytes_accessed=2 * sizes, transcendentals=0
        ),
        name=name,
    )(*operands)


def merge_kernel(rows_ref, cols_ref, stored_ref, blocks_ref, *refs):
    tiles, (rows, cols, stored, held, total, done, index_sems, sems, tile_sems) = (
        refs[:4],
        refs[4:],
    )
    row_id, core = lax.axis_index("row"), lax.axis_index("col") & 1
    chunks = MAXB // CHUNK
    indices = [
        pltpu.make_async_copy(source, target, index_sems.at[k])
        for k, (source, target) in enumerate(
            ((stored_ref, stored), (rows_ref, rows), (cols_ref, cols))
        )
    ]

    def copy(g):
        part = pl.ds(g * CHUNK, CHUNK)
        return pltpu.make_async_copy(blocks_ref.at[part], held.at[part], sems.at[g])

    for index in indices:
        index.start()
    for g in range(chunks):
        copy(g).start()

    @pl.loop(0, COLBLK)
    def _(j):
        total[j] = jnp.zeros(total.shape[1:], total.dtype)

    for index in indices:
        index.wait()
    count = stored[0]

    @pl.loop(0, chunks)
    def _(g):
        copy(g).wait()

        @pl.when(g * CHUNK < count)
        def _():
            @pl.loop(0, CHUNK // UNROLL)
            def _(u):
                for k in range(UNROLL):
                    e = g * CHUNK + u * UNROLL + k
                    col = cols[e]
                    col = ((col // 2 - row_id // 2) & 3) * 2 + ((col ^ row_id) & 1)
                    col = jnp.where(e < count, col, COLBLK)
                    row = rows[e]
                    part = pl.ds(pl.multiple_of(row // 2 * RUN, RUN), RUN)
                    block = held[e].astype(F32).reshape(HALF, 2, RUN, BLOCK)
                    place = (col, row & 1, slice(None), slice(None), part, slice(None))
                    total[place] = total[place] + block

    out = []
    for p in range(2):
        for i in range(2):
            target, source = abs(1 - p - core), abs(1 - i - core)
            tile = done.at[i] if p else tiles[i]
            for j in range(COLBLK):
                terms = total[j, source, :, target]
                tile[:, j * BLOCK : (j + 1) * BLOCK] = (
                    terms.reshape(QUARTER, BLOCK).astype(done.dtype)
                )
            if p:
                out.append(pltpu.make_async_copy(tile, tiles[2 + i], tile_sems.at[i]))
                out[-1].start()
    for copied in out:
        copied.wait()


def merge(tile_rows, tile_cols, stored, tile_blocks):
    quarter = jax.ShapeDtypeStruct((QUARTER, COLBLK * BLOCK), BF16)
    return pl.pallas_call(
        merge_kernel,
        out_shape=[quarter] * 4,
        in_specs=[HBM] * 4,
        out_specs=[VMEM, VMEM, HBM, HBM],
        scratch_shapes=[
            pltpu.SMEM((MAXB,), jnp.int32),
            pltpu.SMEM((MAXB,), jnp.int32),
            pltpu.SMEM((1,), jnp.int32),
            pltpu.VMEM((MAXB, BLOCK, BLOCK), BF16),
            pltpu.VMEM((COLBLK + 1, 2, HALF, 2, HALF * RUN, BLOCK), F32),
            pltpu.VMEM((2,) + quarter.shape, BF16),
            pltpu.SemaphoreType.DMA((3,)),
            pltpu.SemaphoreType.DMA((MAXB // CHUNK,)),
            pltpu.SemaphoreType.DMA((2,)),
        ],
        compiler_params=pltpu.CompilerParams(vmem_limit_bytes=60 * 1024 * 1024),
        cost_estimate=pl.CostEstimate(
            flops=MAXB * BLOCK * BLOCK,
            bytes_accessed=(MAXB + BR * COLBLK) * BLOCK * BLOCK * 2,
            transcendentals=0,
        ),
        name="merge_blocks",
    )(tile_rows, tile_cols, stored, tile_blocks)


def copies_kernel(own_ref, out_ref, held, own_sem, sems):
    load = pltpu.make_async_copy(own_ref, held, own_sem)
    load.start()
    load.wait()
    stores = [
        pltpu.make_async_copy(held, out_ref.at[k], sems.at[k]) for k in range(out_ref.shape[0])
    ]
    for store in stores:
        store.start()
    for store in stores:
        store.wait()


def copies(own, count):
    return pl.pallas_call(
        copies_kernel,
        out_shape=jax.ShapeDtypeStruct((count,) + own.shape, own.dtype),
        in_specs=[HBM],
        out_specs=HBM,
        scratch_shapes=[
            pltpu.VMEM(own.shape, own.dtype),
            pltpu.SemaphoreType.DMA,
            pltpu.SemaphoreType.DMA((count,)),
        ],
        compiler_params=pltpu.CompilerParams(vmem_limit_bytes=MERGE_VMEM),
        name="copies",
    )(own)


def dot(a, b):
    return jnp.dot(a, b, preferred_element_type=F32)


def put_together(part_refs, panel):
    rows = panel.shape[0] // len(part_refs)
    for k, part_ref in enumerate(part_refs):
        panel[k * rows : (k + 1) * rows, :] = part_ref[...]


def step_kernel(keep, first, *refs):
    tiles, refs = refs[:2], refs[2:]
    row_id, col_id = lax.axis_index("row"), lax.axis_index("col")
    core = col_id & 1
    if first:
        dealt_ref, out_ref, panel, total = refs[0], refs[1], refs[-2], refs[-1]
        for k in range(COLBLK):
            part = ((row_id // 2 + k // 2) & 3) * 2 + ((row_id ^ k) & 1)
            part = pl.ds(pl.multiple_of(part * BLOCK, BLOCK), BLOCK)
            panel[k * BLOCK : (k + 1) * BLOCK, :] = dealt_ref[part, :]
        if not keep:
            refs[2][...] = panel[:PAIR, :]
    else:
        out_ref, panel, total = refs[4:]
        put_together(refs[:4], panel)
    for i in range(2):
        terms = dot(tiles[i][...], panel[...])
        terms = terms.reshape(HALF, HALF, RUN, terms.shape[1])
        for t in range(HALF):
            away = ((t // 2 - col_id // 4) & 3) * 2 + ((t ^ (col_id // 2)) & 1)
            total[away, :, core if i else 1 - core] = terms[t]
    out_ref[...] = total[...].reshape(out_ref.shape).astype(out_ref.dtype)


def last_kernel(keep, *refs):
    tiles, parts, (first_ref, out_ref, panel, total) = refs[:2], refs[2:6], refs[6:]
    put_together(parts, panel)
    col_id = lax.axis_index("col")
    core = col_id & 1
    for j in range(2):
        terms = dot(tiles[j][...], panel[...])
        terms = terms.reshape(HALF, HALF, RUN, terms.shape[1])
        for t in range(HALF):
            total[:, t, core if j else 1 - core] = terms[t]
    first = first_ref[:BLOCK, :].astype(F32).reshape(HALF, 2, RUN, first_ref.shape[1])
    target = core if keep else 1 - core
    first = jnp.where(target == 0, first[:, 0], first[:, 1])
    mine = col_id // 2
    total[:, mine, core] = total[:, mine, core] - 0.5 * first
    out_ref[...] = total[...].reshape(out_ref.shape).astype(out_ref.dtype)


def add_kernel(a_ref, b_ref, *out_refs):
    rows = out_refs[0].shape[0]
    for k, out_ref in enumerate(out_refs):
        part = slice(k * rows, (k + 1) * rows)
        out_ref[...] = (a_ref[part, :].astype(F32) + b_ref[part, :].astype(F32)).astype(BF16)


def sum_kernel(a_ref, b_ref, c_ref, d_ref, *out_refs):
    rows = out_refs[0].shape[0]
    for k, out_ref in enumerate(out_refs):
        part = slice(k * rows, (k + 1) * rows)
        terms = [ref[part, :].astype(F32) for ref in (a_ref, b_ref, c_ref, d_ref)]
        out_ref[...] = ((terms[0] + terms[1]) + (terms[2] + terms[3])).astype(BF16)


def next_kernel(scale, own_ref, arrived_ref, near_ref, far_ref, *refs):
    out_ref = refs[-1]
    pairs = ((own_ref, arrived_ref), (near_ref, far_ref))
    for k, (a_ref, b_ref) in enumerate(pairs):
        part = slice(k * BLOCK, (k + 1) * BLOCK)
        summed = a_ref[...].astype(F32) + b_ref[...].astype(F32)
        if len(refs) > 1:
            summed = scale * summed - refs[0][part, :].astype(F32)
        out_ref[part, :] = summed.astype(BF16)


def per_device(vectors, blocks, block_rows, block_cols, counts):
    col_count = lax.axis_size("col")
    row_count = lax.axis_size("row")
    devices = row_count * col_count
    shard_rows, width = vectors.shape
    half_rows = 2 * QUARTER
    flops = 2 * half_rows * COLBLK * BLOCK * width

    def exchange(parts, axes, groups=None):
        return lax.all_to_all(
            parts, axes, split_axis=0, concat_axis=0, tiled=True, axis_index_groups=groups
        )

    def other_core(x):
        return lax.ppermute(x, "col", [(i, i ^ 1) for i in range(col_count)])

    def along_x(x, k):
        return lax.ppermute(x, "col", [(i, (i + 4 * k) % col_count) for i in range(col_count)])

    def along_y(x, k):
        return lax.ppermute(x, "row", [(i, (i + 2 * k) % row_count) for i in range(row_count)])

    def near_z(x):
        return lax.ppermute(x, "row", [(i, i ^ 1) for i in range(row_count)])

    def far_z(x):
        return lax.ppermute(x, "col", [(i, i ^ 2) for i in range(col_count)])

    def both_z(x):
        pairs = [
            (r * col_count + c, (r ^ 1) * col_count + (c ^ 2))
            for r in range(row_count)
            for c in range(col_count)
        ]
        return lax.ppermute(x, ("row", "col"), pairs)

    scratch = [
        pltpu.VMEM((COLBLK * BLOCK, width), BF16),
        pltpu.VMEM((HALF, HALF, 2, RUN, width), F32),
    ]

    def step(tiles, parts, first, previous):
        wide = (half_rows, width)
        sent, *pair = small_call(
            functools.partial(step_kernel, False, first),
            "send",
            [wide] + ([(PAIR, width)] if first else []),
            (tiles[0], tiles[1]) + parts,
            scratch,
            flops,
        )
        previous = pair[0] if first else previous
        arrived = other_core(sent)
        (kept,) = small_call(
            functools.partial(step_kernel, True, first),
            "keep",
            [wide],
            (tiles[2], tiles[3]) + parts,
            scratch,
            flops,
        )
        terms = small_call(add_kernel, "add", [(PAIR, width)] * 4, (kept, arrived))
        arrived = [along_x(terms[k], k) for k in (2, 1, 3)]
        own, other = small_call(
            sum_kernel, "sum_x", [(BLOCK, width)] * 2, (terms[0], *arrived)
        )
        arrived, far, near = far_z(other), both_z(other), near_z(own)
        operands = (own, arrived, near, far) + (() if first else (previous,))
        (pair,) = small_call(
            functools.partial(next_kernel, 2.0), "next", [(PAIR, width)], operands
        )
        sides = {k: along_y(pair, k) for k in (2, 1, 3)}
        return (pair, sides[3], sides[2], sides[1]), previous

    with jax.named_scope("merge"):
        tiles = merge(block_rows[0, 0], block_cols[0, 0], counts[0], blocks[0, 0])
    with jax.named_scope("deal"):
        panel = exchange(copies(vectors, row_count).reshape(devices, RUN, width), ("row", "col"))
        panel = panel.reshape(row_count * shard_rows, width)
    with jax.named_scope("step1"):
        parts, previous = step(tiles, (panel,), True, None)
        first = parts[0]
    with jax.named_scope("step2"):
        parts, _ = step(tiles, parts, False, previous)
    with jax.named_scope("step3"):
        halves = []
        for keep in (False, True):
            (half,) = small_call(
                functools.partial(last_kernel, keep),
                "last_keep" if keep else "last_send",
                [(half_rows, width)],
                (tiles[int(keep)], tiles[2 + int(keep)]) + parts + (first,),
                scratch,
                flops,
            )
            halves.append(half if keep else other_core(half))
        (terms,) = small_call(add_kernel, "add", [(half_rows, width)], tuple(halves))
        same_core = [list(range(c, col_count, 2)) for c in range(2)]
        arrived = exchange(terms.reshape(HALF, shard_rows, width), "col", same_core)
        summed = jnp.sum(arrived.astype(F32), axis=0)
        filtered = (2.0 * summed).astype(BF16)
    with jax.named_scope("gram"):
        local = dot(filtered.T, filtered).astype(BF16)
        arrived = exchange(local.reshape(devices, width // devices, width), ("row", "col"))
        gram = jnp.sum(arrived.astype(F32), axis=0) / (BR * BLOCK // col_count)
    return filtered, gram


def solution(mesh):
    in_specs = (
        P(("row", "col"), None),
        P("row", "col", None, None, None),
        P("row", "col", None),
        P("row", "col", None),
        P("row", "col"),
    )
    out_specs = (P(("row", "col"), None), P(("row", "col"), None))
    return jax.shard_map(
        per_device, mesh=mesh, in_specs=in_specs, out_specs=out_specs, check_vma=False
    )
```

time: 767 us -> 128 us (0.17)
  waiting for transfers between devices: 366 us -> 36.9 us
  other arithmetic: 168 us -> 0.83 us
  matrix products: 89.5 us -> 0.21 us
  blocking collectives: 69.4 us -> 28.9 us
  local copies, waits for them, and re-layouts: 34.1 us -> 7.43 us
  starting transfers between devices: 23.6 us -> 38.1 us
  Pallas kernels: 0 us -> 14 us
  between operations: 14.5 us -> 1.46 us
    reduce_scatter x3 -> x0, waiting for transfers between devices: 198 us -> none  [per_device(): lax.psum_scatter(tile_summed.reshape(BR * BLOCK, vec_width).astype(jnp.bf...]
    scatter-add x12 -> x0, other arithmetic: 149 us -> none  [add_group(): return accumulated.at[part_rows].add(products)]
    unnamed x5 -> x0, waiting for transfers between devices: 146 us -> none
    dot_general x13 -> x1, matrix products: 89.5 us -> 0.21 us  [dot(): return jnp.dot(a, b, preferred_element_type=F32)]
    all_gather x3 -> x0, blocking collectives: 69.4 us -> none  [per_device(): gathered = lax.all_gather(dealt_panel, 'row', axis=0, tiled=True)]
    gather x12 -> x0, local copies, waits for them, and re-layouts: 33.4 us -> none  [add_group(): pieces = jnp.take(column_blocks, part_cols, axis=0)]
    ppermute x0 -> x21, waiting for transfers between devices: none -> 30.9 us  [the longest x6 12 us: along_x(): lax.ppermute(x, 'col', [(i, (i + 4 * k) % col_count) for i in range(col_c...]
    all_to_all x0 -> x2, blocking collectives: none -> 28.9 us  [exchange(): lax.all_to_all(parts, axes, split_axis=0, concat_axis=0, tiled=True, axis...]
  transfers between devices with their start and end apart: 7 -> 22, of which waited for: 7 -> 18; matrix products, arithmetic and copies ran while one was open for 0% -> 0% of each run, Pallas kernels for 0% -> 7%
where the time goes in v2:
time: 128 us
  starting transfers between devices  38.1 us (30%)
  waiting for transfers between devices  36.9 us (29%)
  blocking collectives  28.9 us (23%)
  Pallas kernels  14 us (11%)
  local copies, waits for them, and re-layouts  7.43 us (6%)
  between operations  1.46 us (1%)
    all_to_all x2, blocking collectives, exchange(): lax.all_to_all(parts, axes, split_axis=0, concat_axis=0, tiled=True, axis...  28.9 us
    ppermute x6, waiting for transfers between devices, along_x(): lax.ppermute(x, 'col', [(i, (i + 4 * k) % col_count) for i in range(col_c...  12 us
    all_to_all x1, starting transfers between devices, exchange(): lax.all_to_all(parts, axes, split_axis=0, concat_axis=0, tiled=True, axis...  11.5 us
    ppermute x6, waiting for transfers between devices, along_y(): lax.ppermute(x, 'row', [(i, (i + 2 * k) % row_count) for i in range(row_c...  11.1 us
    ppermute x3, starting transfers between devices, other_core(): return lax.ppermute(x, 'col', [(i, i ^ 1) for i in range(col_count)])  7.87 us
    ppermute x6, starting transfers between devices, along_x(): lax.ppermute(x, 'col', [(i, (i + 4 * k) % col_count) for i in range(col_c...  7.64 us
    unnamed x22, local copies, waits for them, and re-layouts  7.37 us
    pallas_call x1, Pallas kernels, merge(): pl.pallas_call(merge_kernel, out_shape=[quarter] * 4, in_specs=[HBM] * 4,...  6.9 us
  transfers between devices with their start and end apart: 22, of which 18 were waited for; matrix products, arithmetic and copies ran while one was open for 0% of the time, Pallas kernels for 7%

profile of v2, /device:TPU:1, one launch (start us, length us, event | category | flops | bytes accessed | tf_op | source)
XLA Modules:
  0.0 127.8 jit_solution(3624404434584953198)
XLA Ops:
  0.6 1.7 %copies.1 = bf16[8,128,256]{2,1,0:T(8,128)(2,1)} custom-call(bf16[128,256]{1,0:T(8,128)(2,1)} %own_ref.1), custom_call_target="tpu_custom_call" | custom-call | tf_op jit(solution)/shard_map/deal/copies/pallas_call | solution.py:154
  2.4 11.5 %all-to-all-start = ((bf16[128,8,256]{2,1,0:T(8,128)(2,1)}), bf16[128,8,256]{2,1,0:T(8,128)(2,1)S(1)}, u32[]{:S(2)}, u32[]{:S(2)}) async-start(bf16[128,8,256]{2,1,0:T(8,128)(2,1)} %bitcast.14), calls=%async_computation | async-start | bytes 1048576 | tf_op jit(solution)/shard_map/deal/all_to_all | solution.py:256
  14.5 6.9 %merge_blocks.1 = (bf16[512,1024]{1,0:T(8,128)(2,1)}, bf16[512,1024]{1,0:T(8,128)(2,1)}, bf16[512,1024]{1,0:T(8,128)(2,1)}, bf16[512,1024]{1,0:T(8,128)(2,1)}) custom-call(s32[256]{0:T(256)} %bitcast.15, s32[256]{0:T(256)} %bitcast.16, s32[1]{0:T(128)} %bitcast.9.stored_ref, bf16[256,128,128]{2,1,0:T(8,128)(2,1)} %bitcast.13), custom_call_target="tpu_custom_call" | custom-call | flops 4194304 | bytes 12582912 | tf_op jit(solution)/shard_map/merge/merge_blocks/pallas_call | solution.py:114
  21.5 6.0 %all-to-all-done = bf16[128,8,256]{2,1,0:T(8,128)(2,1)S(1)} async-done(((bf16[128,8,256]{2,1,0:T(8,128)(2,1)}), bf16[128,8,256]{2,1,0:T(8,128)(2,1)S(1)}, u32[]{:S(2)}, u32[]{:S(2)}) %all-to-all-start) | async-done | bytes 524320 | tf_op jit(solution)/shard_map/deal/all_to_all | solution.py:256
  27.4 1.2 copy-done.4
  28.6 1.2 copy-done.7
  29.9 0.8 send.2
  30.7 1.2 collective-permute-start
  31.9 1.2 copy-done
  33.1 1.2 copy-done.2
  34.4 0.8 keep.2.a_ref
  35.2 0.1 add.3
  35.3 1.1 collective-permute-start.1
  36.4 0.4 collective-permute-start.2
  36.8 2.3 %collective-permute-start.3 = (bf16[256,256]{1,0:T(8,128)(2,1)S(1)}, bf16[256,256]{1,0:T(8,128)(2,1)S(1)}, u32[]{:S(2)}, u32[]{:S(2)}) collective-permute-start(bf16[256,256]{1,0:T(8,128)(2,1)S(1)} %get-tuple-element.28), channel_id=1, source_target_pairs={{0,12},{1,13},{2,14},{3,15},{4,0},{5,1},{6,2},{7,3},{8,4},{9,5},{1... | collective-permute-start | bytes 393224 | tf_op jit(solution)/shard_map/step1/ppermute | solution.py:264
  39.1 2.9 %collective-permute-done.1.b_ref = bf16[256,256]{1,0:T(8,128)(2,1)S(1)} collective-permute-done((bf16[256,256]{1,0:T(8,128)(2,1)S(1)}, bf16[256,256]{1,0:T(8,128)(2,1)S(1)}, u32[]{:S(2)}, u32[]{:S(2)}) %collective-permute-start.1) | collective-permute-done | bytes 131104 | tf_op jit(solution)/shard_map/step1/ppermute | solution.py:264
  42.0 3.1 %collective-permute-done.2.c_ref = bf16[256,256]{1,0:T(8,128)(2,1)S(1)} collective-permute-done((bf16[256,256]{1,0:T(8,128)(2,1)S(1)}, bf16[256,256]{1,0:T(8,128)(2,1)S(1)}, u32[]{:S(2)}, u32[]{:S(2)}) %collective-permute-start.2) | collective-permute-done | bytes 131104 | tf_op jit(solution)/shard_map/step1/ppermute | solution.py:264
  45.2 0.1 sum_x.2
  45.2 0.8 collective-permute-start.4
  46.1 2.5 %collective-permute-start.6 = (bf16[128,256]{1,0:T(8,128)(2,1)S(1)}, bf16[128,256]{1,0:T(8,128)(2,1)S(1)}, u32[]{:S(2)}, u32[]{:S(2)}) collective-permute-start(bf16[128,256]{1,0:T(8,128)(2,1)S(1)} %get-tuple-element.30), channel_id=1, source_target_pairs={{0,18},{1,19},{2,16},{3,17},{4,22},{5,23},{6,20},{7,21},{8,26},{9,... | collective-permute-start | bytes 196616 | tf_op jit(solution)/shard_map/step1/ppermute | solution.py:281
  48.6 1.4 %collective-permute-done.4.arrived_ref = bf16[128,256]{1,0:T(8,128)(2,1)S(1)} collective-permute-done((bf16[128,256]{1,0:T(8,128)(2,1)S(1)}, bf16[128,256]{1,0:T(8,128)(2,1)S(1)}, u32[]{:S(2)}, u32[]{:S(2)}) %collective-permute-start.4) | collective-permute-done | bytes 65568 | tf_op jit(solution)/shard_map/step1/ppermute | solution.py:273
  49.9 1.4 %collective-permute-done.6.far_ref = bf16[128,256]{1,0:T(8,128)(2,1)S(1)} collective-permute-done((bf16[128,256]{1,0:T(8,128)(2,1)S(1)}, bf16[128,256]{1,0:T(8,128)(2,1)S(1)}, u32[]{:S(2)}, u32[]{:S(2)}) %collective-permute-start.6) | collective-permute-done | bytes 65568 | tf_op jit(solution)/shard_map/step1/ppermute | solution.py:281
  51.4 0.9 collective-permute-start.7
  52.3 1.3 %collective-permute-start.8 = (bf16[256,256]{1,0:T(8,128)(2,1)S(1)}, bf16[256,256]{1,0:T(8,128)(2,1)S(1)}, u32[]{:S(2)}, u32[]{:S(2)}) collective-permute-start(bf16[256,256]{1,0:T(8,128)(2,1)S(1)} %next.2.refs_2_.refs_6_), channel_id=1, source_target_pairs={{0,64},{16,80},{32,96},{48,112},{64,0},{80,16},{96,32},{112,48},{1... | collective-permute-start | bytes 393224 | tf_op jit(solution)/shard_map/step1/ppermute | solution.py:267
  53.6 1.7 %collective-permute-done.7.refs_3_ = bf16[256,256]{1,0:T(8,128)(2,1)S(1)} collective-permute-done((bf16[256,256]{1,0:T(8,128)(2,1)S(1)}, bf16[256,256]{1,0:T(8,128)(2,1)S(1)}, u32[]{:S(2)}, u32[]{:S(2)}) %collective-permute-start.7) | collective-permute-done | bytes 131104 | tf_op jit(solution)/shard_map/step1/ppermute | solution.py:267
  55.3 2.4 %collective-permute-done.8.refs_4_ = bf16[256,256]{1,0:T(8,128)(2,1)S(1)} collective-permute-done((bf16[256,256]{1,0:T(8,128)(2,1)S(1)}, bf16[256,256]{1,0:T(8,128)(2,1)S(1)}, u32[]{:S(2)}, u32[]{:S(2)}) %collective-permute-start.8) | collective-permute-done | bytes 131104 | tf_op jit(solution)/shard_map/step1/ppermute | solution.py:267
  57.7 2.3 %collective-permute-done.9.refs_5_ = bf16[256,256]{1,0:T(8,128)(2,1)S(1)} collective-permute-done((bf16[256,256]{1,0:T(8,128)(2,1)S(1)}, bf16[256,256]{1,0:T(8,128)(2,1)S(1)}, u32[]{:S(2)}, u32[]{:S(2)}) %collective-permute-start.9) | collective-permute-done | bytes 131104 | tf_op jit(solution)/shard_map/step1/ppermute | solution.py:267
  59.9 1.2 copy-done.5
  61.2 1.2 copy-done.8
  62.4 0.8 send.3
  63.2 2.7 %collective-permute-start.10 = (bf16[1024,256]{1,0:T(8,128)(2,1)S(1)}, bf16[1024,256]{1,0:T(8,128)(2,1)S(1)}, u32[]{:S(2)}, u32[]{:S(2)}) collective-permute-start(bf16[1024,256]{1,0:T(8,128)(2,1)S(1)} %send.3), channel_id=1, source_target_pairs={{0,1},{1,0},{2,3},{3,2},{4,5},{5,4},{6,7},{7,6},{8,9},{9,8},{10,11... | collective-permute-start | bytes 1572872 | tf_op jit(solution)/shard_map/step2/ppermute | solution.py:261
  65.9 0.8 keep.3.a_ref
  66.7 0.7 collective-permute-done.10.b_ref
  67.4 0.1 add.4
  67.5 1.2 collective-permute-start.11
  68.7 0.8 collective-permute-start.12
  69.5 1.9 %collective-permute-start.13 = (bf16[256,256]{1,0:T(8,128)(2,1)S(1)}, bf16[256,256]{1,0:T(8,128)(2,1)S(1)}, u32[]{:S(2)}, u32[]{:S(2)}) collective-permute-start(bf16[256,256]{1,0:T(8,128)(2,1)S(1)} %get-tuple-element.34), channel_id=1, source_target_pairs={{0,12},{1,13},{2,14},{3,15},{4,0},{5,1},{6,2},{7,3},{8,4},{9,5},{1... | collective-permute-start | bytes 393224 | tf_op jit(solution)/shard_map/step2/ppermute | solution.py:264
  71.4 2.5 %collective-permute-done.11.b_ref = bf16[256,256]{1,0:T(8,128)(2,1)S(1)} collective-permute-done((bf16[256,256]{1,0:T(8,128)(2,1)S(1)}, bf16[256,256]{1,0:T(8,128)(2,1)S(1)}, u32[]{:S(2)}, u32[]{:S(2)}) %collective-permute-start.11) | collective-permute-done | bytes 131104 | tf_op jit(solution)/shard_map/step2/ppermute | solution.py:264
  73.8 3.5 %collective-permute-done.12.c_ref = bf16[256,256]{1,0:T(8,128)(2,1)S(1)} collective-permute-done((bf16[256,256]{1,0:T(8,128)(2,1)S(1)}, bf16[256,256]{1,0:T(8,128)(2,1)S(1)}, u32[]{:S(2)}, u32[]{:S(2)}) %collective-permute-start.12) | collective-permute-done | bytes 131104 | tf_op jit(solution)/shard_map/step2/ppermute | solution.py:264
  77.4 0.1 sum_x.3
  77.4 1.5 %collective-permute-start.14 = (bf16[128,256]{1,0:T(8,128)(2,1)S(1)}, bf16[128,256]{1,0:T(8,128)(2,1)S(1)}, u32[]{:S(2)}, u32[]{:S(2)}) collective-permute-start(bf16[128,256]{1,0:T(8,128)(2,1)S(1)} %get-tuple-element.36), channel_id=1, source_target_pairs={{0,2},{1,3},{2,0},{3,1},{4,6},{5,7},{6,4},{7,5},{8,10},{9,11},{10,... | collective-permute-start | bytes 196616 | tf_op jit(solution)/shard_map/step2/ppermute | solution.py:273
  79.0 0.7 collective-permute-start.15
  79.7 1.1 collective-permute-start.16
  80.8 1.4 %collective-permute-done.14.arrived_ref = bf16[128,256]{1,0:T(8,128)(2,1)S(1)} collective-permute-done((bf16[128,256]{1,0:T(8,128)(2,1)S(1)}, bf16[128,256]{1,0:T(8,128)(2,1)S(1)}, u32[]{:S(2)}, u32[]{:S(2)}) %collective-permute-start.14) | collective-permute-done | bytes 65568 | tf_op jit(solution)/shard_map/step2/ppermute | solution.py:273
  82.1 0.8 collective-permute-done.15.near_ref
  82.9 1.3 %collective-permute-done.16.far_ref = bf16[128,256]{1,0:T(8,128)(2,1)S(1)} collective-permute-done((bf16[128,256]{1,0:T(8,128)(2,1)S(1)}, bf16[128,256]{1,0:T(8,128)(2,1)S(1)}, u32[]{:S(2)}, u32[]{:S(2)}) %collective-permute-start.16) | collective-permute-done | bytes 65568 | tf_op jit(solution)/shard_map/step2/ppermute | solution.py:281
  84.2 0.1 next.3.refs_2_
  84.3 0.3 collective-permute-start.17
  84.6 1.3 %collective-permute-start.18 = (bf16[256,256]{1,0:T(8,128)(2,1)S(1)}, bf16[256,256]{1,0:T(8,128)(2,1)S(1)}, u32[]{:S(2)}, u32[]{:S(2)}) collective-permute-start(bf16[256,256]{1,0:T(8,128)(2,1)S(1)} %next.3.refs_2_), channel_id=1, source_target_pairs={{0,64},{16,80},{32,96},{48,112},{64,0},{80,16},{96,32},{112,48},{1... | collective-permute-start | bytes 393224 | tf_op jit(solution)/shard_map/step2/ppermute | solution.py:267
  86.0 0.6 collective-permute-start.19
  86.5 1.6 %collective-permute-done.17.refs_3_ = bf16[256,256]{1,0:T(8,128)(2,1)S(1)} collective-permute-done((bf16[256,256]{1,0:T(8,128)(2,1)S(1)}, bf16[256,256]{1,0:T(8,128)(2,1)S(1)}, u32[]{:S(2)}, u32[]{:S(2)}) %collective-permute-start.17) | collective-permute-done | bytes 131104 | tf_op jit(solution)/shard_map/step2/ppermute | solution.py:267
  88.2 1.8 %collective-permute-done.18.refs_4_ = bf16[256,256]{1,0:T(8,128)(2,1)S(1)} collective-permute-done((bf16[256,256]{1,0:T(8,128)(2,1)S(1)}, bf16[256,256]{1,0:T(8,128)(2,1)S(1)}, u32[]{:S(2)}, u32[]{:S(2)}) %collective-permute-start.18) | collective-permute-done | bytes 131104 | tf_op jit(solution)/shard_map/step2/ppermute | solution.py:267
  90.0 1.4 %collective-permute-done.19.refs_5_ = bf16[256,256]{1,0:T(8,128)(2,1)S(1)} collective-permute-done((bf16[256,256]{1,0:T(8,128)(2,1)S(1)}, bf16[256,256]{1,0:T(8,128)(2,1)S(1)}, u32[]{:S(2)}, u32[]{:S(2)}) %collective-permute-start.19) | collective-permute-done | bytes 131104 | tf_op jit(solution)/shard_map/step2/ppermute | solution.py:267
  91.4 0.8 last_send.1
  92.1 4.0 %collective-permute-start.20 = (bf16[1024,256]{1,0:T(8,128)(2,1)S(1)}, bf16[1024,256]{1,0:T(8,128)(2,1)S(1)}, u32[]{:S(2)}, u32[]{:S(2)}) collective-permute-start(bf16[1024,256]{1,0:T(8,128)(2,1)S(1)} %last_send.1), channel_id=1, source_target_pairs={{0,1},{1,0},{2,3},{3,2},{4,5},{5,4},{6,7},{7,6},{8,9},{9,8},{10,11... | collective-permute-start | bytes 1572872 | tf_op jit(solution)/shard_map/step3/ppermute | solution.py:261
  96.1 0.8 last_keep.1.b_ref
  96.9 0.8 collective-permute-done.20.a_ref
  97.7 0.1 add.5
  97.8 12.7 %all_to_all.15 = bf16[8,128,256]{2,1,0:T(8,128)(2,1)S(1)} all-to-all(bf16[8,128,256]{2,1,0:T(8,128)(2,1)S(1)} %bitcast.12), channel_id=1, replica_groups={{0,2,4,6,8,10,12,14},{1,3,5,7,9,11,13,15},{16,18,20,22,24,26,28,30},{17..., dimensions={0} | all-to-all | bytes 1048576 | tf_op jit(solution)/shard_map/step3/all_to_all | solution.py:256
  110.5 0.1 convert_reduce_fusion
  110.6 0.2 convolution_convert_fusion
  110.9 16.2 %all_to_all.16 = bf16[128,2,256]{2,1,0:T(2,128)(2,1)S(1)} all-to-all(bf16[128,2,256]{2,1,0:T(2,128)(2,1)S(1)} %reshape.19), channel_id=1, replica_groups=mesh['row'=8,'col'=16] {'row','col'}, dimensions={0} | all-to-all | bytes 262144 | tf_op jit(solution)/shard_map/gram/all_to_all | solution.py:256
  127.1 0.2 convert_reduce_fusion.1
  127.2 0.6 broadcast_multiply_fusion
  (25 shorter events, 0.1 us)
Async XLA Ops:
  2.4 25.0 %all-to-all-start = ((bf16[128,8,256]{2,1,0:T(8,128)(2,1)}), bf16[128,8,256]{2,1,0:T(8,128)(2,1)S(1)}, u32[]{:S(2)}, u32[]{:S(2)}) async-start(bf16[128,8,256]{2,1,0:T(8,128)(2,1)} %bitcast.14), calls=%async_computation | async-start | bytes 1048576 | tf_op jit(solution)/shard_map/deal/all_to_all | solution.py:256
  21.4 44.4 %copy-start.1 = (bf16[512,1024]{1,0:T(8,128)(2,1)S(1)}, bf16[512,1024]{1,0:T(8,128)(2,1)}, u32[]{:S(2)}) copy-start(bf16[512,1024]{1,0:T(8,128)(2,1)} %get-tuple-element.22.refs_1_) | copy-start | bytes 3145732
  21.4 44.4 %copy-start.3 = (bf16[512,1024]{1,0:T(8,128)(2,1)S(1)}, bf16[512,1024]{1,0:T(8,128)(2,1)}, u32[]{:S(2)}) copy-start(bf16[512,1024]{1,0:T(8,128)(2,1)} %get-tuple-element.21.refs_0_.refs_1_) | copy-start | bytes 3145732
  27.4 1.2 copy-start.4
  28.6 1.2 copy-start.7
  30.7 4.5 %collective-permute-start = (bf16[1024,256]{1,0:T(8,128)(2,1)S(1)}, bf16[1024,256]{1,0:T(8,128)(2,1)S(1)}, u32[]{:S(2)}, u32[]{:S(2)}) collective-permute-start(bf16[1024,256]{1,0:T(8,128)(2,1)S(1)} %get-tuple-element.24), channel_id=1, source_target_pairs={{0,1},{1,0},{2,3},{3,2},{4,5},{5,4},{6,7},{7,6},{8,9},{9,8},{10,11... | collective-permute-start | bytes 1572872 | tf_op jit(solution)/shard_map/step1/ppermute | solution.py:261
  31.9 1.2 copy-start
  33.1 1.2 copy-start.2
  34.3 57.0 %copy-start.9 = (bf16[512,1024]{1,0:T(8,128)(2,1)S(1)}, bf16[512,1024]{1,0:T(8,128)(2,1)}, u32[]{:S(2)}) copy-start(bf16[512,1024]{1,0:T(8,128)(2,1)} %get-tuple-element.20.refs_0_) | copy-start | bytes 3145732
  34.4 61.8 %copy-start.6 = (bf16[512,1024]{1,0:T(8,128)(2,1)S(1)}, bf16[512,1024]{1,0:T(8,128)(2,1)}, u32[]{:S(2)}) copy-start(bf16[512,1024]{1,0:T(8,128)(2,1)} %get-tuple-element.23.refs_1_.refs_0_) | copy-start | bytes 3145732
  35.3 6.7 %collective-permute-start.1 = (bf16[256,256]{1,0:T(8,128)(2,1)S(1)}, bf16[256,256]{1,0:T(8,128)(2,1)S(1)}, u32[]{:S(2)}, u32[]{:S(2)}) collective-permute-start(bf16[256,256]{1,0:T(8,128)(2,1)S(1)} %get-tuple-element.26), channel_id=1, source_target_pairs={{0,8},{1,9},{2,10},{3,11},{4,12},{5,13},{6,14},{7,15},{8,0},{9,1},... | collective-permute-start | bytes 393224 | tf_op jit(solution)/shard_map/step1/ppermute | solution.py:264
  36.4 8.7 %collective-permute-start.2 = (bf16[256,256]{1,0:T(8,128)(2,1)S(1)}, bf16[256,256]{1,0:T(8,128)(2,1)S(1)}, u32[]{:S(2)}, u32[]{:S(2)}) collective-permute-start(bf16[256,256]{1,0:T(8,128)(2,1)S(1)} %get-tuple-element.27), channel_id=1, source_target_pairs={{0,4},{1,5},{2,6},{3,7},{4,8},{5,9},{6,10},{7,11},{8,12},{9,13},{1... | collective-permute-start | bytes 393224 | tf_op jit(solution)/shard_map/step1/ppermute | solution.py:264
  36.8 8.3 %collective-permute-start.3 = (bf16[256,256]{1,0:T(8,128)(2,1)S(1)}, bf16[256,256]{1,0:T(8,128)(2,1)S(1)}, u32[]{:S(2)}, u32[]{:S(2)}) collective-permute-start(bf16[256,256]{1,0:T(8,128)(2,1)S(1)} %get-tuple-element.28), channel_id=1, source_target_pairs={{0,12},{1,13},{2,14},{3,15},{4,0},{5,1},{6,2},{7,3},{8,4},{9,5},{1... | collective-permute-start | bytes 393224 | tf_op jit(solution)/shard_map/step1/ppermute | solution.py:264
  45.2 4.7 %collective-permute-start.4 = (bf16[128,256]{1,0:T(8,128)(2,1)S(1)}, bf16[128,256]{1,0:T(8,128)(2,1)S(1)}, u32[]{:S(2)}, u32[]{:S(2)}) collective-permute-start(bf16[128,256]{1,0:T(8,128)(2,1)S(1)} %get-tuple-element.30), channel_id=1, source_target_pairs={{0,2},{1,3},{2,0},{3,1},{4,6},{5,7},{6,4},{7,5},{8,10},{9,11},{10,... | collective-permute-start | bytes 196616 | tf_op jit(solution)/shard_map/step1/ppermute | solution.py:273
  46.1 3.9 %collective-permute-start.5 = (bf16[128,256]{1,0:T(8,128)(2,1)S(1)}, bf16[128,256]{1,0:T(8,128)(2,1)S(1)}, u32[]{:S(2)}, u32[]{:S(2)}) collective-permute-start(bf16[128,256]{1,0:T(8,128)(2,1)S(1)} %get-tuple-element.29.own_ref), channel_id=1, source_target_pairs={{0,16},{16,0},{32,48},{48,32},{64,80},{80,64},{96,112},{112,96},{1... | collective-permute-start | bytes 196616 | tf_op jit(solution)/shard_map/step1/ppermute | solution.py:270
  46.1 5.3 %collective-permute-start.6 = (bf16[128,256]{1,0:T(8,128)(2,1)S(1)}, bf16[128,256]{1,0:T(8,128)(2,1)S(1)}, u32[]{:S(2)}, u32[]{:S(2)}) collective-permute-start(bf16[128,256]{1,0:T(8,128)(2,1)S(1)} %get-tuple-element.30), channel_id=1, source_target_pairs={{0,18},{1,19},{2,16},{3,17},{4,22},{5,23},{6,20},{7,21},{8,26},{9,... | collective-permute-start | bytes 196616 | tf_op jit(solution)/shard_map/step1/ppermute | solution.py:281
  51.4 3.9 %collective-permute-start.7 = (bf16[256,256]{1,0:T(8,128)(2,1)S(1)}, bf16[256,256]{1,0:T(8,128)(2,1)S(1)}, u32[]{:S(2)}, u32[]{:S(2)}) collective-permute-start(bf16[256,256]{1,0:T(8,128)(2,1)S(1)} %next.2.refs_2_.refs_6_), channel_id=1, source_target_pairs={{0,96},{16,112},{32,0},{48,16},{64,32},{80,48},{96,64},{112,80},{1... | collective-permute-start | bytes 393224 | tf_op jit(solution)/shard_map/step1/ppermute | solution.py:267
  52.3 5.4 %collective-permute-start.8 = (bf16[256,256]{1,0:T(8,128)(2,1)S(1)}, bf16[256,256]{1,0:T(8,128)(2,1)S(1)}, u32[]{:S(2)}, u32[]{:S(2)}) collective-permute-start(bf16[256,256]{1,0:T(8,128)(2,1)S(1)} %next.2.refs_2_.refs_6_), channel_id=1, source_target_pairs={{0,64},{16,80},{32,96},{48,112},{64,0},{80,16},{96,32},{112,48},{1... | collective-permute-start | bytes 393224 | tf_op jit(solution)/shard_map/step1/ppermute | solution.py:267
  53.6 6.3 %collective-permute-start.9 = (bf16[256,256]{1,0:T(8,128)(2,1)S(1)}, bf16[256,256]{1,0:T(8,128)(2,1)S(1)}, u32[]{:S(2)}, u32[]{:S(2)}) collective-permute-start(bf16[256,256]{1,0:T(8,128)(2,1)S(1)} %next.2.refs_2_.refs_6_), channel_id=1, source_target_pairs={{0,32},{16,48},{32,64},{48,80},{64,96},{80,112},{96,0},{112,16},{1... | collective-permute-start | bytes 393224 | tf_op jit(solution)/shard_map/step1/ppermute | solution.py:267
  59.9 1.2 copy-start.5
  61.2 1.2 copy-start.8
  63.2 4.2 %collective-permute-start.10 = (bf16[1024,256]{1,0:T(8,128)(2,1)S(1)}, bf16[1024,256]{1,0:T(8,128)(2,1)S(1)}, u32[]{:S(2)}, u32[]{:S(2)}) collective-permute-start(bf16[1024,256]{1,0:T(8,128)(2,1)S(1)} %send.3), channel_id=1, source_target_pairs={{0,1},{1,0},{2,3},{3,2},{4,5},{5,4},{6,7},{7,6},{8,9},{9,8},{10,11... | collective-permute-start | bytes 1572872 | tf_op jit(solution)/shard_map/step2/ppermute | solution.py:261
  67.5 6.3 %collective-permute-start.11 = (bf16[256,256]{1,0:T(8,128)(2,1)S(1)}, bf16[256,256]{1,0:T(8,128)(2,1)S(1)}, u32[]{:S(2)}, u32[]{:S(2)}) collective-permute-start(bf16[256,256]{1,0:T(8,128)(2,1)S(1)} %get-tuple-element.32), channel_id=1, source_target_pairs={{0,8},{1,9},{2,10},{3,11},{4,12},{5,13},{6,14},{7,15},{8,0},{9,1},... | collective-permute-start | bytes 393224 | tf_op jit(solution)/shard_map/step2/ppermute | solution.py:264
  68.7 8.7 %collective-permute-start.12 = (bf16[256,256]{1,0:T(8,128)(2,1)S(1)}, bf16[256,256]{1,0:T(8,128)(2,1)S(1)}, u32[]{:S(2)}, u32[]{:S(2)}) collective-permute-start(bf16[256,256]{1,0:T(8,128)(2,1)S(1)} %get-tuple-element.33), channel_id=1, source_target_pairs={{0,4},{1,5},{2,6},{3,7},{4,8},{5,9},{6,10},{7,11},{8,12},{9,13},{1... | collective-permute-start | bytes 393224 | tf_op jit(solution)/shard_map/step2/ppermute | solution.py:264
  69.5 7.9 %collective-permute-start.13 = (bf16[256,256]{1,0:T(8,128)(2,1)S(1)}, bf16[256,256]{1,0:T(8,128)(2,1)S(1)}, u32[]{:S(2)}, u32[]{:S(2)}) collective-permute-start(bf16[256,256]{1,0:T(8,128)(2,1)S(1)} %get-tuple-element.34), channel_id=1, source_target_pairs={{0,12},{1,13},{2,14},{3,15},{4,0},{5,1},{6,2},{7,3},{8,4},{9,5},{1... | collective-permute-start | bytes 393224 | tf_op jit(solution)/shard_map/step2/ppermute | solution.py:264
  77.4 4.7 %collective-permute-start.14 = (bf16[128,256]{1,0:T(8,128)(2,1)S(1)}, bf16[128,256]{1,0:T(8,128)(2,1)S(1)}, u32[]{:S(2)}, u32[]{:S(2)}) collective-permute-start(bf16[128,256]{1,0:T(8,128)(2,1)S(1)} %get-tuple-element.36), channel_id=1, source_target_pairs={{0,2},{1,3},{2,0},{3,1},{4,6},{5,7},{6,4},{7,5},{8,10},{9,11},{10,... | collective-permute-start | bytes 196616 | tf_op jit(solution)/shard_map/step2/ppermute | solution.py:273
  79.0 3.9 %collective-permute-start.15 = (bf16[128,256]{1,0:T(8,128)(2,1)S(1)}, bf16[128,256]{1,0:T(8,128)(2,1)S(1)}, u32[]{:S(2)}, u32[]{:S(2)}) collective-permute-start(bf16[128,256]{1,0:T(8,128)(2,1)S(1)} %get-tuple-element.35.own_ref), channel_id=1, source_target_pairs={{0,16},{16,0},{32,48},{48,32},{64,80},{80,64},{96,112},{112,96},{1... | collective-permute-start | bytes 196616 | tf_op jit(solution)/shard_map/step2/ppermute | solution.py:270
  79.7 4.6 %collective-permute-start.16 = (bf16[128,256]{1,0:T(8,128)(2,1)S(1)}, bf16[128,256]{1,0:T(8,128)(2,1)S(1)}, u32[]{:S(2)}, u32[]{:S(2)}) collective-permute-start(bf16[128,256]{1,0:T(8,128)(2,1)S(1)} %get-tuple-element.36), channel_id=1, source_target_pairs={{0,18},{1,19},{2,16},{3,17},{4,22},{5,23},{6,20},{7,21},{8,26},{9,... | collective-permute-start | bytes 196616 | tf_op jit(solution)/shard_map/step2/ppermute | solution.py:281
  84.3 3.9 %collective-permute-start.17 = (bf16[256,256]{1,0:T(8,128)(2,1)S(1)}, bf16[256,256]{1,0:T(8,128)(2,1)S(1)}, u32[]{:S(2)}, u32[]{:S(2)}) collective-permute-start(bf16[256,256]{1,0:T(8,128)(2,1)S(1)} %next.3.refs_2_), channel_id=1, source_target_pairs={{0,96},{16,112},{32,0},{48,16},{64,32},{80,48},{96,64},{112,80},{1... | collective-permute-start | bytes 393224 | tf_op jit(solution)/shard_map/step2/ppermute | solution.py:267
  84.6 5.4 %collective-permute-start.18 = (bf16[256,256]{1,0:T(8,128)(2,1)S(1)}, bf16[256,256]{1,0:T(8,128)(2,1)S(1)}, u32[]{:S(2)}, u32[]{:S(2)}) collective-permute-start(bf16[256,256]{1,0:T(8,128)(2,1)S(1)} %next.3.refs_2_), channel_id=1, source_target_pairs={{0,64},{16,80},{32,96},{48,112},{64,0},{80,16},{96,32},{112,48},{1... | collective-permute-start | bytes 393224 | tf_op jit(solution)/shard_map/step2/ppermute | solution.py:267
  86.0 5.4 %collective-permute-start.19 = (bf16[256,256]{1,0:T(8,128)(2,1)S(1)}, bf16[256,256]{1,0:T(8,128)(2,1)S(1)}, u32[]{:S(2)}, u32[]{:S(2)}) collective-permute-start(bf16[256,256]{1,0:T(8,128)(2,1)S(1)} %next.3.refs_2_), channel_id=1, source_target_pairs={{0,32},{16,48},{32,64},{48,80},{64,96},{80,112},{96,0},{112,16},{1... | collective-permute-start | bytes 393224 | tf_op jit(solution)/shard_map/step2/ppermute | solution.py:267
  92.1 5.5 %collective-permute-start.20 = (bf16[1024,256]{1,0:T(8,128)(2,1)S(1)}, bf16[1024,256]{1,0:T(8,128)(2,1)S(1)}, u32[]{:S(2)}, u32[]{:S(2)}) collective-permute-start(bf16[1024,256]{1,0:T(8,128)(2,1)S(1)} %last_send.1), channel_id=1, source_target_pairs={{0,1},{1,0},{2,3},{3,2},{4,5},{5,4},{6,7},{7,6},{8,9},{9,8},{10,11... | collective-permute-start | bytes 1572872 | tf_op jit(solution)/shard_map/step3/ppermute | solution.py:261
  110.6 17.2 %copy-start.10 = (bf16[128,256]{1,0:T(8,128)(2,1)}, bf16[128,256]{1,0:T(8,128)(2,1)S(1)}, u32[]{:S(2)}) copy-start(bf16[128,256]{1,0:T(8,128)(2,1)S(1)} %multiply_convert_fusion) | copy-start | bytes 196612

commit v3 on v2

--- a/solution.py
+++ b/solution.py
@@ -16,37 +16,40 @@
 QUARTER = HALF * HALF * RUN
 PAIR = 2 * BLOCK
 CHUNK = 16
-UNROLL = 4
-MERGE_VMEM = 64 * 1024 * 1024 - 4096
+UNROLL = 16
+PIECES = 4
+MERGE_VMEM = 60 * 1024 * 1024
 SMALL_VMEM = 8 * 1024 * 1024
+PRODUCT_VMEM = 50 * 1024 * 1024
+ROOM = 16
 VMEM = pl.BlockSpec(memory_space=pltpu.VMEM)
 HBM = pl.BlockSpec(memory_space=pltpu.HBM)
 F32 = jnp.float32
 BF16 = jnp.bfloat16
 
 
-def small_call(kernel, name, out_shapes, operands, scratch=(), flops=0):
+def small_call(kernel, name, out_shapes, operands, scratch=(), flops=0, tile=None):
+    tiles = [] if tile is None else [tile]
     outs = [jax.ShapeDtypeStruct(shape, BF16) for shape in out_shapes]
     sizes = sum(x.size for x in operands) + sum(x.size for x in outs)
     return pl.pallas_call(
         kernel,
         out_shape=outs,
-        in_specs=[VMEM] * len(operands),
+        in_specs=[HBM] * len(tiles) + [VMEM] * len(operands),
         out_specs=[VMEM] * len(outs),
         scratch_shapes=list(scratch),
-        compiler_params=pltpu.CompilerParams(vmem_limit_bytes=SMALL_VMEM),
+        compiler_params=pltpu.CompilerParams(vmem_limit_bytes=PRODUCT_VMEM if tiles else SMALL_VMEM),
         cost_estimate=pl.CostEstimate(
             flops=flops, bytes_accessed=2 * sizes, transcendentals=0
         ),
         name=name,
-    )(*operands)
-
-
-def merge_kernel(rows_ref, cols_ref, stored_ref, blocks_ref, *refs):
-    tiles, (rows, cols, stored, held, total, done, index_sems, sems, tile_sems) = (
-        refs[:4],
-        refs[4:],
-    )
+    )(*tiles, *operands)
+
+
+def merge_kernel(
+    rows_ref, cols_ref, stored_ref, blocks_ref, tile_ref,
+    rows, cols, stored, held, total, done, index_sems, sems, tile_sems,
+):
     row_id, core = lax.axis_index("row"), lax.axis_index("col") & 1
     chunks = MAXB // CHUNK
     indices = [
@@ -96,38 +99,37 @@
     for p in range(2):
         for i in range(2):
             target, source = abs(1 - p - core), abs(1 - i - core)
-            tile = done.at[i] if p else tiles[i]
+            k = 2 * p + i
             for j in range(COLBLK):
                 terms = total[j, source, :, target]
-                tile[:, j * BLOCK : (j + 1) * BLOCK] = (
+                done[k, :, j * BLOCK : (j + 1) * BLOCK] = (
                     terms.reshape(QUARTER, BLOCK).astype(done.dtype)
                 )
-            if p:
-                out.append(pltpu.make_async_copy(tile, tiles[2 + i], tile_sems.at[i]))
-                out[-1].start()
+            out.append(pltpu.make_async_copy(done.at[k], tile_ref.at[k], tile_sems.at[k]))
+            out[-1].start()
     for copied in out:
         copied.wait()
 
 
 def merge(tile_rows, tile_cols, stored, tile_blocks):
-    quarter = jax.ShapeDtypeStruct((QUARTER, COLBLK * BLOCK), BF16)
+    quarter = (QUARTER, COLBLK * BLOCK)
     return pl.pallas_call(
         merge_kernel,
-        out_shape=[quarter] * 4,
+        out_shape=jax.ShapeDtypeStruct((ROOM,) + quarter, BF16),
         in_specs=[HBM] * 4,
-        out_specs=[VMEM, VMEM, HBM, HBM],
+        out_specs=HBM,
         scratch_shapes=[
             pltpu.SMEM((MAXB,), jnp.int32),
             pltpu.SMEM((MAXB,), jnp.int32),
             pltpu.SMEM((1,), jnp.int32),
             pltpu.VMEM((MAXB, BLOCK, BLOCK), BF16),
             pltpu.VMEM((COLBLK + 1, 2, HALF, 2, HALF * RUN, BLOCK), F32),
-            pltpu.VMEM((2,) + quarter.shape, BF16),
+            pltpu.VMEM((4,) + quarter, BF16),
             pltpu.SemaphoreType.DMA((3,)),
             pltpu.SemaphoreType.DMA((MAXB // CHUNK,)),
-            pltpu.SemaphoreType.DMA((2,)),
+            pltpu.SemaphoreType.DMA((4,)),
         ],
-        compiler_params=pltpu.CompilerParams(vmem_limit_bytes=60 * 1024 * 1024),
+        compiler_params=pltpu.CompilerParams(vmem_limit_bytes=MERGE_VMEM),
         cost_estimate=pl.CostEstimate(
             flops=MAXB * BLOCK * BLOCK,
             bytes_accessed=(MAXB + BR * COLBLK) * BLOCK * BLOCK * 2,
@@ -176,12 +178,31 @@
         panel[k * rows : (k + 1) * rows, :] = part_ref[...]
 
 
-def step_kernel(keep, first, *refs):
-    tiles, refs = refs[:2], refs[2:]
+def fetch_kernel(halves, tile_ref, *refs):
+    *out_refs, sems = refs[-1 - len(halves) :]
+    rows = QUARTER // PIECES
+    copies = []
+    for h, (out_ref, half) in enumerate(zip(out_refs, halves)):
+        for q, quarter in enumerate(half):
+            for k in range(PIECES):
+                part = pl.ds(k * rows, rows)
+                copies.append(
+                    pltpu.make_async_copy(
+                        tile_ref.at[quarter, part], out_ref.at[q, part], sems.at[h, q, k]
+                    )
+                )
+                copies[-1].start()
+    for copy in copies:
+        copy.wait()
+
+
+def step_kernel(first, keep, *refs):
+    tile_ref, refs = refs[0], refs[1:]
+    refs, (panel, total) = refs[:-2], refs[-2:]
     row_id, col_id = lax.axis_index("row"), lax.axis_index("col")
     core = col_id & 1
     if first:
-        dealt_ref, out_ref, panel, total = refs[0], refs[1], refs[-2], refs[-1]
+        dealt_ref, out_ref = refs[:2]
         for k in range(COLBLK):
             part = ((row_id // 2 + k // 2) & 3) * 2 + ((row_id ^ k) & 1)
             part = pl.ds(pl.multiple_of(part * BLOCK, BLOCK), BLOCK)
@@ -189,10 +210,10 @@
         if not keep:
             refs[2][...] = panel[:PAIR, :]
     else:
-        out_ref, panel, total = refs[4:]
+        out_ref = refs[4]
         put_together(refs[:4], panel)
     for i in range(2):
-        terms = dot(tiles[i][...], panel[...])
+        terms = dot(tile_ref[i], panel[...])
         terms = terms.reshape(HALF, HALF, RUN, terms.shape[1])
         for t in range(HALF):
             away = ((t // 2 - col_id // 4) & 3) * 2 + ((t ^ (col_id // 2)) & 1)
@@ -200,13 +221,13 @@
     out_ref[...] = total[...].reshape(out_ref.shape).astype(out_ref.dtype)
 
 
-def last_kernel(keep, *refs):
-    tiles, parts, (first_ref, out_ref, panel, total) = refs[:2], refs[2:6], refs[6:]
+def last_kernel(keep, tile_ref, *refs):
+    parts, (first_ref, out_ref, panel, total) = refs[:4], refs[4:]
     put_together(parts, panel)
     col_id = lax.axis_index("col")
     core = col_id & 1
     for j in range(2):
-        terms = dot(tiles[j][...], panel[...])
+        terms = dot(tile_ref[j], panel[...])
         terms = terms.reshape(HALF, HALF, RUN, terms.shape[1])
         for t in range(HALF):
             total[:, t, core if j else 1 - core] = terms[t]
@@ -284,63 +305,66 @@
         pltpu.VMEM((COLBLK * BLOCK, width), BF16),
         pltpu.VMEM((HALF, HALF, 2, RUN, width), F32),
     ]
-
-    def step(tiles, parts, first, previous):
+    sems = pltpu.SemaphoreType.DMA((2, 2, PIECES))
+    quarters = (2, QUARTER, COLBLK * BLOCK)
+
+    def fetch(tile, *halves, after=()):
+        kernel = functools.partial(fetch_kernel, halves)
+        return small_call(kernel, "fetch", [quarters] * len(halves), after, [sems], 0, tile)
+
+    def product(kernel, name, fetched, operands, more=()):
         wide = (half_rows, width)
-        sent, *pair = small_call(
-            functools.partial(step_kernel, False, first),
-            "send",
-            [wide] + ([(PAIR, width)] if first else []),
-            (tiles[0], tiles[1]) + parts,
+        sent, *rest = small_call(
+            functools.partial(kernel, False),
+            name + "_send",
+            [wide, *more],
+            (fetched[0], *operands),
             scratch,
             flops,
         )
-        previous = pair[0] if first else previous
         arrived = other_core(sent)
         (kept,) = small_call(
-            functools.partial(step_kernel, True, first),
-            "keep",
+            functools.partial(kernel, True),
+            name + "_keep",
             [wide],
-            (tiles[2], tiles[3]) + parts,
+            (fetched[1], *operands),
             scratch,
             flops,
         )
-        terms = small_call(add_kernel, "add", [(PAIR, width)] * 4, (kept, arrived))
+        return (kept, arrived), rest
+
+    def step(tile, fetched, parts, first, previous, which):
+        kernel = functools.partial(step_kernel, first)
+        more = [(PAIR, width)] if first else []
+        terms, rest = product(kernel, "first" if first else "step", fetched, parts, more)
+        terms = small_call(add_kernel, "add", [(PAIR, width)] * 4, terms)
         arrived = [along_x(terms[k], k) for k in (2, 1, 3)]
+        fetched = fetch(tile, *which, after=(terms[0],))
         own, other = small_call(
             sum_kernel, "sum_x", [(BLOCK, width)] * 2, (terms[0], *arrived)
         )
-        arrived, far, near = far_z(other), both_z(other), near_z(own)
+        near, far, arrived = near_z(own), both_z(other), far_z(other)
         operands = (own, arrived, near, far) + (() if first else (previous,))
         (pair,) = small_call(
             functools.partial(next_kernel, 2.0), "next", [(PAIR, width)], operands
         )
-        sides = {k: along_y(pair, k) for k in (2, 1, 3)}
-        return (pair, sides[3], sides[2], sides[1]), previous
+        sides = {k: along_y(pair, k) for k in (1, 3, 2)}
+        return (pair, sides[3], sides[2], sides[1]), fetched, (rest[0] if first else None)
 
     with jax.named_scope("merge"):
-        tiles = merge(block_rows[0, 0], block_cols[0, 0], counts[0], blocks[0, 0])
+        tile = merge(block_rows[0, 0], block_cols[0, 0], counts[0], blocks[0, 0])
     with jax.named_scope("deal"):
         panel = exchange(copies(vectors, row_count).reshape(devices, RUN, width), ("row", "col"))
         panel = panel.reshape(row_count * shard_rows, width)
     with jax.named_scope("step1"):
-        parts, previous = step(tiles, (panel,), True, None)
+        fetched = [*fetch(tile, (0, 1)), *fetch(tile, (2, 3))]
+        parts, fetched, previous = step(tile, fetched, (panel,), True, None, ((0, 1), (2, 3)))
         first = parts[0]
     with jax.named_scope("step2"):
-        parts, _ = step(tiles, parts, False, previous)
+        parts, fetched, _ = step(tile, fetched, parts, False, previous, ((0, 2), (1, 3)))
     with jax.named_scope("step3"):
-        halves = []
-        for keep in (False, True):
-            (half,) = small_call(
-                functools.partial(last_kernel, keep),
-                "last_keep" if keep else "last_send",
-                [(half_rows, width)],
-                (tiles[int(keep)], tiles[2 + int(keep)]) + parts + (first,),
-                scratch,
-                flops,
-            )
-            halves.append(half if keep else other_core(half))
-        (terms,) = small_call(add_kernel, "add", [(half_rows, width)], tuple(halves))
+        terms, _ = product(last_kernel, "last", fetched, parts + (first,))
+        (terms,) = small_call(add_kernel, "add", [(half_rows, width)], terms)
         same_core = [list(range(c, col_count, 2)) for c in range(2)]
         arrived = exchange(terms.reshape(HALF, shard_rows, width), "col", same_core)
         summed = jnp.sum(arrived.astype(F32), axis=0)

time: 128 us -> 123 us (0.961)
  waiting for transfers between devices: 36.9 us -> 26.8 us
  Pallas kernels: 14 us -> 23.4 us
  local copies, waits for them, and re-layouts: 7.43 us -> 0.07 us
  starting transfers between devices: 38.1 us -> 40.2 us
    ppermute x6, waiting for transfers between devices: 11.1 us -> 1.57 us  [along_y(): lax.ppermute(x, 'row', [(i, (i + 2 * k) % row_count) for i in range(row_c...]
    pallas_call x14 -> x18, Pallas kernels: 12.2 us -> 21.6 us  [the longest x17 15.8 us: small_call(): pl.pallas_call(kernel, out_shape=outs, in_specs=[HBM] * len(tiles) + [VME...]
    unnamed x22 -> x6, local copies, waits for them, and re-layouts: 7.37 us -> 0.02 us
    ppermute x6, starting transfers between devices: 4.46 us -> 6.22 us  [along_y(): lax.ppermute(x, 'row', [(i, (i + 2 * k) % row_count) for i in range(row_c...]
  transfers between devices with their start and end apart: 22 -> 22, of which waited for: 18 -> 15; matrix products, arithmetic and copies ran while one was open for 0% -> 0% of each run, Pallas kernels for 7% -> 15%
where the time goes in v3:
time: 123 us; the launch traced here: 122 us
  starting transfers between devices  40.2 us (33%)
  blocking collectives  29.4 us (24%)
  waiting for transfers between devices  26.8 us (22%)
  Pallas kernels  23.4 us (19%)
  between operations  1.49 us (1%)
    all_to_all x2, blocking collectives, exchange(): lax.all_to_all(parts, axes, split_axis=0, concat_axis=0, tiled=True, axis...  29.4 us
    pallas_call x17, Pallas kernels, small_call(): pl.pallas_call(kernel, out_shape=outs, in_specs=[HBM] * len(tiles) + [VME...  15.8 us
    ppermute x6, waiting for transfers between devices, along_x(): lax.ppermute(x, 'col', [(i, (i + 4 * k) % col_count) for i in range(col_c...  12 us
    all_to_all x1, starting transfers between devices, exchange(): lax.all_to_all(parts, axes, split_axis=0, concat_axis=0, tiled=True, axis...  11.5 us
    ppermute x3, starting transfers between devices, other_core(): return lax.ppermute(x, 'col', [(i, i ^ 1) for i in range(col_count)])  8.23 us
    ppermute x6, starting transfers between devices, along_x(): lax.ppermute(x, 'col', [(i, (i + 4 * k) % col_count) for i in range(col_c...  7.62 us
    ppermute x6, starting transfers between devices, along_y(): lax.ppermute(x, 'row', [(i, (i + 2 * k) % row_count) for i in range(row_c...  6.22 us
    pallas_call x1, Pallas kernels, merge(): pl.pallas_call(merge_kernel, out_shape=jax.ShapeDtypeStruct((ROOM,) + qua...  5.81 us
  transfers between devices with their start and end apart: 22, of which 15 were waited for; matrix products, arithmetic and copies ran while one was open for 0% of the time, Pallas kernels for 15%

profile of v3, /device:TPU:1, one launch (start us, length us, event | category | flops | bytes accessed | tf_op | source)
XLA Modules:
  0.0 122.4 jit_solution(8049165597073455441)
XLA Ops:
  0.6 1.7 %copies.1 = bf16[8,128,256]{2,1,0:T(8,128)(2,1)} custom-call(bf16[128,256]{1,0:T(8,128)(2,1)} %own_ref.1), custom_call_target="tpu_custom_call" | custom-call | tf_op jit(solution)/shard_map/deal/copies/pallas_call | solution.py:156
  2.4 11.5 %all-to-all-start = ((bf16[128,8,256]{2,1,0:T(8,128)(2,1)}), bf16[128,8,256]{2,1,0:T(8,128)(2,1)S(1)}, u32[]{:S(2)}, u32[]{:S(2)}) async-start(bf16[128,8,256]{2,1,0:T(8,128)(2,1)} %bitcast.14), calls=%async_computation | async-start | bytes 1048576 | tf_op jit(solution)/shard_map/deal/all_to_all | solution.py:277
  14.5 5.8 %merge_blocks.1.tile_ref = bf16[16,512,1024]{2,1,0:T(8,128)(2,1)} custom-call(s32[256]{0:T(256)} %bitcast.15, s32[256]{0:T(256)} %bitcast.16, s32[1]{0:T(128)} %bitcast.9.stored_ref, bf16[256,128,128]{2,1,0:T(8,128)(2,1)} %bitcast.13), custom_call_target="tpu_custom_call" | custom-call | flops 4194304 | bytes 12582912 | tf_op jit(solution)/shard_map/merge/merge_blocks/pallas_call | solution.py:116
  20.3 1.6 %fetch.5.refs_0_ = bf16[2,512,1024]{2,1,0:T(8,128)(2,1)S(1)} custom-call(bf16[16,512,1024]{2,1,0:T(8,128)(2,1)} %merge_blocks.1.tile_ref), custom_call_target="tpu_custom_call" | custom-call | bytes 2097152 | tf_op jit(solution)/shard_map/step1/fetch/pallas_call | solution.py:35
  22.0 5.4 %all-to-all-done = bf16[128,8,256]{2,1,0:T(8,128)(2,1)S(1)} async-done(((bf16[128,8,256]{2,1,0:T(8,128)(2,1)}), bf16[128,8,256]{2,1,0:T(8,128)(2,1)S(1)}, u32[]{:S(2)}, u32[]{:S(2)}) %all-to-all-start) | async-done | bytes 524320 | tf_op jit(solution)/shard_map/deal/all_to_all | solution.py:277
  27.4 0.8 first_send.1
  28.2 1.2 collective-permute-start
  29.4 1.6 %fetch.4.refs_0_ = bf16[2,512,1024]{2,1,0:T(8,128)(2,1)S(1)} custom-call(bf16[16,512,1024]{2,1,0:T(8,128)(2,1)} %merge_blocks.1.tile_ref), custom_call_target="tpu_custom_call" | custom-call | bytes 2097152 | tf_op jit(solution)/shard_map/step1/fetch/pallas_call | solution.py:35
  31.1 0.8 first_keep.1.a_ref
  31.9 0.0 collective-permute-done.b_ref
  31.9 0.1 add.3
  32.0 1.1 collective-permute-start.1
  33.2 0.4 collective-permute-start.2
  33.5 2.3 %collective-permute-start.3 = (bf16[256,256]{1,0:T(8,128)(2,1)S(1)}, bf16[256,256]{1,0:T(8,128)(2,1)S(1)}, u32[]{:S(2)}, u32[]{:S(2)}) collective-permute-start(bf16[256,256]{1,0:T(8,128)(2,1)S(1)} %get-tuple-element.25), channel_id=1, source_target_pairs={{0,12},{1,13},{2,14},{3,15},{4,0},{5,1},{6,2},{7,3},{8,4},{9,5},{1... | collective-permute-start | bytes 393224 | tf_op jit(solution)/shard_map/step1/ppermute | solution.py:285
  35.9 2.9 %collective-permute-done.1.b_ref = bf16[256,256]{1,0:T(8,128)(2,1)S(1)} collective-permute-done((bf16[256,256]{1,0:T(8,128)(2,1)S(1)}, bf16[256,256]{1,0:T(8,128)(2,1)S(1)}, u32[]{:S(2)}, u32[]{:S(2)}) %collective-permute-start.1) | collective-permute-done | bytes 131104 | tf_op jit(solution)/shard_map/step1/ppermute | solution.py:285
  38.8 3.1 %collective-permute-done.2.c_ref = bf16[256,256]{1,0:T(8,128)(2,1)S(1)} collective-permute-done((bf16[256,256]{1,0:T(8,128)(2,1)S(1)}, bf16[256,256]{1,0:T(8,128)(2,1)S(1)}, u32[]{:S(2)}, u32[]{:S(2)}) %collective-permute-start.2) | collective-permute-done | bytes 131104 | tf_op jit(solution)/shard_map/step1/ppermute | solution.py:285
  41.9 0.0 collective-permute-done.3.d_ref
  41.9 0.1 sum_x.2
  42.0 0.2 collective-permute-start.5
  42.2 0.9 collective-permute-start.6
  43.1 2.2 %collective-permute-start.4 = (bf16[128,256]{1,0:T(8,128)(2,1)S(1)}, bf16[128,256]{1,0:T(8,128)(2,1)S(1)}, u32[]{:S(2)}, u32[]{:S(2)}) collective-permute-start(bf16[128,256]{1,0:T(8,128)(2,1)S(1)} %get-tuple-element.27), channel_id=1, source_target_pairs={{0,2},{1,3},{2,0},{3,1},{4,6},{5,7},{6,4},{7,5},{8,10},{9,11},{10,... | collective-permute-start | bytes 196616 | tf_op jit(solution)/shard_map/step1/ppermute | solution.py:294
  45.3 1.2 %collective-permute-done.6.far_ref = bf16[128,256]{1,0:T(8,128)(2,1)S(1)} collective-permute-done((bf16[128,256]{1,0:T(8,128)(2,1)S(1)}, bf16[128,256]{1,0:T(8,128)(2,1)S(1)}, u32[]{:S(2)}, u32[]{:S(2)}) %collective-permute-start.6) | collective-permute-done | bytes 65568 | tf_op jit(solution)/shard_map/step1/ppermute | solution.py:302
  46.5 1.2 %collective-permute-done.4.arrived_ref = bf16[128,256]{1,0:T(8,128)(2,1)S(1)} collective-permute-done((bf16[128,256]{1,0:T(8,128)(2,1)S(1)}, bf16[128,256]{1,0:T(8,128)(2,1)S(1)}, u32[]{:S(2)}, u32[]{:S(2)}) %collective-permute-start.4) | collective-permute-done | bytes 65568 | tf_op jit(solution)/shard_map/step1/ppermute | solution.py:294
  47.8 0.1 collective-permute-start.9
  47.9 1.9 %collective-permute-start.8 = (bf16[256,256]{1,0:T(8,128)(2,1)S(1)}, bf16[256,256]{1,0:T(8,128)(2,1)S(1)}, u32[]{:S(2)}, u32[]{:S(2)}) collective-permute-start(bf16[256,256]{1,0:T(8,128)(2,1)S(1)} %next.2.refs_1_.refs_4_), channel_id=1, source_target_pairs={{0,64},{16,80},{32,96},{48,112},{64,0},{80,16},{96,32},{112,48},{1... | collective-permute-start | bytes 393224 | tf_op jit(solution)/shard_map/step1/ppermute | solution.py:288
  49.8 0.7 collective-permute-start.7
  50.5 3.6 %fetch.6 = (bf16[2,512,1024]{2,1,0:T(8,128)(2,1)S(1)}, bf16[2,512,1024]{2,1,0:T(8,128)(2,1)}) custom-call(bf16[16,512,1024]{2,1,0:T(8,128)(2,1)} %merge_blocks.1.tile_ref, bf16[256,256]{1,0:T(8,128)(2,1)S(1)} %get-tuple-element.21.refs_0_.a_ref), custom_call_target="tpu_custom_call" | custom-call | bytes 4325376 | tf_op jit(solution)/shard_map/step1/fetch/pallas_call | solution.py:35
  54.1 0.6 collective-permute-done.9.refs_4_
  54.7 0.5 collective-permute-done.7.refs_2_
  55.2 0.8 step_send.1
  56.0 3.3 %collective-permute-start.10 = (bf16[1024,256]{1,0:T(8,128)(2,1)S(1)}, bf16[1024,256]{1,0:T(8,128)(2,1)S(1)}, u32[]{:S(2)}, u32[]{:S(2)}) collective-permute-start(bf16[1024,256]{1,0:T(8,128)(2,1)S(1)} %step_send.1), channel_id=1, source_target_pairs={{0,1},{1,0},{2,3},{3,2},{4,5},{5,4},{6,7},{7,6},{8,9},{9,8},{10,11... | collective-permute-start | bytes 1572872 | tf_op jit(solution)/shard_map/step2/ppermute | solution.py:282
  59.4 0.8 step_keep.1.a_ref
  60.2 0.7 collective-permute-done.10.b_ref
  60.9 0.1 add.4
  61.0 1.1 collective-permute-start.11
  62.1 0.2 collective-permute-start.12
  62.3 2.5 %collective-permute-start.13 = (bf16[256,256]{1,0:T(8,128)(2,1)S(1)}, bf16[256,256]{1,0:T(8,128)(2,1)S(1)}, u32[]{:S(2)}, u32[]{:S(2)}) collective-permute-start(bf16[256,256]{1,0:T(8,128)(2,1)S(1)} %get-tuple-element.33), channel_id=1, source_target_pairs={{0,12},{1,13},{2,14},{3,15},{4,0},{5,1},{6,2},{7,3},{8,4},{9,5},{1... | collective-permute-start | bytes 393224 | tf_op jit(solution)/shard_map/step2/ppermute | solution.py:285
  64.8 2.5 %collective-permute-done.11.b_ref = bf16[256,256]{1,0:T(8,128)(2,1)S(1)} collective-permute-done((bf16[256,256]{1,0:T(8,128)(2,1)S(1)}, bf16[256,256]{1,0:T(8,128)(2,1)S(1)}, u32[]{:S(2)}, u32[]{:S(2)}) %collective-permute-start.11) | collective-permute-done | bytes 131104 | tf_op jit(solution)/shard_map/step2/ppermute | solution.py:285
  67.3 3.5 %collective-permute-done.12.c_ref = bf16[256,256]{1,0:T(8,128)(2,1)S(1)} collective-permute-done((bf16[256,256]{1,0:T(8,128)(2,1)S(1)}, bf16[256,256]{1,0:T(8,128)(2,1)S(1)}, u32[]{:S(2)}, u32[]{:S(2)}) %collective-permute-start.12) | collective-permute-done | bytes 131104 | tf_op jit(solution)/shard_map/step2/ppermute | solution.py:285
  70.8 0.1 sum_x.3
  70.9 0.6 collective-permute-start.15
  71.5 2.0 %collective-permute-start.16 = (bf16[128,256]{1,0:T(8,128)(2,1)S(1)}, bf16[128,256]{1,0:T(8,128)(2,1)S(1)}, u32[]{:S(2)}, u32[]{:S(2)}) collective-permute-start(bf16[128,256]{1,0:T(8,128)(2,1)S(1)} %get-tuple-element.35), channel_id=1, source_target_pairs={{0,18},{1,19},{2,16},{3,17},{4,22},{5,23},{6,20},{7,21},{8,26},{9,... | collective-permute-start | bytes 196616 | tf_op jit(solution)/shard_map/step2/ppermute | solution.py:302
  73.5 0.8 collective-permute-start.14
  74.2 1.5 %collective-permute-done.16.far_ref = bf16[128,256]{1,0:T(8,128)(2,1)S(1)} collective-permute-done((bf16[128,256]{1,0:T(8,128)(2,1)S(1)}, bf16[128,256]{1,0:T(8,128)(2,1)S(1)}, u32[]{:S(2)}, u32[]{:S(2)}) %collective-permute-start.16) | collective-permute-done | bytes 65568 | tf_op jit(solution)/shard_map/step2/ppermute | solution.py:302
  75.8 2.3 %collective-permute-done.14.arrived_ref = bf16[128,256]{1,0:T(8,128)(2,1)S(1)} collective-permute-done((bf16[128,256]{1,0:T(8,128)(2,1)S(1)}, bf16[128,256]{1,0:T(8,128)(2,1)S(1)}, u32[]{:S(2)}, u32[]{:S(2)}) %collective-permute-start.14) | collective-permute-done | bytes 65568 | tf_op jit(solution)/shard_map/step2/ppermute | solution.py:294
  78.1 0.1 next.3.refs_0_
  78.2 0.4 collective-permute-start.19
  78.5 3.1 %collective-permute-start.18 = (bf16[256,256]{1,0:T(8,128)(2,1)S(1)}, bf16[256,256]{1,0:T(8,128)(2,1)S(1)}, u32[]{:S(2)}, u32[]{:S(2)}) collective-permute-start(bf16[256,256]{1,0:T(8,128)(2,1)S(1)} %next.3.refs_0_), channel_id=1, source_target_pairs={{0,64},{16,80},{32,96},{48,112},{64,0},{80,16},{96,32},{112,48},{1... | collective-permute-start | bytes 393224 | tf_op jit(solution)/shard_map/step2/ppermute | solution.py:288
  81.6 3.6 %fetch.7 = (bf16[2,512,1024]{2,1,0:T(8,128)(2,1)S(1)}, bf16[2,512,1024]{2,1,0:T(8,128)(2,1)}) custom-call(bf16[16,512,1024]{2,1,0:T(8,128)(2,1)} %merge_blocks.1.tile_ref, bf16[256,256]{1,0:T(8,128)(2,1)S(1)} %get-tuple-element.29.refs_0_.a_ref), custom_call_target="tpu_custom_call" | custom-call | bytes 4325376 | tf_op jit(solution)/shard_map/step2/fetch/pallas_call | solution.py:35
  85.3 0.2 collective-permute-done.18.refs_2_
  85.5 0.3 collective-permute-done.17.refs_1_
  85.8 0.8 last_send.1
  86.6 3.7 %collective-permute-start.20 = (bf16[1024,256]{1,0:T(8,128)(2,1)S(1)}, bf16[1024,256]{1,0:T(8,128)(2,1)S(1)}, u32[]{:S(2)}, u32[]{:S(2)}) collective-permute-start(bf16[1024,256]{1,0:T(8,128)(2,1)S(1)} %last_send.1), channel_id=1, source_target_pairs={{0,1},{1,0},{2,3},{3,2},{4,5},{5,4},{6,7},{7,6},{8,9},{9,8},{10,11... | collective-permute-start | bytes 1572872 | tf_op jit(solution)/shard_map/step3/ppermute | solution.py:282
  90.2 0.8 last_keep.1.a_ref
  91.0 0.8 collective-permute-done.20.b_ref
  91.8 0.1 add.5
  91.9 12.7 %all_to_all.15 = bf16[8,128,256]{2,1,0:T(8,128)(2,1)S(1)} all-to-all(bf16[8,128,256]{2,1,0:T(8,128)(2,1)S(1)} %bitcast.12), channel_id=1, replica_groups={{0,2,4,6,8,10,12,14},{1,3,5,7,9,11,13,15},{16,18,20,22,24,26,28,30},{17..., dimensions={0} | all-to-all | bytes 1048576 | tf_op jit(solution)/shard_map/step3/all_to_all | solution.py:277
  104.6 0.1 convert_reduce_fusion
  104.7 0.0 copy-start.2
  104.7 0.2 convolution_convert_fusion
  104.9 0.1 reshape.19
  105.0 16.7 %all_to_all.16 = bf16[128,2,256]{2,1,0:T(2,128)(2,1)S(1)} all-to-all(bf16[128,2,256]{2,1,0:T(2,128)(2,1)S(1)} %reshape.19), channel_id=1, replica_groups=mesh['row'=8,'col'=16] {'row','col'}, dimensions={0} | all-to-all | bytes 262144 | tf_op jit(solution)/shard_map/gram/all_to_all | solution.py:277
  121.7 0.2 convert_reduce_fusion.1
  121.9 0.6 broadcast_multiply_fusion
  (13 shorter events, 0.1 us)
Async XLA Ops:
  2.4 25.0 %all-to-all-start = ((bf16[128,8,256]{2,1,0:T(8,128)(2,1)}), bf16[128,8,256]{2,1,0:T(8,128)(2,1)S(1)}, u32[]{:S(2)}, u32[]{:S(2)}) async-start(bf16[128,8,256]{2,1,0:T(8,128)(2,1)} %bitcast.14), calls=%async_computation | async-start | bytes 1048576 | tf_op jit(solution)/shard_map/deal/all_to_all | solution.py:277
  28.2 3.7 %collective-permute-start = (bf16[1024,256]{1,0:T(8,128)(2,1)S(1)}, bf16[1024,256]{1,0:T(8,128)(2,1)S(1)}, u32[]{:S(2)}, u32[]{:S(2)}) collective-permute-start(bf16[1024,256]{1,0:T(8,128)(2,1)S(1)} %get-tuple-element.20), channel_id=1, source_target_pairs={{0,1},{1,0},{2,3},{3,2},{4,5},{5,4},{6,7},{7,6},{8,9},{9,8},{10,11... | collective-permute-start | bytes 1572872 | tf_op jit(solution)/shard_map/step1/ppermute | solution.py:282
  32.0 6.7 %collective-permute-start.1 = (bf16[256,256]{1,0:T(8,128)(2,1)S(1)}, bf16[256,256]{1,0:T(8,128)(2,1)S(1)}, u32[]{:S(2)}, u32[]{:S(2)}) collective-permute-start(bf16[256,256]{1,0:T(8,128)(2,1)S(1)} %get-tuple-element.23), channel_id=1, source_target_pairs={{0,8},{1,9},{2,10},{3,11},{4,12},{5,13},{6,14},{7,15},{8,0},{9,1},... | collective-permute-start | bytes 393224 | tf_op jit(solution)/shard_map/step1/ppermute | solution.py:285
  33.2 8.7 %collective-permute-start.2 = (bf16[256,256]{1,0:T(8,128)(2,1)S(1)}, bf16[256,256]{1,0:T(8,128)(2,1)S(1)}, u32[]{:S(2)}, u32[]{:S(2)}) collective-permute-start(bf16[256,256]{1,0:T(8,128)(2,1)S(1)} %get-tuple-element.24), channel_id=1, source_target_pairs={{0,4},{1,5},{2,6},{3,7},{4,8},{5,9},{6,10},{7,11},{8,12},{9,13},{1... | collective-permute-start | bytes 393224 | tf_op jit(solution)/shard_map/step1/ppermute | solution.py:285
  33.5 8.3 %collective-permute-start.3 = (bf16[256,256]{1,0:T(8,128)(2,1)S(1)}, bf16[256,256]{1,0:T(8,128)(2,1)S(1)}, u32[]{:S(2)}, u32[]{:S(2)}) collective-permute-start(bf16[256,256]{1,0:T(8,128)(2,1)S(1)} %get-tuple-element.25), channel_id=1, source_target_pairs={{0,12},{1,13},{2,14},{3,15},{4,0},{5,1},{6,2},{7,3},{8,4},{9,5},{1... | collective-permute-start | bytes 393224 | tf_op jit(solution)/shard_map/step1/ppermute | solution.py:285
  42.0 3.3 %collective-permute-start.5 = (bf16[128,256]{1,0:T(8,128)(2,1)S(1)}, bf16[128,256]{1,0:T(8,128)(2,1)S(1)}, u32[]{:S(2)}, u32[]{:S(2)}) collective-permute-start(bf16[128,256]{1,0:T(8,128)(2,1)S(1)} %get-tuple-element.26.own_ref), channel_id=1, source_target_pairs={{0,16},{16,0},{32,48},{48,32},{64,80},{80,64},{96,112},{112,96},{1... | collective-permute-start | bytes 196616 | tf_op jit(solution)/shard_map/step1/ppermute | solution.py:291
  42.2 4.3 %collective-permute-start.6 = (bf16[128,256]{1,0:T(8,128)(2,1)S(1)}, bf16[128,256]{1,0:T(8,128)(2,1)S(1)}, u32[]{:S(2)}, u32[]{:S(2)}) collective-permute-start(bf16[128,256]{1,0:T(8,128)(2,1)S(1)} %get-tuple-element.27), channel_id=1, source_target_pairs={{0,18},{1,19},{2,16},{3,17},{4,22},{5,23},{6,20},{7,21},{8,26},{9,... | collective-permute-start | bytes 196616 | tf_op jit(solution)/shard_map/step1/ppermute | solution.py:302
  43.1 4.7 %collective-permute-start.4 = (bf16[128,256]{1,0:T(8,128)(2,1)S(1)}, bf16[128,256]{1,0:T(8,128)(2,1)S(1)}, u32[]{:S(2)}, u32[]{:S(2)}) collective-permute-start(bf16[128,256]{1,0:T(8,128)(2,1)S(1)} %get-tuple-element.27), channel_id=1, source_target_pairs={{0,2},{1,3},{2,0},{3,1},{4,6},{5,7},{6,4},{7,5},{8,10},{9,11},{10,... | collective-permute-start | bytes 196616 | tf_op jit(solution)/shard_map/step1/ppermute | solution.py:294
  47.8 7.0 %collective-permute-start.9 = (bf16[256,256]{1,0:T(8,128)(2,1)S(1)}, bf16[256,256]{1,0:T(8,128)(2,1)S(1)}, u32[]{:S(2)}, u32[]{:S(2)}) collective-permute-start(bf16[256,256]{1,0:T(8,128)(2,1)S(1)} %next.2.refs_1_.refs_4_), channel_id=1, source_target_pairs={{0,32},{16,48},{32,64},{48,80},{64,96},{80,112},{96,0},{112,16},{1... | collective-permute-start | bytes 393224 | tf_op jit(solution)/shard_map/step1/ppermute | solution.py:288
  47.9 6.9 %collective-permute-start.8 = (bf16[256,256]{1,0:T(8,128)(2,1)S(1)}, bf16[256,256]{1,0:T(8,128)(2,1)S(1)}, u32[]{:S(2)}, u32[]{:S(2)}) collective-permute-start(bf16[256,256]{1,0:T(8,128)(2,1)S(1)} %next.2.refs_1_.refs_4_), channel_id=1, source_target_pairs={{0,64},{16,80},{32,96},{48,112},{64,0},{80,16},{96,32},{112,48},{1... | collective-permute-start | bytes 393224 | tf_op jit(solution)/shard_map/step1/ppermute | solution.py:288
  49.8 5.4 %collective-permute-start.7 = (bf16[256,256]{1,0:T(8,128)(2,1)S(1)}, bf16[256,256]{1,0:T(8,128)(2,1)S(1)}, u32[]{:S(2)}, u32[]{:S(2)}) collective-permute-start(bf16[256,256]{1,0:T(8,128)(2,1)S(1)} %next.2.refs_1_.refs_4_), channel_id=1, source_target_pairs={{0,96},{16,112},{32,0},{48,16},{64,32},{80,48},{96,64},{112,80},{1... | collective-permute-start | bytes 393224 | tf_op jit(solution)/shard_map/step1/ppermute | solution.py:288
  54.1 5.2 %copy-start = (bf16[2,512,1024]{2,1,0:T(8,128)(2,1)S(1)}, bf16[2,512,1024]{2,1,0:T(8,128)(2,1)}, u32[]{:S(2)}) copy-start(bf16[2,512,1024]{2,1,0:T(8,128)(2,1)} %get-tuple-element.22.refs_0_) | copy-start | bytes 6291460
  56.0 4.9 %collective-permute-start.10 = (bf16[1024,256]{1,0:T(8,128)(2,1)S(1)}, bf16[1024,256]{1,0:T(8,128)(2,1)S(1)}, u32[]{:S(2)}, u32[]{:S(2)}) collective-permute-start(bf16[1024,256]{1,0:T(8,128)(2,1)S(1)} %step_send.1), channel_id=1, source_target_pairs={{0,1},{1,0},{2,3},{3,2},{4,5},{5,4},{6,7},{7,6},{8,9},{9,8},{10,11... | collective-permute-start | bytes 1572872 | tf_op jit(solution)/shard_map/step2/ppermute | solution.py:282
  61.0 6.3 %collective-permute-start.11 = (bf16[256,256]{1,0:T(8,128)(2,1)S(1)}, bf16[256,256]{1,0:T(8,128)(2,1)S(1)}, u32[]{:S(2)}, u32[]{:S(2)}) collective-permute-start(bf16[256,256]{1,0:T(8,128)(2,1)S(1)} %get-tuple-element.31), channel_id=1, source_target_pairs={{0,8},{1,9},{2,10},{3,11},{4,12},{5,13},{6,14},{7,15},{8,0},{9,1},... | collective-permute-start | bytes 393224 | tf_op jit(solution)/shard_map/step2/ppermute | solution.py:285
  62.1 8.7 %collective-permute-start.12 = (bf16[256,256]{1,0:T(8,128)(2,1)S(1)}, bf16[256,256]{1,0:T(8,128)(2,1)S(1)}, u32[]{:S(2)}, u32[]{:S(2)}) collective-permute-start(bf16[256,256]{1,0:T(8,128)(2,1)S(1)} %get-tuple-element.32), channel_id=1, source_target_pairs={{0,4},{1,5},{2,6},{3,7},{4,8},{5,9},{6,10},{7,11},{8,12},{9,13},{1... | collective-permute-start | bytes 393224 | tf_op jit(solution)/shard_map/step2/ppermute | solution.py:285
  62.3 8.5 %collective-permute-start.13 = (bf16[256,256]{1,0:T(8,128)(2,1)S(1)}, bf16[256,256]{1,0:T(8,128)(2,1)S(1)}, u32[]{:S(2)}, u32[]{:S(2)}) collective-permute-start(bf16[256,256]{1,0:T(8,128)(2,1)S(1)} %get-tuple-element.33), channel_id=1, source_target_pairs={{0,12},{1,13},{2,14},{3,15},{4,0},{5,1},{6,2},{7,3},{8,4},{9,5},{1... | collective-permute-start | bytes 393224 | tf_op jit(solution)/shard_map/step2/ppermute | solution.py:285
  70.9 3.3 %collective-permute-start.15 = (bf16[128,256]{1,0:T(8,128)(2,1)S(1)}, bf16[128,256]{1,0:T(8,128)(2,1)S(1)}, u32[]{:S(2)}, u32[]{:S(2)}) collective-permute-start(bf16[128,256]{1,0:T(8,128)(2,1)S(1)} %get-tuple-element.34.own_ref), channel_id=1, source_target_pairs={{0,16},{16,0},{32,48},{48,32},{64,80},{80,64},{96,112},{112,96},{1... | collective-permute-start | bytes 196616 | tf_op jit(solution)/shard_map/step2/ppermute | solution.py:291
  71.5 4.3 %collective-permute-start.16 = (bf16[128,256]{1,0:T(8,128)(2,1)S(1)}, bf16[128,256]{1,0:T(8,128)(2,1)S(1)}, u32[]{:S(2)}, u32[]{:S(2)}) collective-permute-start(bf16[128,256]{1,0:T(8,128)(2,1)S(1)} %get-tuple-element.35), channel_id=1, source_target_pairs={{0,18},{1,19},{2,16},{3,17},{4,22},{5,23},{6,20},{7,21},{8,26},{9,... | collective-permute-start | bytes 196616 | tf_op jit(solution)/shard_map/step2/ppermute | solution.py:302
  73.5 4.6 %collective-permute-start.14 = (bf16[128,256]{1,0:T(8,128)(2,1)S(1)}, bf16[128,256]{1,0:T(8,128)(2,1)S(1)}, u32[]{:S(2)}, u32[]{:S(2)}) collective-permute-start(bf16[128,256]{1,0:T(8,128)(2,1)S(1)} %get-tuple-element.35), channel_id=1, source_target_pairs={{0,2},{1,3},{2,0},{3,1},{4,6},{5,7},{6,4},{7,5},{8,10},{9,11},{10,... | collective-permute-start | bytes 196616 | tf_op jit(solution)/shard_map/step2/ppermute | solution.py:294
  78.2 7.1 %collective-permute-start.19 = (bf16[256,256]{1,0:T(8,128)(2,1)S(1)}, bf16[256,256]{1,0:T(8,128)(2,1)S(1)}, u32[]{:S(2)}, u32[]{:S(2)}) collective-permute-start(bf16[256,256]{1,0:T(8,128)(2,1)S(1)} %next.3.refs_0_), channel_id=1, source_target_pairs={{0,32},{16,48},{32,64},{48,80},{64,96},{80,112},{96,0},{112,16},{1... | collective-permute-start | bytes 393224 | tf_op jit(solution)/shard_map/step2/ppermute | solution.py:288
  78.5 7.0 %collective-permute-start.18 = (bf16[256,256]{1,0:T(8,128)(2,1)S(1)}, bf16[256,256]{1,0:T(8,128)(2,1)S(1)}, u32[]{:S(2)}, u32[]{:S(2)}) collective-permute-start(bf16[256,256]{1,0:T(8,128)(2,1)S(1)} %next.3.refs_0_), channel_id=1, source_target_pairs={{0,64},{16,80},{32,96},{48,112},{64,0},{80,16},{96,32},{112,48},{1... | collective-permute-start | bytes 393224 | tf_op jit(solution)/shard_map/step2/ppermute | solution.py:288
  81.6 4.1 %collective-permute-start.17 = (bf16[256,256]{1,0:T(8,128)(2,1)S(1)}, bf16[256,256]{1,0:T(8,128)(2,1)S(1)}, u32[]{:S(2)}, u32[]{:S(2)}) collective-permute-start(bf16[256,256]{1,0:T(8,128)(2,1)S(1)} %next.3.refs_0_), channel_id=1, source_target_pairs={{0,96},{16,112},{32,0},{48,16},{64,32},{80,48},{96,64},{112,80},{1... | collective-permute-start | bytes 393224 | tf_op jit(solution)/shard_map/step2/ppermute | solution.py:288
  85.2 5.0 %copy-start.1 = (bf16[2,512,1024]{2,1,0:T(8,128)(2,1)S(1)}, bf16[2,512,1024]{2,1,0:T(8,128)(2,1)}, u32[]{:S(2)}) copy-start(bf16[2,512,1024]{2,1,0:T(8,128)(2,1)} %get-tuple-element.30.tile_ref) | copy-start | bytes 6291460
  86.6 5.2 %collective-permute-start.20 = (bf16[1024,256]{1,0:T(8,128)(2,1)S(1)}, bf16[1024,256]{1,0:T(8,128)(2,1)S(1)}, u32[]{:S(2)}, u32[]{:S(2)}) collective-permute-start(bf16[1024,256]{1,0:T(8,128)(2,1)S(1)} %last_send.1), channel_id=1, source_target_pairs={{0,1},{1,0},{2,3},{3,2},{4,5},{5,4},{6,7},{7,6},{8,9},{9,8},{10,11... | collective-permute-start | bytes 1572872 | tf_op jit(solution)/shard_map/step3/ppermute | solution.py:282
  104.7 17.7 %copy-start.2 = (bf16[128,256]{1,0:T(8,128)(2,1)}, bf16[128,256]{1,0:T(8,128)(2,1)S(1)}, u32[]{:S(2)}) copy-start(bf16[128,256]{1,0:T(8,128)(2,1)S(1)} %multiply_convert_fusion) | copy-start | bytes 196612

commit v4 on v3

--- a/solution.py
+++ b/solution.py
@@ -17,6 +17,7 @@
 PAIR = 2 * BLOCK
 CHUNK = 16
 UNROLL = 16
+PANEL_ORDER = (0, 2, 3, 1)
 PIECES = 4
 MERGE_VMEM = 60 * 1024 * 1024
 SMALL_VMEM = 8 * 1024 * 1024
@@ -211,7 +212,7 @@
             refs[2][...] = panel[:PAIR, :]
     else:
         out_ref = refs[4]
-        put_together(refs[:4], panel)
+        put_together([refs[k] for k in PANEL_ORDER], panel)
     for i in range(2):
         terms = dot(tile_ref[i], panel[...])
         terms = terms.reshape(HALF, HALF, RUN, terms.shape[1])
@@ -223,7 +224,7 @@
 
 def last_kernel(keep, tile_ref, *refs):
     parts, (first_ref, out_ref, panel, total) = refs[:4], refs[4:]
-    put_together(parts, panel)
+    put_together([parts[k] for k in PANEL_ORDER], panel)
     col_id = lax.axis_index("col")
     core = col_id & 1
     for j in range(2):
@@ -254,7 +255,7 @@
         out_ref[...] = ((terms[0] + terms[1]) + (terms[2] + terms[3])).astype(BF16)
 
 
-def next_kernel(scale, own_ref, arrived_ref, near_ref, far_ref, *refs):
+def next_kernel(scale, own_ref, arrived_ref, far_ref, near_ref, *refs):
     out_ref = refs[-1]
     pairs = ((own_ref, arrived_ref), (near_ref, far_ref))
     for k, (a_ref, b_ref) in enumerate(pairs):
@@ -344,12 +345,12 @@
             sum_kernel, "sum_x", [(BLOCK, width)] * 2, (terms[0], *arrived)
         )
         near, far, arrived = near_z(own), both_z(other), far_z(other)
-        operands = (own, arrived, near, far) + (() if first else (previous,))
+        operands = (own, arrived, far, near) + (() if first else (previous,))
         (pair,) = small_call(
             functools.partial(next_kernel, 2.0), "next", [(PAIR, width)], operands
         )
         sides = {k: along_y(pair, k) for k in (1, 3, 2)}
-        return (pair, sides[3], sides[2], sides[1]), fetched, (rest[0] if first else None)
+        return (pair, sides[1], sides[3], sides[2]), fetched, (rest[0] if first else None)
 
     with jax.named_scope("merge"):
         tile = merge(block_rows[0, 0], block_cols[0, 0], counts[0], blocks[0, 0])
@@ -370,9 +371,9 @@
         summed = jnp.sum(arrived.astype(F32), axis=0)
         filtered = (2.0 * summed).astype(BF16)
     with jax.named_scope("gram"):
-        local = dot(filtered.T, filtered).astype(BF16)
+        local = (dot(filtered.T, filtered) / (BR * BLOCK // col_count)).astype(BF16)
         arrived = exchange(local.reshape(devices, width // devices, width), ("row", "col"))
-        gram = jnp.sum(arrived.astype(F32), axis=0) / (BR * BLOCK // col_count)
+        gram = jnp.sum(arrived.astype(F32), axis=0)
     return filtered, gram
 
 

time: 123 us -> 122 us (level)
  starting transfers between devices: 40.2 us -> 37.2 us
  waiting for transfers between devices: 26.8 us -> 29.4 us
  blocking collectives: 29.4 us -> 28 us
    ppermute x6, waiting for transfers between devices: 1.57 us -> 4.76 us  [along_y(): lax.ppermute(x, 'row', [(i, (i + 2 * k) % row_count) for i in range(row_c...]
    ppermute x6, starting transfers between devices: 6.22 us -> 4.11 us  [along_y(): lax.ppermute(x, 'row', [(i, (i + 2 * k) % row_count) for i in range(row_c...]
    all_to_all x2, blocking collectives: 29.4 us -> 28 us  [exchange(): lax.all_to_all(parts, axes, split_axis=0, concat_axis=0, tiled=True, axis...]
  transfers between devices with their start and end apart: 22 -> 22, of which waited for: 15 -> 14; matrix products, arithmetic and copies ran while one was open for 0% -> 0% of each run, Pallas kernels for 15% -> 16%
where the time goes in v4:
time: 122 us; the launch traced here: 121 us
  starting transfers between devices  37.2 us (30%)
  waiting for transfers between devices  29.4 us (24%)
  blocking collectives  28 us (23%)
  Pallas kernels  23.9 us (20%)
  between operations  1.5 us (1%)
    all_to_all x2, blocking collectives, exchange(): lax.all_to_all(parts, axes, split_axis=0, concat_axis=0, tiled=True, axis...  28 us
    pallas_call x17, Pallas kernels, small_call(): pl.pallas_call(kernel, out_shape=outs, in_specs=[HBM] * len(tiles) + [VME...  15.8 us
    ppermute x6, waiting for transfers between devices, along_x(): lax.ppermute(x, 'col', [(i, (i + 4 * k) % col_count) for i in range(col_c...  11.9 us
    all_to_all x1, starting transfers between devices, exchange(): lax.all_to_all(parts, axes, split_axis=0, concat_axis=0, tiled=True, axis...  11.5 us
    ppermute x6, starting transfers between devices, along_x(): lax.ppermute(x, 'col', [(i, (i + 4 * k) % col_count) for i in range(col_c...  7.75 us
    ppermute x3, starting transfers between devices, other_core(): return lax.ppermute(x, 'col', [(i, i ^ 1) for i in range(col_count)])  7.16 us
    pallas_call x1, Pallas kernels, merge(): pl.pallas_call(merge_kernel, out_shape=jax.ShapeDtypeStruct((ROOM,) + qua...  6.37 us
    all_to_all x1, waiting for transfers between devices, exchange(): lax.all_to_all(parts, axes, split_axis=0, concat_axis=0, tiled=True, axis...  4.85 us
  transfers between devices with their start and end apart: 22, of which 14 were waited for; matrix products, arithmetic and copies ran while one was open for 0% of the time, Pallas kernels for 16%

profile of v4, /device:TPU:1, one launch (start us, length us, event | category | flops | bytes accessed | tf_op | source)
XLA Modules:
  0.0 121.2 jit_solution(12599376061324968181)
XLA Ops:
  0.6 1.7 %copies.1 = bf16[8,128,256]{2,1,0:T(8,128)(2,1)} custom-call(bf16[128,256]{1,0:T(8,128)(2,1)} %own_ref.1), custom_call_target="tpu_custom_call" | custom-call | tf_op jit(solution)/shard_map/deal/copies/pallas_call | solution.py:157
  2.4 11.5 %all-to-all-start = ((bf16[128,8,256]{2,1,0:T(8,128)(2,1)}), bf16[128,8,256]{2,1,0:T(8,128)(2,1)S(1)}, u32[]{:S(2)}, u32[]{:S(2)}) async-start(bf16[128,8,256]{2,1,0:T(8,128)(2,1)} %bitcast.14), calls=%async_computation | async-start | bytes 1048576 | tf_op jit(solution)/shard_map/deal/all_to_all | solution.py:278
  14.5 6.4 %merge_blocks.1.tile_ref = bf16[16,512,1024]{2,1,0:T(8,128)(2,1)} custom-call(s32[256]{0:T(256)} %bitcast.15, s32[256]{0:T(256)} %bitcast.16, s32[1]{0:T(128)} %bitcast.9.stored_ref, bf16[256,128,128]{2,1,0:T(8,128)(2,1)} %bitcast.13), custom_call_target="tpu_custom_call" | custom-call | flops 4194304 | bytes 12582912 | tf_op jit(solution)/shard_map/merge/merge_blocks/pallas_call | solution.py:117
  20.9 1.6 %fetch.5.refs_0_ = bf16[2,512,1024]{2,1,0:T(8,128)(2,1)S(1)} custom-call(bf16[16,512,1024]{2,1,0:T(8,128)(2,1)} %merge_blocks.1.tile_ref), custom_call_target="tpu_custom_call" | custom-call | bytes 2097152 | tf_op jit(solution)/shard_map/step1/fetch/pallas_call | solution.py:36
  22.6 4.9 %all-to-all-done = bf16[128,8,256]{2,1,0:T(8,128)(2,1)S(1)} async-done(((bf16[128,8,256]{2,1,0:T(8,128)(2,1)}), bf16[128,8,256]{2,1,0:T(8,128)(2,1)S(1)}, u32[]{:S(2)}, u32[]{:S(2)}) %all-to-all-start) | async-done | bytes 524320 | tf_op jit(solution)/shard_map/deal/all_to_all | solution.py:278
  27.4 0.8 first_send.1
  28.2 1.2 %collective-permute-start = (bf16[1024,256]{1,0:T(8,128)(2,1)S(1)}, bf16[1024,256]{1,0:T(8,128)(2,1)S(1)}, u32[]{:S(2)}, u32[]{:S(2)}) collective-permute-start(bf16[1024,256]{1,0:T(8,128)(2,1)S(1)} %get-tuple-element.20), channel_id=1, source_target_pairs={{0,1},{1,0},{2,3},{3,2},{4,5},{5,4},{6,7},{7,6},{8,9},{9,8},{10,11... | collective-permute-start | bytes 1572872 | tf_op jit(solution)/shard_map/step1/ppermute | solution.py:283
  29.4 1.6 %fetch.4.refs_0_ = bf16[2,512,1024]{2,1,0:T(8,128)(2,1)S(1)} custom-call(bf16[16,512,1024]{2,1,0:T(8,128)(2,1)} %merge_blocks.1.tile_ref), custom_call_target="tpu_custom_call" | custom-call | bytes 2097152 | tf_op jit(solution)/shard_map/step1/fetch/pallas_call | solution.py:36
  31.1 0.8 first_keep.1.a_ref
  31.9 0.0 collective-permute-done.b_ref
  31.9 0.1 add.3
  32.0 1.1 collective-permute-start.1
  33.2 0.4 collective-permute-start.2
  33.5 2.3 %collective-permute-start.3 = (bf16[256,256]{1,0:T(8,128)(2,1)S(1)}, bf16[256,256]{1,0:T(8,128)(2,1)S(1)}, u32[]{:S(2)}, u32[]{:S(2)}) collective-permute-start(bf16[256,256]{1,0:T(8,128)(2,1)S(1)} %get-tuple-element.25), channel_id=1, source_target_pairs={{0,12},{1,13},{2,14},{3,15},{4,0},{5,1},{6,2},{7,3},{8,4},{9,5},{1... | collective-permute-start | bytes 393224 | tf_op jit(solution)/shard_map/step1/ppermute | solution.py:286
  35.9 2.9 %collective-permute-done.1.b_ref = bf16[256,256]{1,0:T(8,128)(2,1)S(1)} collective-permute-done((bf16[256,256]{1,0:T(8,128)(2,1)S(1)}, bf16[256,256]{1,0:T(8,128)(2,1)S(1)}, u32[]{:S(2)}, u32[]{:S(2)}) %collective-permute-start.1) | collective-permute-done | bytes 131104 | tf_op jit(solution)/shard_map/step1/ppermute | solution.py:286
  38.8 3.1 %collective-permute-done.2.c_ref = bf16[256,256]{1,0:T(8,128)(2,1)S(1)} collective-permute-done((bf16[256,256]{1,0:T(8,128)(2,1)S(1)}, bf16[256,256]{1,0:T(8,128)(2,1)S(1)}, u32[]{:S(2)}, u32[]{:S(2)}) %collective-permute-start.2) | collective-permute-done | bytes 131104 | tf_op jit(solution)/shard_map/step1/ppermute | solution.py:286
  41.9 0.0 collective-permute-done.3.d_ref
  41.9 0.1 sum_x.2
  42.0 0.2 collective-permute-start.6
  42.2 0.9 collective-permute-start.5
  43.1 2.2 %collective-permute-start.4 = (bf16[128,256]{1,0:T(8,128)(2,1)S(1)}, bf16[128,256]{1,0:T(8,128)(2,1)S(1)}, u32[]{:S(2)}, u32[]{:S(2)}) collective-permute-start(bf16[128,256]{1,0:T(8,128)(2,1)S(1)} %get-tuple-element.27), channel_id=1, source_target_pairs={{0,2},{1,3},{2,0},{3,1},{4,6},{5,7},{6,4},{7,5},{8,10},{9,11},{10,... | collective-permute-start | bytes 196616 | tf_op jit(solution)/shard_map/step1/ppermute | solution.py:295
  45.3 0.0 collective-permute-done.6.near_ref
  45.3 1.2 %collective-permute-done.5.far_ref = bf16[128,256]{1,0:T(8,128)(2,1)S(1)} collective-permute-done((bf16[128,256]{1,0:T(8,128)(2,1)S(1)}, bf16[128,256]{1,0:T(8,128)(2,1)S(1)}, u32[]{:S(2)}, u32[]{:S(2)}) %collective-permute-start.5) | collective-permute-done | bytes 65568 | tf_op jit(solution)/shard_map/step1/ppermute | solution.py:303
  46.5 1.2 %collective-permute-done.4.arrived_ref = bf16[128,256]{1,0:T(8,128)(2,1)S(1)} collective-permute-done((bf16[128,256]{1,0:T(8,128)(2,1)S(1)}, bf16[128,256]{1,0:T(8,128)(2,1)S(1)}, u32[]{:S(2)}, u32[]{:S(2)}) %collective-permute-start.4) | collective-permute-done | bytes 65568 | tf_op jit(solution)/shard_map/step1/ppermute | solution.py:295
  47.8 0.6 collective-permute-start.9
  48.3 1.9 %collective-permute-start.8 = (bf16[256,256]{1,0:T(8,128)(2,1)S(1)}, bf16[256,256]{1,0:T(8,128)(2,1)S(1)}, u32[]{:S(2)}, u32[]{:S(2)}) collective-permute-start(bf16[256,256]{1,0:T(8,128)(2,1)S(1)} %next.2.refs_1_.refs_4_), channel_id=1, source_target_pairs={{0,96},{16,112},{32,0},{48,16},{64,32},{80,48},{96,64},{112,80},{1... | collective-permute-start | bytes 393224 | tf_op jit(solution)/shard_map/step1/ppermute | solution.py:289
  50.3 0.0 collective-permute-start.7
  50.3 3.6 %fetch.6 = (bf16[2,512,1024]{2,1,0:T(8,128)(2,1)S(1)}, bf16[2,512,1024]{2,1,0:T(8,128)(2,1)}) custom-call(bf16[16,512,1024]{2,1,0:T(8,128)(2,1)} %merge_blocks.1.tile_ref, bf16[256,256]{1,0:T(8,128)(2,1)S(1)} %get-tuple-element.21.refs_0_.a_ref), custom_call_target="tpu_custom_call" | custom-call | bytes 4325376 | tf_op jit(solution)/shard_map/step1/fetch/pallas_call | solution.py:36
  53.9 0.0 collective-permute-done.8.refs_3_
  53.9 2.8 %collective-permute-done.7.refs_2_ = bf16[256,256]{1,0:T(8,128)(2,1)S(1)} collective-permute-done((bf16[256,256]{1,0:T(8,128)(2,1)S(1)}, bf16[256,256]{1,0:T(8,128)(2,1)S(1)}, u32[]{:S(2)}, u32[]{:S(2)}) %collective-permute-start.7) | collective-permute-done | bytes 131104 | tf_op jit(solution)/shard_map/step1/ppermute | solution.py:289
  56.7 0.8 step_send.1
  57.5 2.7 %collective-permute-start.10 = (bf16[1024,256]{1,0:T(8,128)(2,1)S(1)}, bf16[1024,256]{1,0:T(8,128)(2,1)S(1)}, u32[]{:S(2)}, u32[]{:S(2)}) collective-permute-start(bf16[1024,256]{1,0:T(8,128)(2,1)S(1)} %step_send.1), channel_id=1, source_target_pairs={{0,1},{1,0},{2,3},{3,2},{4,5},{5,4},{6,7},{7,6},{8,9},{9,8},{10,11... | collective-permute-start | bytes 1572872 | tf_op jit(solution)/shard_map/step2/ppermute | solution.py:283
  60.2 0.8 step_keep.1.a_ref
  61.0 0.7 collective-permute-done.10.b_ref
  61.8 0.1 add.4
  61.9 1.3 %collective-permute-start.11 = (bf16[256,256]{1,0:T(8,128)(2,1)S(1)}, bf16[256,256]{1,0:T(8,128)(2,1)S(1)}, u32[]{:S(2)}, u32[]{:S(2)}) collective-permute-start(bf16[256,256]{1,0:T(8,128)(2,1)S(1)} %get-tuple-element.31), channel_id=1, source_target_pairs={{0,8},{1,9},{2,10},{3,11},{4,12},{5,13},{6,14},{7,15},{8,0},{9,1},... | collective-permute-start | bytes 393224 | tf_op jit(solution)/shard_map/step2/ppermute | solution.py:286
  63.2 2.7 %collective-permute-start.13 = (bf16[256,256]{1,0:T(8,128)(2,1)S(1)}, bf16[256,256]{1,0:T(8,128)(2,1)S(1)}, u32[]{:S(2)}, u32[]{:S(2)}) collective-permute-start(bf16[256,256]{1,0:T(8,128)(2,1)S(1)} %get-tuple-element.33), channel_id=1, source_target_pairs={{0,12},{1,13},{2,14},{3,15},{4,0},{5,1},{6,2},{7,3},{8,4},{9,5},{1... | collective-permute-start | bytes 393224 | tf_op jit(solution)/shard_map/step2/ppermute | solution.py:286
  65.8 2.4 %collective-permute-done.11.b_ref = bf16[256,256]{1,0:T(8,128)(2,1)S(1)} collective-permute-done((bf16[256,256]{1,0:T(8,128)(2,1)S(1)}, bf16[256,256]{1,0:T(8,128)(2,1)S(1)}, u32[]{:S(2)}, u32[]{:S(2)}) %collective-permute-start.11) | collective-permute-done | bytes 131104 | tf_op jit(solution)/shard_map/step2/ppermute | solution.py:286
  68.2 3.5 %collective-permute-done.12.c_ref = bf16[256,256]{1,0:T(8,128)(2,1)S(1)} collective-permute-done((bf16[256,256]{1,0:T(8,128)(2,1)S(1)}, bf16[256,256]{1,0:T(8,128)(2,1)S(1)}, u32[]{:S(2)}, u32[]{:S(2)}) %collective-permute-start.12) | collective-permute-done | bytes 131104 | tf_op jit(solution)/shard_map/step2/ppermute | solution.py:286
  71.7 0.1 sum_x.3
  71.8 0.4 collective-permute-start.16
  72.1 2.4 %collective-permute-start.15 = (bf16[128,256]{1,0:T(8,128)(2,1)S(1)}, bf16[128,256]{1,0:T(8,128)(2,1)S(1)}, u32[]{:S(2)}, u32[]{:S(2)}) collective-permute-start(bf16[128,256]{1,0:T(8,128)(2,1)S(1)} %get-tuple-element.35), channel_id=1, source_target_pairs={{0,18},{1,19},{2,16},{3,17},{4,22},{5,23},{6,20},{7,21},{8,26},{9,... | collective-permute-start | bytes 196616 | tf_op jit(solution)/shard_map/step2/ppermute | solution.py:303
  74.5 0.7 collective-permute-start.14
  75.2 1.3 %collective-permute-done.15.far_ref = bf16[128,256]{1,0:T(8,128)(2,1)S(1)} collective-permute-done((bf16[128,256]{1,0:T(8,128)(2,1)S(1)}, bf16[128,256]{1,0:T(8,128)(2,1)S(1)}, u32[]{:S(2)}, u32[]{:S(2)}) %collective-permute-start.15) | collective-permute-done | bytes 65568 | tf_op jit(solution)/shard_map/step2/ppermute | solution.py:303
  76.5 2.6 %collective-permute-done.14.arrived_ref = bf16[128,256]{1,0:T(8,128)(2,1)S(1)} collective-permute-done((bf16[128,256]{1,0:T(8,128)(2,1)S(1)}, bf16[128,256]{1,0:T(8,128)(2,1)S(1)}, u32[]{:S(2)}, u32[]{:S(2)}) %collective-permute-start.14) | collective-permute-done | bytes 65568 | tf_op jit(solution)/shard_map/step2/ppermute | solution.py:295
  79.1 0.1 next.3.refs_0_
  79.2 0.1 collective-permute-start.19
  79.3 0.9 collective-permute-start.18
  80.2 0.6 collective-permute-start.17
  80.8 3.6 %fetch.7 = (bf16[2,512,1024]{2,1,0:T(8,128)(2,1)S(1)}, bf16[2,512,1024]{2,1,0:T(8,128)(2,1)}) custom-call(bf16[16,512,1024]{2,1,0:T(8,128)(2,1)} %merge_blocks.1.tile_ref, bf16[256,256]{1,0:T(8,128)(2,1)S(1)} %get-tuple-element.29.refs_0_.a_ref), custom_call_target="tpu_custom_call" | custom-call | bytes 4325376 | tf_op jit(solution)/shard_map/step2/fetch/pallas_call | solution.py:36
  84.4 0.2 collective-permute-done.19.refs_3_
  84.7 1.7 %collective-permute-done.17.refs_1_ = bf16[256,256]{1,0:T(8,128)(2,1)S(1)} collective-permute-done((bf16[256,256]{1,0:T(8,128)(2,1)S(1)}, bf16[256,256]{1,0:T(8,128)(2,1)S(1)}, u32[]{:S(2)}, u32[]{:S(2)}) %collective-permute-start.17) | collective-permute-done | bytes 131104 | tf_op jit(solution)/shard_map/step2/ppermute | solution.py:289
  86.4 0.8 last_send.1
  87.2 3.2 %collective-permute-start.20 = (bf16[1024,256]{1,0:T(8,128)(2,1)S(1)}, bf16[1024,256]{1,0:T(8,128)(2,1)S(1)}, u32[]{:S(2)}, u32[]{:S(2)}) collective-permute-start(bf16[1024,256]{1,0:T(8,128)(2,1)S(1)} %last_send.1), channel_id=1, source_target_pairs={{0,1},{1,0},{2,3},{3,2},{4,5},{5,4},{6,7},{7,6},{8,9},{9,8},{10,11... | collective-permute-start | bytes 1572872 | tf_op jit(solution)/shard_map/step3/ppermute | solution.py:283
  90.4 0.8 last_keep.1.a_ref
  91.2 0.8 collective-permute-done.20.b_ref
  91.9 0.1 add.5
  92.1 12.7 %all_to_all.15 = bf16[8,128,256]{2,1,0:T(8,128)(2,1)S(1)} all-to-all(bf16[8,128,256]{2,1,0:T(8,128)(2,1)S(1)} %bitcast.12), channel_id=1, replica_groups={{0,2,4,6,8,10,12,14},{1,3,5,7,9,11,13,15},{16,18,20,22,24,26,28,30},{17..., dimensions={0} | all-to-all | bytes 1048576 | tf_op jit(solution)/shard_map/step3/all_to_all | solution.py:278
  104.7 0.1 convert_reduce_fusion
  104.8 0.0 copy-start.2
  104.8 0.2 fusion
  105.0 0.1 reshape.19
  105.1 15.4 %all_to_all.16 = bf16[128,2,256]{2,1,0:T(2,128)(2,1)S(1)} all-to-all(bf16[128,2,256]{2,1,0:T(2,128)(2,1)S(1)} %reshape.19), channel_id=1, replica_groups=mesh['row'=8,'col'=16] {'row','col'}, dimensions={0} | all-to-all | bytes 262144 | tf_op jit(solution)/shard_map/gram/all_to_all | solution.py:278
  120.5 0.7 convert_reduce_fusion.1
  (12 shorter events, 0.1 us)
Async XLA Ops:
  2.4 25.0 %all-to-all-start = ((bf16[128,8,256]{2,1,0:T(8,128)(2,1)}), bf16[128,8,256]{2,1,0:T(8,128)(2,1)S(1)}, u32[]{:S(2)}, u32[]{:S(2)}) async-start(bf16[128,8,256]{2,1,0:T(8,128)(2,1)} %bitcast.14), calls=%async_computation | async-start | bytes 1048576 | tf_op jit(solution)/shard_map/deal/all_to_all | solution.py:278
  28.2 3.7 %collective-permute-start = (bf16[1024,256]{1,0:T(8,128)(2,1)S(1)}, bf16[1024,256]{1,0:T(8,128)(2,1)S(1)}, u32[]{:S(2)}, u32[]{:S(2)}) collective-permute-start(bf16[1024,256]{1,0:T(8,128)(2,1)S(1)} %get-tuple-element.20), channel_id=1, source_target_pairs={{0,1},{1,0},{2,3},{3,2},{4,5},{5,4},{6,7},{7,6},{8,9},{9,8},{10,11... | collective-permute-start | bytes 1572872 | tf_op jit(solution)/shard_map/step1/ppermute | solution.py:283
  32.0 6.7 %collective-permute-start.1 = (bf16[256,256]{1,0:T(8,128)(2,1)S(1)}, bf16[256,256]{1,0:T(8,128)(2,1)S(1)}, u32[]{:S(2)}, u32[]{:S(2)}) collective-permute-start(bf16[256,256]{1,0:T(8,128)(2,1)S(1)} %get-tuple-element.23), channel_id=1, source_target_pairs={{0,8},{1,9},{2,10},{3,11},{4,12},{5,13},{6,14},{7,15},{8,0},{9,1},... | collective-permute-start | bytes 393224 | tf_op jit(solution)/shard_map/step1/ppermute | solution.py:286
  33.2 8.7 %collective-permute-start.2 = (bf16[256,256]{1,0:T(8,128)(2,1)S(1)}, bf16[256,256]{1,0:T(8,128)(2,1)S(1)}, u32[]{:S(2)}, u32[]{:S(2)}) collective-permute-start(bf16[256,256]{1,0:T(8,128)(2,1)S(1)} %get-tuple-element.24), channel_id=1, source_target_pairs={{0,4},{1,5},{2,6},{3,7},{4,8},{5,9},{6,10},{7,11},{8,12},{9,13},{1... | collective-permute-start | bytes 393224 | tf_op jit(solution)/shard_map/step1/ppermute | solution.py:286
  33.5 8.3 %collective-permute-start.3 = (bf16[256,256]{1,0:T(8,128)(2,1)S(1)}, bf16[256,256]{1,0:T(8,128)(2,1)S(1)}, u32[]{:S(2)}, u32[]{:S(2)}) collective-permute-start(bf16[256,256]{1,0:T(8,128)(2,1)S(1)} %get-tuple-element.25), channel_id=1, source_target_pairs={{0,12},{1,13},{2,14},{3,15},{4,0},{5,1},{6,2},{7,3},{8,4},{9,5},{1... | collective-permute-start | bytes 393224 | tf_op jit(solution)/shard_map/step1/ppermute | solution.py:286
  42.0 3.3 %collective-permute-start.6 = (bf16[128,256]{1,0:T(8,128)(2,1)S(1)}, bf16[128,256]{1,0:T(8,128)(2,1)S(1)}, u32[]{:S(2)}, u32[]{:S(2)}) collective-permute-start(bf16[128,256]{1,0:T(8,128)(2,1)S(1)} %get-tuple-element.26.own_ref), channel_id=1, source_target_pairs={{0,16},{16,0},{32,48},{48,32},{64,80},{80,64},{96,112},{112,96},{1... | collective-permute-start | bytes 196616 | tf_op jit(solution)/shard_map/step1/ppermute | solution.py:292
  42.2 4.3 %collective-permute-start.5 = (bf16[128,256]{1,0:T(8,128)(2,1)S(1)}, bf16[128,256]{1,0:T(8,128)(2,1)S(1)}, u32[]{:S(2)}, u32[]{:S(2)}) collective-permute-start(bf16[128,256]{1,0:T(8,128)(2,1)S(1)} %get-tuple-element.27), channel_id=1, source_target_pairs={{0,18},{1,19},{2,16},{3,17},{4,22},{5,23},{6,20},{7,21},{8,26},{9,... | collective-permute-start | bytes 196616 | tf_op jit(solution)/shard_map/step1/ppermute | solution.py:303
  43.1 4.7 %collective-permute-start.4 = (bf16[128,256]{1,0:T(8,128)(2,1)S(1)}, bf16[128,256]{1,0:T(8,128)(2,1)S(1)}, u32[]{:S(2)}, u32[]{:S(2)}) collective-permute-start(bf16[128,256]{1,0:T(8,128)(2,1)S(1)} %get-tuple-element.27), channel_id=1, source_target_pairs={{0,2},{1,3},{2,0},{3,1},{4,6},{5,7},{6,4},{7,5},{8,10},{9,11},{10,... | collective-permute-start | bytes 196616 | tf_op jit(solution)/shard_map/step1/ppermute | solution.py:295
  47.8 6.1 %collective-permute-start.9 = (bf16[256,256]{1,0:T(8,128)(2,1)S(1)}, bf16[256,256]{1,0:T(8,128)(2,1)S(1)}, u32[]{:S(2)}, u32[]{:S(2)}) collective-permute-start(bf16[256,256]{1,0:T(8,128)(2,1)S(1)} %next.2.refs_1_.refs_4_), channel_id=1, source_target_pairs={{0,64},{16,80},{32,96},{48,112},{64,0},{80,16},{96,32},{112,48},{1... | collective-permute-start | bytes 393224 | tf_op jit(solution)/shard_map/step1/ppermute | solution.py:289
  48.3 5.6 %collective-permute-start.8 = (bf16[256,256]{1,0:T(8,128)(2,1)S(1)}, bf16[256,256]{1,0:T(8,128)(2,1)S(1)}, u32[]{:S(2)}, u32[]{:S(2)}) collective-permute-start(bf16[256,256]{1,0:T(8,128)(2,1)S(1)} %next.2.refs_1_.refs_4_), channel_id=1, source_target_pairs={{0,96},{16,112},{32,0},{48,16},{64,32},{80,48},{96,64},{112,80},{1... | collective-permute-start | bytes 393224 | tf_op jit(solution)/shard_map/step1/ppermute | solution.py:289
  50.3 6.4 %collective-permute-start.7 = (bf16[256,256]{1,0:T(8,128)(2,1)S(1)}, bf16[256,256]{1,0:T(8,128)(2,1)S(1)}, u32[]{:S(2)}, u32[]{:S(2)}) collective-permute-start(bf16[256,256]{1,0:T(8,128)(2,1)S(1)} %next.2.refs_1_.refs_4_), channel_id=1, source_target_pairs={{0,32},{16,48},{32,64},{48,80},{64,96},{80,112},{96,0},{112,16},{1... | collective-permute-start | bytes 393224 | tf_op jit(solution)/shard_map/step1/ppermute | solution.py:289
  53.9 6.3 %copy-start = (bf16[2,512,1024]{2,1,0:T(8,128)(2,1)S(1)}, bf16[2,512,1024]{2,1,0:T(8,128)(2,1)}, u32[]{:S(2)}) copy-start(bf16[2,512,1024]{2,1,0:T(8,128)(2,1)} %get-tuple-element.22.refs_0_) | copy-start | bytes 6291460
  57.5 4.2 %collective-permute-start.10 = (bf16[1024,256]{1,0:T(8,128)(2,1)S(1)}, bf16[1024,256]{1,0:T(8,128)(2,1)S(1)}, u32[]{:S(2)}, u32[]{:S(2)}) collective-permute-start(bf16[1024,256]{1,0:T(8,128)(2,1)S(1)} %step_send.1), channel_id=1, source_target_pairs={{0,1},{1,0},{2,3},{3,2},{4,5},{5,4},{6,7},{7,6},{8,9},{9,8},{10,11... | collective-permute-start | bytes 1572872 | tf_op jit(solution)/shard_map/step2/ppermute | solution.py:283
  61.9 6.3 %collective-permute-start.11 = (bf16[256,256]{1,0:T(8,128)(2,1)S(1)}, bf16[256,256]{1,0:T(8,128)(2,1)S(1)}, u32[]{:S(2)}, u32[]{:S(2)}) collective-permute-start(bf16[256,256]{1,0:T(8,128)(2,1)S(1)} %get-tuple-element.31), channel_id=1, source_target_pairs={{0,8},{1,9},{2,10},{3,11},{4,12},{5,13},{6,14},{7,15},{8,0},{9,1},... | collective-permute-start | bytes 393224 | tf_op jit(solution)/shard_map/step2/ppermute | solution.py:286
  63.1 8.6 %collective-permute-start.12 = (bf16[256,256]{1,0:T(8,128)(2,1)S(1)}, bf16[256,256]{1,0:T(8,128)(2,1)S(1)}, u32[]{:S(2)}, u32[]{:S(2)}) collective-permute-start(bf16[256,256]{1,0:T(8,128)(2,1)S(1)} %get-tuple-element.32), channel_id=1, source_target_pairs={{0,4},{1,5},{2,6},{3,7},{4,8},{5,9},{6,10},{7,11},{8,12},{9,13},{1... | collective-permute-start | bytes 393224 | tf_op jit(solution)/shard_map/step2/ppermute | solution.py:286
  63.2 8.6 %collective-permute-start.13 = (bf16[256,256]{1,0:T(8,128)(2,1)S(1)}, bf16[256,256]{1,0:T(8,128)(2,1)S(1)}, u32[]{:S(2)}, u32[]{:S(2)}) collective-permute-start(bf16[256,256]{1,0:T(8,128)(2,1)S(1)} %get-tuple-element.33), channel_id=1, source_target_pairs={{0,12},{1,13},{2,14},{3,15},{4,0},{5,1},{6,2},{7,3},{8,4},{9,5},{1... | collective-permute-start | bytes 393224 | tf_op jit(solution)/shard_map/step2/ppermute | solution.py:286
  71.8 3.4 %collective-permute-start.16 = (bf16[128,256]{1,0:T(8,128)(2,1)S(1)}, bf16[128,256]{1,0:T(8,128)(2,1)S(1)}, u32[]{:S(2)}, u32[]{:S(2)}) collective-permute-start(bf16[128,256]{1,0:T(8,128)(2,1)S(1)} %get-tuple-element.34.own_ref), channel_id=1, source_target_pairs={{0,16},{16,0},{32,48},{48,32},{64,80},{80,64},{96,112},{112,96},{1... | collective-permute-start | bytes 196616 | tf_op jit(solution)/shard_map/step2/ppermute | solution.py:292
  72.1 4.3 %collective-permute-start.15 = (bf16[128,256]{1,0:T(8,128)(2,1)S(1)}, bf16[128,256]{1,0:T(8,128)(2,1)S(1)}, u32[]{:S(2)}, u32[]{:S(2)}) collective-permute-start(bf16[128,256]{1,0:T(8,128)(2,1)S(1)} %get-tuple-element.35), channel_id=1, source_target_pairs={{0,18},{1,19},{2,16},{3,17},{4,22},{5,23},{6,20},{7,21},{8,26},{9,... | collective-permute-start | bytes 196616 | tf_op jit(solution)/shard_map/step2/ppermute | solution.py:303
  74.5 4.6 %collective-permute-start.14 = (bf16[128,256]{1,0:T(8,128)(2,1)S(1)}, bf16[128,256]{1,0:T(8,128)(2,1)S(1)}, u32[]{:S(2)}, u32[]{:S(2)}) collective-permute-start(bf16[128,256]{1,0:T(8,128)(2,1)S(1)} %get-tuple-element.35), channel_id=1, source_target_pairs={{0,2},{1,3},{2,0},{3,1},{4,6},{5,7},{6,4},{7,5},{8,10},{9,11},{10,... | collective-permute-start | bytes 196616 | tf_op jit(solution)/shard_map/step2/ppermute | solution.py:295
  79.2 5.5 %collective-permute-start.19 = (bf16[256,256]{1,0:T(8,128)(2,1)S(1)}, bf16[256,256]{1,0:T(8,128)(2,1)S(1)}, u32[]{:S(2)}, u32[]{:S(2)}) collective-permute-start(bf16[256,256]{1,0:T(8,128)(2,1)S(1)} %next.3.refs_0_), channel_id=1, source_target_pairs={{0,64},{16,80},{32,96},{48,112},{64,0},{80,16},{96,32},{112,48},{1... | collective-permute-start | bytes 393224 | tf_op jit(solution)/shard_map/step2/ppermute | solution.py:289
  79.3 5.4 %collective-permute-start.18 = (bf16[256,256]{1,0:T(8,128)(2,1)S(1)}, bf16[256,256]{1,0:T(8,128)(2,1)S(1)}, u32[]{:S(2)}, u32[]{:S(2)}) collective-permute-start(bf16[256,256]{1,0:T(8,128)(2,1)S(1)} %next.3.refs_0_), channel_id=1, source_target_pairs={{0,96},{16,112},{32,0},{48,16},{64,32},{80,48},{96,64},{112,80},{1... | collective-permute-start | bytes 393224 | tf_op jit(solution)/shard_map/step2/ppermute | solution.py:289
  80.2 6.2 %collective-permute-start.17 = (bf16[256,256]{1,0:T(8,128)(2,1)S(1)}, bf16[256,256]{1,0:T(8,128)(2,1)S(1)}, u32[]{:S(2)}, u32[]{:S(2)}) collective-permute-start(bf16[256,256]{1,0:T(8,128)(2,1)S(1)} %next.3.refs_0_), channel_id=1, source_target_pairs={{0,32},{16,48},{32,64},{48,80},{64,96},{80,112},{96,0},{112,16},{1... | collective-permute-start | bytes 393224 | tf_op jit(solution)/shard_map/step2/ppermute | solution.py:289
  84.4 6.0 %copy-start.1 = (bf16[2,512,1024]{2,1,0:T(8,128)(2,1)S(1)}, bf16[2,512,1024]{2,1,0:T(8,128)(2,1)}, u32[]{:S(2)}) copy-start(bf16[2,512,1024]{2,1,0:T(8,128)(2,1)} %get-tuple-element.30.tile_ref) | copy-start | bytes 6291460
  87.2 4.8 %collective-permute-start.20 = (bf16[1024,256]{1,0:T(8,128)(2,1)S(1)}, bf16[1024,256]{1,0:T(8,128)(2,1)S(1)}, u32[]{:S(2)}, u32[]{:S(2)}) collective-permute-start(bf16[1024,256]{1,0:T(8,128)(2,1)S(1)} %last_send.1), channel_id=1, source_target_pairs={{0,1},{1,0},{2,3},{3,2},{4,5},{5,4},{6,7},{7,6},{8,9},{9,8},{10,11... | collective-permute-start | bytes 1572872 | tf_op jit(solution)/shard_map/step3/ppermute | solution.py:283
  104.8 16.4 %copy-start.2 = (bf16[128,256]{1,0:T(8,128)(2,1)}, bf16[128,256]{1,0:T(8,128)(2,1)S(1)}, u32[]{:S(2)}) copy-start(bf16[128,256]{1,0:T(8,128)(2,1)S(1)} %multiply_convert_fusion) | copy-start | bytes 196612

commit v5 on v4

--- a/solution.py
+++ b/solution.py
@@ -18,7 +18,7 @@
 CHUNK = 16
 UNROLL = 16
 PANEL_ORDER = (0, 2, 3, 1)
-PIECES = 4
+PIECES = 2
 MERGE_VMEM = 60 * 1024 * 1024
 SMALL_VMEM = 8 * 1024 * 1024
 PRODUCT_VMEM = 50 * 1024 * 1024
@@ -213,9 +213,10 @@
     else:
         out_ref = refs[4]
         put_together([refs[k] for k in PANEL_ORDER], panel)
+    both = dot(tile_ref[...].reshape(2 * QUARTER, panel.shape[0]), panel[...])
+    both = both.reshape(2, HALF, HALF, RUN, panel.shape[1])
     for i in range(2):
-        terms = dot(tile_ref[i], panel[...])
-        terms = terms.reshape(HALF, HALF, RUN, terms.shape[1])
+        terms = both[i]
         for t in range(HALF):
             away = ((t // 2 - col_id // 4) & 3) * 2 + ((t ^ (col_id // 2)) & 1)
             total[away, :, core if i else 1 - core] = terms[t]
@@ -227,9 +228,10 @@
     put_together([parts[k] for k in PANEL_ORDER], panel)
     col_id = lax.axis_index("col")
     core = col_id & 1
+    both = dot(tile_ref[...].reshape(2 * QUARTER, panel.shape[0]), panel[...])
+    both = both.reshape(2, HALF, HALF, RUN, panel.shape[1])
     for j in range(2):
-        terms = dot(tile_ref[j], panel[...])
-        terms = terms.reshape(HALF, HALF, RUN, terms.shape[1])
+        terms = both[j]
         for t in range(HALF):
             total[:, t, core if j else 1 - core] = terms[t]
     first = first_ref[:BLOCK, :].astype(F32).reshape(HALF, 2, RUN, first_ref.shape[1])

time: 122 us -> 121 us (level)
  transfers between devices with their start and end apart: 22 -> 22, of which waited for: 14 -> 14; matrix products, arithmetic and copies ran while one was open for 0% -> 0% of each run, Pallas kernels for 16% -> 15%
where the time goes in v5:
time: 121 us
  starting transfers between devices  37.2 us (31%)
  waiting for transfers between devices  30.2 us (25%)
  blocking collectives  28.1 us (23%)
  Pallas kernels  23 us (19%)
  between operations  1.5 us (1%)
    all_to_all x2, blocking collectives, exchange(): lax.all_to_all(parts, axes, split_axis=0, concat_axis=0, tiled=True, axis...  28.1 us
    pallas_call x17, Pallas kernels, small_call(): pl.pallas_call(kernel, out_shape=outs, in_specs=[HBM] * len(tiles) + [VME...  15.4 us
    ppermute x6, waiting for transfers between devices, along_x(): lax.ppermute(x, 'col', [(i, (i + 4 * k) % col_count) for i in range(col_c...  11.9 us
    all_to_all x1, starting transfers between devices, exchange(): lax.all_to_all(parts, axes, split_axis=0, concat_axis=0, tiled=True, axis...  11.5 us
    ppermute x6, starting transfers between devices, along_x(): lax.ppermute(x, 'col', [(i, (i + 4 * k) % col_count) for i in range(col_c...  7.76 us
    ppermute x3, starting transfers between devices, other_core(): return lax.ppermute(x, 'col', [(i, i ^ 1) for i in range(col_count)])  7.12 us
    pallas_call x1, Pallas kernels, merge(): pl.pallas_call(merge_kernel, out_shape=jax.ShapeDtypeStruct((ROOM,) + qua...  5.81 us
    all_to_all x1, waiting for transfers between devices, exchange(): lax.all_to_all(parts, axes, split_axis=0, concat_axis=0, tiled=True, axis...  5.47 us
  transfers between devices with their start and end apart: 22, of which 14 were waited for; matrix products, arithmetic and copies ran while one was open for 0% of the time, Pallas kernels for 15%

profile of v5, /device:TPU:1, one launch (start us, length us, event | category | flops | bytes accessed | tf_op | source)
XLA Modules:
  0.0 121.1 jit_solution(13912652502495215893)
XLA Ops:
  0.6 1.7 %copies.1 = bf16[8,128,256]{2,1,0:T(8,128)(2,1)} custom-call(bf16[128,256]{1,0:T(8,128)(2,1)} %own_ref.1), custom_call_target="tpu_custom_call" | custom-call | tf_op jit(solution)/shard_map/deal/copies/pallas_call | solution.py:157
  2.4 11.5 %all-to-all-start = ((bf16[128,8,256]{2,1,0:T(8,128)(2,1)}), bf16[128,8,256]{2,1,0:T(8,128)(2,1)S(1)}, u32[]{:S(2)}, u32[]{:S(2)}) async-start(bf16[128,8,256]{2,1,0:T(8,128)(2,1)} %bitcast.14), calls=%async_computation | async-start | bytes 1048576 | tf_op jit(solution)/shard_map/deal/all_to_all | solution.py:280
  14.5 5.8 %merge_blocks.1.tile_ref = bf16[16,512,1024]{2,1,0:T(8,128)(2,1)} custom-call(s32[256]{0:T(256)} %bitcast.15, s32[256]{0:T(256)} %bitcast.16, s32[1]{0:T(128)} %bitcast.9.stored_ref, bf16[256,128,128]{2,1,0:T(8,128)(2,1)} %bitcast.13), custom_call_target="tpu_custom_call" | custom-call | flops 4194304 | bytes 12582912 | tf_op jit(solution)/shard_map/merge/merge_blocks/pallas_call | solution.py:117
  20.3 1.6 %fetch.5.refs_0_ = bf16[2,512,1024]{2,1,0:T(8,128)(2,1)S(1)} custom-call(bf16[16,512,1024]{2,1,0:T(8,128)(2,1)} %merge_blocks.1.tile_ref), custom_call_target="tpu_custom_call" | custom-call | bytes 2097152 | tf_op jit(solution)/shard_map/step1/fetch/pallas_call | solution.py:36
  21.9 5.5 %all-to-all-done = bf16[128,8,256]{2,1,0:T(8,128)(2,1)S(1)} async-done(((bf16[128,8,256]{2,1,0:T(8,128)(2,1)}), bf16[128,8,256]{2,1,0:T(8,128)(2,1)S(1)}, u32[]{:S(2)}, u32[]{:S(2)}) %all-to-all-start) | async-done | bytes 524320 | tf_op jit(solution)/shard_map/deal/all_to_all | solution.py:280
  27.4 0.8 first_send.1
  28.2 1.2 %collective-permute-start = (bf16[1024,256]{1,0:T(8,128)(2,1)S(1)}, bf16[1024,256]{1,0:T(8,128)(2,1)S(1)}, u32[]{:S(2)}, u32[]{:S(2)}) collective-permute-start(bf16[1024,256]{1,0:T(8,128)(2,1)S(1)} %get-tuple-element.20), channel_id=1, source_target_pairs={{0,1},{1,0},{2,3},{3,2},{4,5},{5,4},{6,7},{7,6},{8,9},{9,8},{10,11... | collective-permute-start | bytes 1572872 | tf_op jit(solution)/shard_map/step1/ppermute | solution.py:285
  29.4 1.6 %fetch.4.refs_0_ = bf16[2,512,1024]{2,1,0:T(8,128)(2,1)S(1)} custom-call(bf16[16,512,1024]{2,1,0:T(8,128)(2,1)} %merge_blocks.1.tile_ref), custom_call_target="tpu_custom_call" | custom-call | bytes 2097152 | tf_op jit(solution)/shard_map/step1/fetch/pallas_call | solution.py:36
  31.0 0.8 first_keep.1.a_ref
  31.8 0.0 collective-permute-done.b_ref
  31.8 0.1 add.3
  31.9 1.1 collective-permute-start.1
  33.1 0.4 collective-permute-start.2
  33.4 2.3 %collective-permute-start.3 = (bf16[256,256]{1,0:T(8,128)(2,1)S(1)}, bf16[256,256]{1,0:T(8,128)(2,1)S(1)}, u32[]{:S(2)}, u32[]{:S(2)}) collective-permute-start(bf16[256,256]{1,0:T(8,128)(2,1)S(1)} %get-tuple-element.25), channel_id=1, source_target_pairs={{0,12},{1,13},{2,14},{3,15},{4,0},{5,1},{6,2},{7,3},{8,4},{9,5},{1... | collective-permute-start | bytes 393224 | tf_op jit(solution)/shard_map/step1/ppermute | solution.py:288
  35.7 2.9 %collective-permute-done.1.b_ref = bf16[256,256]{1,0:T(8,128)(2,1)S(1)} collective-permute-done((bf16[256,256]{1,0:T(8,128)(2,1)S(1)}, bf16[256,256]{1,0:T(8,128)(2,1)S(1)}, u32[]{:S(2)}, u32[]{:S(2)}) %collective-permute-start.1) | collective-permute-done | bytes 131104 | tf_op jit(solution)/shard_map/step1/ppermute | solution.py:288
  38.6 3.1 %collective-permute-done.2.c_ref = bf16[256,256]{1,0:T(8,128)(2,1)S(1)} collective-permute-done((bf16[256,256]{1,0:T(8,128)(2,1)S(1)}, bf16[256,256]{1,0:T(8,128)(2,1)S(1)}, u32[]{:S(2)}, u32[]{:S(2)}) %collective-permute-start.2) | collective-permute-done | bytes 131104 | tf_op jit(solution)/shard_map/step1/ppermute | solution.py:288
  41.8 0.0 collective-permute-done.3.d_ref
  41.8 0.1 sum_x.2
  41.8 0.2 collective-permute-start.6
  42.1 0.9 collective-permute-start.5
  43.0 2.2 %collective-permute-start.4 = (bf16[128,256]{1,0:T(8,128)(2,1)S(1)}, bf16[128,256]{1,0:T(8,128)(2,1)S(1)}, u32[]{:S(2)}, u32[]{:S(2)}) collective-permute-start(bf16[128,256]{1,0:T(8,128)(2,1)S(1)} %get-tuple-element.27), channel_id=1, source_target_pairs={{0,2},{1,3},{2,0},{3,1},{4,6},{5,7},{6,4},{7,5},{8,10},{9,11},{10,... | collective-permute-start | bytes 196616 | tf_op jit(solution)/shard_map/step1/ppermute | solution.py:297
  45.2 0.0 collective-permute-done.6.near_ref
  45.2 1.2 %collective-permute-done.5.far_ref = bf16[128,256]{1,0:T(8,128)(2,1)S(1)} collective-permute-done((bf16[128,256]{1,0:T(8,128)(2,1)S(1)}, bf16[128,256]{1,0:T(8,128)(2,1)S(1)}, u32[]{:S(2)}, u32[]{:S(2)}) %collective-permute-start.5) | collective-permute-done | bytes 65568 | tf_op jit(solution)/shard_map/step1/ppermute | solution.py:305
  46.4 1.2 %collective-permute-done.4.arrived_ref = bf16[128,256]{1,0:T(8,128)(2,1)S(1)} collective-permute-done((bf16[128,256]{1,0:T(8,128)(2,1)S(1)}, bf16[128,256]{1,0:T(8,128)(2,1)S(1)}, u32[]{:S(2)}, u32[]{:S(2)}) %collective-permute-start.4) | collective-permute-done | bytes 65568 | tf_op jit(solution)/shard_map/step1/ppermute | solution.py:297
  47.7 0.6 collective-permute-start.9
  48.2 2.0 %collective-permute-start.8 = (bf16[256,256]{1,0:T(8,128)(2,1)S(1)}, bf16[256,256]{1,0:T(8,128)(2,1)S(1)}, u32[]{:S(2)}, u32[]{:S(2)}) collective-permute-start(bf16[256,256]{1,0:T(8,128)(2,1)S(1)} %next.2.refs_1_.refs_4_), channel_id=1, source_target_pairs={{0,96},{16,112},{32,0},{48,16},{64,32},{80,48},{96,64},{112,80},{1... | collective-permute-start | bytes 393224 | tf_op jit(solution)/shard_map/step1/ppermute | solution.py:291
  50.2 0.0 collective-permute-start.7
  50.2 3.5 %fetch.6 = (bf16[2,512,1024]{2,1,0:T(8,128)(2,1)S(1)}, bf16[2,512,1024]{2,1,0:T(8,128)(2,1)}) custom-call(bf16[16,512,1024]{2,1,0:T(8,128)(2,1)} %merge_blocks.1.tile_ref, bf16[256,256]{1,0:T(8,128)(2,1)S(1)} %get-tuple-element.21.refs_0_.a_ref), custom_call_target="tpu_custom_call" | custom-call | bytes 4325376 | tf_op jit(solution)/shard_map/step1/fetch/pallas_call | solution.py:36
  53.8 0.0 collective-permute-done.8.refs_3_
  53.8 2.8 %collective-permute-done.7.refs_2_ = bf16[256,256]{1,0:T(8,128)(2,1)S(1)} collective-permute-done((bf16[256,256]{1,0:T(8,128)(2,1)S(1)}, bf16[256,256]{1,0:T(8,128)(2,1)S(1)}, u32[]{:S(2)}, u32[]{:S(2)}) %collective-permute-start.7) | collective-permute-done | bytes 131104 | tf_op jit(solution)/shard_map/step1/ppermute | solution.py:291
  56.7 0.8 step_send.1
  57.4 2.7 %collective-permute-start.10 = (bf16[1024,256]{1,0:T(8,128)(2,1)S(1)}, bf16[1024,256]{1,0:T(8,128)(2,1)S(1)}, u32[]{:S(2)}, u32[]{:S(2)}) collective-permute-start(bf16[1024,256]{1,0:T(8,128)(2,1)S(1)} %step_send.1), channel_id=1, source_target_pairs={{0,1},{1,0},{2,3},{3,2},{4,5},{5,4},{6,7},{7,6},{8,9},{9,8},{10,11... | collective-permute-start | bytes 1572872 | tf_op jit(solution)/shard_map/step2/ppermute | solution.py:285
  60.1 0.8 step_keep.1.a_ref
  60.9 0.8 collective-permute-done.10.b_ref
  61.6 0.1 add.4
  61.8 1.3 %collective-permute-start.11 = (bf16[256,256]{1,0:T(8,128)(2,1)S(1)}, bf16[256,256]{1,0:T(8,128)(2,1)S(1)}, u32[]{:S(2)}, u32[]{:S(2)}) collective-permute-start(bf16[256,256]{1,0:T(8,128)(2,1)S(1)} %get-tuple-element.31), channel_id=1, source_target_pairs={{0,8},{1,9},{2,10},{3,11},{4,12},{5,13},{6,14},{7,15},{8,0},{9,1},... | collective-permute-start | bytes 393224 | tf_op jit(solution)/shard_map/step2/ppermute | solution.py:288
  63.0 2.7 %collective-permute-start.13 = (bf16[256,256]{1,0:T(8,128)(2,1)S(1)}, bf16[256,256]{1,0:T(8,128)(2,1)S(1)}, u32[]{:S(2)}, u32[]{:S(2)}) collective-permute-start(bf16[256,256]{1,0:T(8,128)(2,1)S(1)} %get-tuple-element.33), channel_id=1, source_target_pairs={{0,12},{1,13},{2,14},{3,15},{4,0},{5,1},{6,2},{7,3},{8,4},{9,5},{1... | collective-permute-start | bytes 393224 | tf_op jit(solution)/shard_map/step2/ppermute | solution.py:288
  65.7 2.3 %collective-permute-done.11.b_ref = bf16[256,256]{1,0:T(8,128)(2,1)S(1)} collective-permute-done((bf16[256,256]{1,0:T(8,128)(2,1)S(1)}, bf16[256,256]{1,0:T(8,128)(2,1)S(1)}, u32[]{:S(2)}, u32[]{:S(2)}) %collective-permute-start.11) | collective-permute-done | bytes 131104 | tf_op jit(solution)/shard_map/step2/ppermute | solution.py:288
  68.0 3.5 %collective-permute-done.12.c_ref = bf16[256,256]{1,0:T(8,128)(2,1)S(1)} collective-permute-done((bf16[256,256]{1,0:T(8,128)(2,1)S(1)}, bf16[256,256]{1,0:T(8,128)(2,1)S(1)}, u32[]{:S(2)}, u32[]{:S(2)}) %collective-permute-start.12) | collective-permute-done | bytes 131104 | tf_op jit(solution)/shard_map/step2/ppermute | solution.py:288
  71.6 0.1 sum_x.3
  71.6 0.3 collective-permute-start.16
  72.0 2.4 %collective-permute-start.15 = (bf16[128,256]{1,0:T(8,128)(2,1)S(1)}, bf16[128,256]{1,0:T(8,128)(2,1)S(1)}, u32[]{:S(2)}, u32[]{:S(2)}) collective-permute-start(bf16[128,256]{1,0:T(8,128)(2,1)S(1)} %get-tuple-element.35), channel_id=1, source_target_pairs={{0,18},{1,19},{2,16},{3,17},{4,22},{5,23},{6,20},{7,21},{8,26},{9,... | collective-permute-start | bytes 196616 | tf_op jit(solution)/shard_map/step2/ppermute | solution.py:305
  74.3 0.7 collective-permute-start.14
  75.0 1.3 %collective-permute-done.15.far_ref = bf16[128,256]{1,0:T(8,128)(2,1)S(1)} collective-permute-done((bf16[128,256]{1,0:T(8,128)(2,1)S(1)}, bf16[128,256]{1,0:T(8,128)(2,1)S(1)}, u32[]{:S(2)}, u32[]{:S(2)}) %collective-permute-start.15) | collective-permute-done | bytes 65568 | tf_op jit(solution)/shard_map/step2/ppermute | solution.py:305
  76.3 2.6 %collective-permute-done.14.arrived_ref = bf16[128,256]{1,0:T(8,128)(2,1)S(1)} collective-permute-done((bf16[128,256]{1,0:T(8,128)(2,1)S(1)}, bf16[128,256]{1,0:T(8,128)(2,1)S(1)}, u32[]{:S(2)}, u32[]{:S(2)}) %collective-permute-start.14) | collective-permute-done | bytes 65568 | tf_op jit(solution)/shard_map/step2/ppermute | solution.py:297
  78.9 0.1 next.3.refs_0_
  79.0 0.1 collective-permute-start.19
  79.1 1.0 collective-permute-start.18
  80.0 0.6 collective-permute-start.17
  80.6 3.5 %fetch.7 = (bf16[2,512,1024]{2,1,0:T(8,128)(2,1)S(1)}, bf16[2,512,1024]{2,1,0:T(8,128)(2,1)}) custom-call(bf16[16,512,1024]{2,1,0:T(8,128)(2,1)} %merge_blocks.1.tile_ref, bf16[256,256]{1,0:T(8,128)(2,1)S(1)} %get-tuple-element.29.refs_0_.a_ref), custom_call_target="tpu_custom_call" | custom-call | bytes 4325376 | tf_op jit(solution)/shard_map/step2/fetch/pallas_call | solution.py:36
  84.2 0.3 collective-permute-done.19.refs_3_
  84.5 1.7 %collective-permute-done.17.refs_1_ = bf16[256,256]{1,0:T(8,128)(2,1)S(1)} collective-permute-done((bf16[256,256]{1,0:T(8,128)(2,1)S(1)}, bf16[256,256]{1,0:T(8,128)(2,1)S(1)}, u32[]{:S(2)}, u32[]{:S(2)}) %collective-permute-start.17) | collective-permute-done | bytes 131104 | tf_op jit(solution)/shard_map/step2/ppermute | solution.py:291
  86.2 0.8 last_send.1
  87.0 3.2 %collective-permute-start.20 = (bf16[1024,256]{1,0:T(8,128)(2,1)S(1)}, bf16[1024,256]{1,0:T(8,128)(2,1)S(1)}, u32[]{:S(2)}, u32[]{:S(2)}) collective-permute-start(bf16[1024,256]{1,0:T(8,128)(2,1)S(1)} %last_send.1), channel_id=1, source_target_pairs={{0,1},{1,0},{2,3},{3,2},{4,5},{5,4},{6,7},{7,6},{8,9},{9,8},{10,11... | collective-permute-start | bytes 1572872 | tf_op jit(solution)/shard_map/step3/ppermute | solution.py:285
  90.2 0.8 last_keep.1.a_ref
  91.0 0.8 collective-permute-done.20.b_ref
  91.8 0.1 add.5
  91.9 12.7 %all_to_all.15 = bf16[8,128,256]{2,1,0:T(8,128)(2,1)S(1)} all-to-all(bf16[8,128,256]{2,1,0:T(8,128)(2,1)S(1)} %bitcast.12), channel_id=1, replica_groups={{0,2,4,6,8,10,12,14},{1,3,5,7,9,11,13,15},{16,18,20,22,24,26,28,30},{17..., dimensions={0} | all-to-all | bytes 1048576 | tf_op jit(solution)/shard_map/step3/all_to_all | solution.py:280
  104.6 0.1 convert_reduce_fusion
  104.7 0.0 copy-start.2
  104.7 0.2 fusion
  104.9 0.1 reshape.19
  105.0 15.4 %all_to_all.16 = bf16[128,2,256]{2,1,0:T(2,128)(2,1)S(1)} all-to-all(bf16[128,2,256]{2,1,0:T(2,128)(2,1)S(1)} %reshape.19), channel_id=1, replica_groups=mesh['row'=8,'col'=16] {'row','col'}, dimensions={0} | all-to-all | bytes 262144 | tf_op jit(solution)/shard_map/gram/all_to_all | solution.py:280
  120.3 0.7 convert_reduce_fusion.1
  (12 shorter events, 0.1 us)
Async XLA Ops:
  2.4 25.0 %all-to-all-start = ((bf16[128,8,256]{2,1,0:T(8,128)(2,1)}), bf16[128,8,256]{2,1,0:T(8,128)(2,1)S(1)}, u32[]{:S(2)}, u32[]{:S(2)}) async-start(bf16[128,8,256]{2,1,0:T(8,128)(2,1)} %bitcast.14), calls=%async_computation | async-start | bytes 1048576 | tf_op jit(solution)/shard_map/deal/all_to_all | solution.py:280
  28.2 3.6 %collective-permute-start = (bf16[1024,256]{1,0:T(8,128)(2,1)S(1)}, bf16[1024,256]{1,0:T(8,128)(2,1)S(1)}, u32[]{:S(2)}, u32[]{:S(2)}) collective-permute-start(bf16[1024,256]{1,0:T(8,128)(2,1)S(1)} %get-tuple-element.20), channel_id=1, source_target_pairs={{0,1},{1,0},{2,3},{3,2},{4,5},{5,4},{6,7},{7,6},{8,9},{9,8},{10,11... | collective-permute-start | bytes 1572872 | tf_op jit(solution)/shard_map/step1/ppermute | solution.py:285
  31.9 6.7 %collective-permute-start.1 = (bf16[256,256]{1,0:T(8,128)(2,1)S(1)}, bf16[256,256]{1,0:T(8,128)(2,1)S(1)}, u32[]{:S(2)}, u32[]{:S(2)}) collective-permute-start(bf16[256,256]{1,0:T(8,128)(2,1)S(1)} %get-tuple-element.23), channel_id=1, source_target_pairs={{0,8},{1,9},{2,10},{3,11},{4,12},{5,13},{6,14},{7,15},{8,0},{9,1},... | collective-permute-start | bytes 393224 | tf_op jit(solution)/shard_map/step1/ppermute | solution.py:288
  33.1 8.7 %collective-permute-start.2 = (bf16[256,256]{1,0:T(8,128)(2,1)S(1)}, bf16[256,256]{1,0:T(8,128)(2,1)S(1)}, u32[]{:S(2)}, u32[]{:S(2)}) collective-permute-start(bf16[256,256]{1,0:T(8,128)(2,1)S(1)} %get-tuple-element.24), channel_id=1, source_target_pairs={{0,4},{1,5},{2,6},{3,7},{4,8},{5,9},{6,10},{7,11},{8,12},{9,13},{1... | collective-permute-start | bytes 393224 | tf_op jit(solution)/shard_map/step1/ppermute | solution.py:288
  33.4 8.3 %collective-permute-start.3 = (bf16[256,256]{1,0:T(8,128)(2,1)S(1)}, bf16[256,256]{1,0:T(8,128)(2,1)S(1)}, u32[]{:S(2)}, u32[]{:S(2)}) collective-permute-start(bf16[256,256]{1,0:T(8,128)(2,1)S(1)} %get-tuple-element.25), channel_id=1, source_target_pairs={{0,12},{1,13},{2,14},{3,15},{4,0},{5,1},{6,2},{7,3},{8,4},{9,5},{1... | collective-permute-start | bytes 393224 | tf_op jit(solution)/shard_map/step1/ppermute | solution.py:288
  41.8 3.3 %collective-permute-start.6 = (bf16[128,256]{1,0:T(8,128)(2,1)S(1)}, bf16[128,256]{1,0:T(8,128)(2,1)S(1)}, u32[]{:S(2)}, u32[]{:S(2)}) collective-permute-start(bf16[128,256]{1,0:T(8,128)(2,1)S(1)} %get-tuple-element.26.own_ref), channel_id=1, source_target_pairs={{0,16},{16,0},{32,48},{48,32},{64,80},{80,64},{96,112},{112,96},{1... | collective-permute-start | bytes 196616 | tf_op jit(solution)/shard_map/step1/ppermute | solution.py:294
  42.1 4.3 %collective-permute-start.5 = (bf16[128,256]{1,0:T(8,128)(2,1)S(1)}, bf16[128,256]{1,0:T(8,128)(2,1)S(1)}, u32[]{:S(2)}, u32[]{:S(2)}) collective-permute-start(bf16[128,256]{1,0:T(8,128)(2,1)S(1)} %get-tuple-element.27), channel_id=1, source_target_pairs={{0,18},{1,19},{2,16},{3,17},{4,22},{5,23},{6,20},{7,21},{8,26},{9,... | collective-permute-start | bytes 196616 | tf_op jit(solution)/shard_map/step1/ppermute | solution.py:305
  43.0 4.7 %collective-permute-start.4 = (bf16[128,256]{1,0:T(8,128)(2,1)S(1)}, bf16[128,256]{1,0:T(8,128)(2,1)S(1)}, u32[]{:S(2)}, u32[]{:S(2)}) collective-permute-start(bf16[128,256]{1,0:T(8,128)(2,1)S(1)} %get-tuple-element.27), channel_id=1, source_target_pairs={{0,2},{1,3},{2,0},{3,1},{4,6},{5,7},{6,4},{7,5},{8,10},{9,11},{10,... | collective-permute-start | bytes 196616 | tf_op jit(solution)/shard_map/step1/ppermute | solution.py:297
  47.7 6.1 %collective-permute-start.9 = (bf16[256,256]{1,0:T(8,128)(2,1)S(1)}, bf16[256,256]{1,0:T(8,128)(2,1)S(1)}, u32[]{:S(2)}, u32[]{:S(2)}) collective-permute-start(bf16[256,256]{1,0:T(8,128)(2,1)S(1)} %next.2.refs_1_.refs_4_), channel_id=1, source_target_pairs={{0,64},{16,80},{32,96},{48,112},{64,0},{80,16},{96,32},{112,48},{1... | collective-permute-start | bytes 393224 | tf_op jit(solution)/shard_map/step1/ppermute | solution.py:291
  48.2 5.6 %collective-permute-start.8 = (bf16[256,256]{1,0:T(8,128)(2,1)S(1)}, bf16[256,256]{1,0:T(8,128)(2,1)S(1)}, u32[]{:S(2)}, u32[]{:S(2)}) collective-permute-start(bf16[256,256]{1,0:T(8,128)(2,1)S(1)} %next.2.refs_1_.refs_4_), channel_id=1, source_target_pairs={{0,96},{16,112},{32,0},{48,16},{64,32},{80,48},{96,64},{112,80},{1... | collective-permute-start | bytes 393224 | tf_op jit(solution)/shard_map/step1/ppermute | solution.py:291
  50.2 6.4 %collective-permute-start.7 = (bf16[256,256]{1,0:T(8,128)(2,1)S(1)}, bf16[256,256]{1,0:T(8,128)(2,1)S(1)}, u32[]{:S(2)}, u32[]{:S(2)}) collective-permute-start(bf16[256,256]{1,0:T(8,128)(2,1)S(1)} %next.2.refs_1_.refs_4_), channel_id=1, source_target_pairs={{0,32},{16,48},{32,64},{48,80},{64,96},{80,112},{96,0},{112,16},{1... | collective-permute-start | bytes 393224 | tf_op jit(solution)/shard_map/step1/ppermute | solution.py:291
  53.8 6.3 %copy-start = (bf16[2,512,1024]{2,1,0:T(8,128)(2,1)S(1)}, bf16[2,512,1024]{2,1,0:T(8,128)(2,1)}, u32[]{:S(2)}) copy-start(bf16[2,512,1024]{2,1,0:T(8,128)(2,1)} %get-tuple-element.22.refs_0_) | copy-start | bytes 6291460
  57.4 4.2 %collective-permute-start.10 = (bf16[1024,256]{1,0:T(8,128)(2,1)S(1)}, bf16[1024,256]{1,0:T(8,128)(2,1)S(1)}, u32[]{:S(2)}, u32[]{:S(2)}) collective-permute-start(bf16[1024,256]{1,0:T(8,128)(2,1)S(1)} %step_send.1), channel_id=1, source_target_pairs={{0,1},{1,0},{2,3},{3,2},{4,5},{5,4},{6,7},{7,6},{8,9},{9,8},{10,11... | collective-permute-start | bytes 1572872 | tf_op jit(solution)/shard_map/step2/ppermute | solution.py:285
  61.8 6.3 %collective-permute-start.11 = (bf16[256,256]{1,0:T(8,128)(2,1)S(1)}, bf16[256,256]{1,0:T(8,128)(2,1)S(1)}, u32[]{:S(2)}, u32[]{:S(2)}) collective-permute-start(bf16[256,256]{1,0:T(8,128)(2,1)S(1)} %get-tuple-element.31), channel_id=1, source_target_pairs={{0,8},{1,9},{2,10},{3,11},{4,12},{5,13},{6,14},{7,15},{8,0},{9,1},... | collective-permute-start | bytes 393224 | tf_op jit(solution)/shard_map/step2/ppermute | solution.py:288
  63.0 8.5 %collective-permute-start.12 = (bf16[256,256]{1,0:T(8,128)(2,1)S(1)}, bf16[256,256]{1,0:T(8,128)(2,1)S(1)}, u32[]{:S(2)}, u32[]{:S(2)}) collective-permute-start(bf16[256,256]{1,0:T(8,128)(2,1)S(1)} %get-tuple-element.32), channel_id=1, source_target_pairs={{0,4},{1,5},{2,6},{3,7},{4,8},{5,9},{6,10},{7,11},{8,12},{9,13},{1... | collective-permute-start | bytes 393224 | tf_op jit(solution)/shard_map/step2/ppermute | solution.py:288
  63.0 8.5 %collective-permute-start.13 = (bf16[256,256]{1,0:T(8,128)(2,1)S(1)}, bf16[256,256]{1,0:T(8,128)(2,1)S(1)}, u32[]{:S(2)}, u32[]{:S(2)}) collective-permute-start(bf16[256,256]{1,0:T(8,128)(2,1)S(1)} %get-tuple-element.33), channel_id=1, source_target_pairs={{0,12},{1,13},{2,14},{3,15},{4,0},{5,1},{6,2},{7,3},{8,4},{9,5},{1... | collective-permute-start | bytes 393224 | tf_op jit(solution)/shard_map/step2/ppermute | solution.py:288
  71.6 3.3 %collective-permute-start.16 = (bf16[128,256]{1,0:T(8,128)(2,1)S(1)}, bf16[128,256]{1,0:T(8,128)(2,1)S(1)}, u32[]{:S(2)}, u32[]{:S(2)}) collective-permute-start(bf16[128,256]{1,0:T(8,128)(2,1)S(1)} %get-tuple-element.34.own_ref), channel_id=1, source_target_pairs={{0,16},{16,0},{32,48},{48,32},{64,80},{80,64},{96,112},{112,96},{1... | collective-permute-start | bytes 196616 | tf_op jit(solution)/shard_map/step2/ppermute | solution.py:294
  72.0 4.3 %collective-permute-start.15 = (bf16[128,256]{1,0:T(8,128)(2,1)S(1)}, bf16[128,256]{1,0:T(8,128)(2,1)S(1)}, u32[]{:S(2)}, u32[]{:S(2)}) collective-permute-start(bf16[128,256]{1,0:T(8,128)(2,1)S(1)} %get-tuple-element.35), channel_id=1, source_target_pairs={{0,18},{1,19},{2,16},{3,17},{4,22},{5,23},{6,20},{7,21},{8,26},{9,... | collective-permute-start | bytes 196616 | tf_op jit(solution)/shard_map/step2/ppermute | solution.py:305
  74.3 4.6 %collective-permute-start.14 = (bf16[128,256]{1,0:T(8,128)(2,1)S(1)}, bf16[128,256]{1,0:T(8,128)(2,1)S(1)}, u32[]{:S(2)}, u32[]{:S(2)}) collective-permute-start(bf16[128,256]{1,0:T(8,128)(2,1)S(1)} %get-tuple-element.35), channel_id=1, source_target_pairs={{0,2},{1,3},{2,0},{3,1},{4,6},{5,7},{6,4},{7,5},{8,10},{9,11},{10,... | collective-permute-start | bytes 196616 | tf_op jit(solution)/shard_map/step2/ppermute | solution.py:297
  79.0 5.5 %collective-permute-start.19 = (bf16[256,256]{1,0:T(8,128)(2,1)S(1)}, bf16[256,256]{1,0:T(8,128)(2,1)S(1)}, u32[]{:S(2)}, u32[]{:S(2)}) collective-permute-start(bf16[256,256]{1,0:T(8,128)(2,1)S(1)} %next.3.refs_0_), channel_id=1, source_target_pairs={{0,64},{16,80},{32,96},{48,112},{64,0},{80,16},{96,32},{112,48},{1... | collective-permute-start | bytes 393224 | tf_op jit(solution)/shard_map/step2/ppermute | solution.py:291
  79.1 5.4 %collective-permute-start.18 = (bf16[256,256]{1,0:T(8,128)(2,1)S(1)}, bf16[256,256]{1,0:T(8,128)(2,1)S(1)}, u32[]{:S(2)}, u32[]{:S(2)}) collective-permute-start(bf16[256,256]{1,0:T(8,128)(2,1)S(1)} %next.3.refs_0_), channel_id=1, source_target_pairs={{0,96},{16,112},{32,0},{48,16},{64,32},{80,48},{96,64},{112,80},{1... | collective-permute-start | bytes 393224 | tf_op jit(solution)/shard_map/step2/ppermute | solution.py:291
  80.0 6.2 %collective-permute-start.17 = (bf16[256,256]{1,0:T(8,128)(2,1)S(1)}, bf16[256,256]{1,0:T(8,128)(2,1)S(1)}, u32[]{:S(2)}, u32[]{:S(2)}) collective-permute-start(bf16[256,256]{1,0:T(8,128)(2,1)S(1)} %next.3.refs_0_), channel_id=1, source_target_pairs={{0,32},{16,48},{32,64},{48,80},{64,96},{80,112},{96,0},{112,16},{1... | collective-permute-start | bytes 393224 | tf_op jit(solution)/shard_map/step2/ppermute | solution.py:291
  84.2 6.0 %copy-start.1 = (bf16[2,512,1024]{2,1,0:T(8,128)(2,1)S(1)}, bf16[2,512,1024]{2,1,0:T(8,128)(2,1)}, u32[]{:S(2)}) copy-start(bf16[2,512,1024]{2,1,0:T(8,128)(2,1)} %get-tuple-element.30.tile_ref) | copy-start | bytes 6291460
  87.0 4.8 %collective-permute-start.20 = (bf16[1024,256]{1,0:T(8,128)(2,1)S(1)}, bf16[1024,256]{1,0:T(8,128)(2,1)S(1)}, u32[]{:S(2)}, u32[]{:S(2)}) collective-permute-start(bf16[1024,256]{1,0:T(8,128)(2,1)S(1)} %last_send.1), channel_id=1, source_target_pairs={{0,1},{1,0},{2,3},{3,2},{4,5},{5,4},{6,7},{7,6},{8,9},{9,8},{10,11... | collective-permute-start | bytes 1572872 | tf_op jit(solution)/shard_map/step3/ppermute | solution.py:285
  104.7 16.4 %copy-start.2 = (bf16[128,256]{1,0:T(8,128)(2,1)}, bf16[128,256]{1,0:T(8,128)(2,1)S(1)}, u32[]{:S(2)}) copy-start(bf16[128,256]{1,0:T(8,128)(2,1)S(1)} %multiply_convert_fusion) | copy-start | bytes 196612

commit v6 on v5

--- a/solution.py
+++ b/solution.py
@@ -29,7 +29,7 @@
 BF16 = jnp.bfloat16
 
 
-def small_call(kernel, name, out_shapes, operands, scratch=(), flops=0, tile=None):
+def small_call(kernel, name, out_shapes, operands, scratch=(), flops=0, tile=None, far=False):
     tiles = [] if tile is None else [tile]
     outs = [jax.ShapeDtypeStruct(shape, BF16) for shape in out_shapes]
     sizes = sum(x.size for x in operands) + sum(x.size for x in outs)
@@ -37,7 +37,7 @@
         kernel,
         out_shape=outs,
         in_specs=[HBM] * len(tiles) + [VMEM] * len(operands),
-        out_specs=[VMEM] * len(outs),
+        out_specs=[VMEM] + [HBM if far else VMEM] * (len(outs) - 1),
         scratch_shapes=list(scratch),
         compiler_params=pltpu.CompilerParams(vmem_limit_bytes=PRODUCT_VMEM if tiles else SMALL_VMEM),
         cost_estimate=pl.CostEstimate(
@@ -180,21 +180,30 @@
 
 
 def fetch_kernel(halves, tile_ref, *refs):
-    *out_refs, sems = refs[-1 - len(halves) :]
+    *out_refs, held, sems, store_sems = refs[-3 - len(halves) :]
     rows = QUARTER // PIECES
-    copies = []
+    copies, stores = [], []
     for h, (out_ref, half) in enumerate(zip(out_refs, halves)):
         for q, quarter in enumerate(half):
             for k in range(PIECES):
                 part = pl.ds(k * rows, rows)
+                target = held.at[q, part] if h else out_ref.at[q, part]
                 copies.append(
-                    pltpu.make_async_copy(
-                        tile_ref.at[quarter, part], out_ref.at[q, part], sems.at[h, q, k]
-                    )
+                    pltpu.make_async_copy(tile_ref.at[quarter, part], target, sems.at[h, q, k])
                 )
                 copies[-1].start()
-    for copy in copies:
+                if h:
+                    store = pltpu.make_async_copy(
+                        target, out_ref.at[q, part], store_sems.at[q, k]
+                    )
+                    stores.append((len(copies) - 1, store))
+    stored = dict(stores)
+    for n, copy in enumerate(copies):
         copy.wait()
+        if n in stored:
+            stored[n].start()
+    for _, store in stores:
+        store.wait()
 
 
 def step_kernel(first, keep, *refs):
@@ -309,11 +318,13 @@
         pltpu.VMEM((HALF, HALF, 2, RUN, width), F32),
     ]
     sems = pltpu.SemaphoreType.DMA((2, 2, PIECES))
+    room = [pltpu.VMEM((2, QUARTER, COLBLK * BLOCK), BF16), sems]
+    room.append(pltpu.SemaphoreType.DMA((2, PIECES)))
     quarters = (2, QUARTER, COLBLK * BLOCK)
 
     def fetch(tile, *halves, after=()):
         kernel = functools.partial(fetch_kernel, halves)
-        return small_call(kernel, "fetch", [quarters] * len(halves), after, [sems], 0, tile)
+        return small_call(kernel, "fetch", [quarters] * len(halves), after, room, 0, tile, True)
 
     def product(kernel, name, fetched, operands, more=()):
         wide = (half_rows, width)

time: 121 us -> 121 us (level)
  no operation moved by 1% of the time
where the time goes in v6:
time: 121 us
  starting transfers between devices  37.2 us (31%)
  waiting for transfers between devices  31 us (26%)
  blocking collectives  28 us (23%)
  Pallas kernels  22.2 us (18%)
  between operations  1.5 us (1%)
    all_to_all x2, blocking collectives, exchange(): lax.all_to_all(parts, axes, split_axis=0, concat_axis=0, tiled=True, axis...  28 us
    pallas_call x17, Pallas kernels, small_call(): pl.pallas_call(kernel, out_shape=outs, in_specs=[HBM] * len(tiles) + [VME...  14.6 us
    ppermute x6, waiting for transfers between devices, along_x(): lax.ppermute(x, 'col', [(i, (i + 4 * k) % col_count) for i in range(col_c...  11.9 us
    all_to_all x1, starting transfers between devices, exchange(): lax.all_to_all(parts, axes, split_axis=0, concat_axis=0, tiled=True, axis...  11.5 us
    ppermute x6, starting transfers between devices, along_x(): lax.ppermute(x, 'col', [(i, (i + 4 * k) % col_count) for i in range(col_c...  7.75 us
    ppermute x3, starting transfers between devices, other_core(): return lax.ppermute(x, 'col', [(i, i ^ 1) for i in range(col_count)])  7.16 us
    pallas_call x1, Pallas kernels, merge(): pl.pallas_call(merge_kernel, out_shape=jax.ShapeDtypeStruct((ROOM,) + qua...  5.81 us
    ppermute x6, waiting for transfers between devices, along_y(): lax.ppermute(x, 'row', [(i, (i + 2 * k) % row_count) for i in range(row_c...  5.75 us
  transfers between devices with their start and end apart: 22, of which 14 were waited for; matrix products, arithmetic and copies ran while one was open for 0% of the time, Pallas kernels for 15%

profile of v6, /device:TPU:1, one launch (start us, length us, event | category | flops | bytes accessed | tf_op | source)
XLA Modules:
  0.0 121.1 jit_solution(13743074727774880370)
XLA Ops:
  0.6 1.7 %copies.1 = bf16[8,128,256]{2,1,0:T(8,128)(2,1)} custom-call(bf16[128,256]{1,0:T(8,128)(2,1)} %own_ref.1), custom_call_target="tpu_custom_call" | custom-call | tf_op jit(solution)/shard_map/deal/copies/pallas_call | solution.py:157
  2.4 11.5 %all-to-all-start = ((bf16[128,8,256]{2,1,0:T(8,128)(2,1)}), bf16[128,8,256]{2,1,0:T(8,128)(2,1)S(1)}, u32[]{:S(2)}, u32[]{:S(2)}) async-start(bf16[128,8,256]{2,1,0:T(8,128)(2,1)} %bitcast.14), calls=%async_computation | async-start | bytes 1048576 | tf_op jit(solution)/shard_map/deal/all_to_all | solution.py:289
  14.5 5.8 %merge_blocks.1.tile_ref = bf16[16,512,1024]{2,1,0:T(8,128)(2,1)} custom-call(s32[256]{0:T(256)} %bitcast.15, s32[256]{0:T(256)} %bitcast.16, s32[1]{0:T(128)} %bitcast.9.stored_ref, bf16[256,128,128]{2,1,0:T(8,128)(2,1)} %bitcast.13), custom_call_target="tpu_custom_call" | custom-call | flops 4194304 | bytes 12582912 | tf_op jit(solution)/shard_map/merge/merge_blocks/pallas_call | solution.py:117
  20.3 1.6 %fetch.5.refs_0_ = bf16[2,512,1024]{2,1,0:T(8,128)(2,1)S(1)} custom-call(bf16[16,512,1024]{2,1,0:T(8,128)(2,1)} %merge_blocks.1.tile_ref), custom_call_target="tpu_custom_call" | custom-call | bytes 2097152 | tf_op jit(solution)/shard_map/step1/fetch/pallas_call | solution.py:36
  22.0 5.4 %all-to-all-done = bf16[128,8,256]{2,1,0:T(8,128)(2,1)S(1)} async-done(((bf16[128,8,256]{2,1,0:T(8,128)(2,1)}), bf16[128,8,256]{2,1,0:T(8,128)(2,1)S(1)}, u32[]{:S(2)}, u32[]{:S(2)}) %all-to-all-start) | async-done | bytes 524320 | tf_op jit(solution)/shard_map/deal/all_to_all | solution.py:289
  27.4 0.8 first_send.1
  28.2 1.2 %collective-permute-start = (bf16[1024,256]{1,0:T(8,128)(2,1)S(1)}, bf16[1024,256]{1,0:T(8,128)(2,1)S(1)}, u32[]{:S(2)}, u32[]{:S(2)}) collective-permute-start(bf16[1024,256]{1,0:T(8,128)(2,1)S(1)} %get-tuple-element.20), channel_id=1, source_target_pairs={{0,1},{1,0},{2,3},{3,2},{4,5},{5,4},{6,7},{7,6},{8,9},{9,8},{10,11... | collective-permute-start | bytes 1572872 | tf_op jit(solution)/shard_map/step1/ppermute | solution.py:294
  29.4 1.6 %fetch.4.refs_0_ = bf16[2,512,1024]{2,1,0:T(8,128)(2,1)S(1)} custom-call(bf16[16,512,1024]{2,1,0:T(8,128)(2,1)} %merge_blocks.1.tile_ref), custom_call_target="tpu_custom_call" | custom-call | bytes 2097152 | tf_op jit(solution)/shard_map/step1/fetch/pallas_call | solution.py:36
  31.0 0.8 first_keep.1.a_ref
  31.8 0.0 collective-permute-done.b_ref
  31.8 0.1 add.3
  32.0 1.1 collective-permute-start.1
  33.1 0.4 collective-permute-start.2
  33.5 2.3 %collective-permute-start.3 = (bf16[256,256]{1,0:T(8,128)(2,1)S(1)}, bf16[256,256]{1,0:T(8,128)(2,1)S(1)}, u32[]{:S(2)}, u32[]{:S(2)}) collective-permute-start(bf16[256,256]{1,0:T(8,128)(2,1)S(1)} %get-tuple-element.25), channel_id=1, source_target_pairs={{0,12},{1,13},{2,14},{3,15},{4,0},{5,1},{6,2},{7,3},{8,4},{9,5},{1... | collective-permute-start | bytes 393224 | tf_op jit(solution)/shard_map/step1/ppermute | solution.py:297
  35.8 2.9 %collective-permute-done.1.b_ref = bf16[256,256]{1,0:T(8,128)(2,1)S(1)} collective-permute-done((bf16[256,256]{1,0:T(8,128)(2,1)S(1)}, bf16[256,256]{1,0:T(8,128)(2,1)S(1)}, u32[]{:S(2)}, u32[]{:S(2)}) %collective-permute-start.1) | collective-permute-done | bytes 131104 | tf_op jit(solution)/shard_map/step1/ppermute | solution.py:297
  38.7 3.1 %collective-permute-done.2.c_ref = bf16[256,256]{1,0:T(8,128)(2,1)S(1)} collective-permute-done((bf16[256,256]{1,0:T(8,128)(2,1)S(1)}, bf16[256,256]{1,0:T(8,128)(2,1)S(1)}, u32[]{:S(2)}, u32[]{:S(2)}) %collective-permute-start.2) | collective-permute-done | bytes 131104 | tf_op jit(solution)/shard_map/step1/ppermute | solution.py:297
  41.8 0.0 collective-permute-done.3.d_ref
  41.8 0.1 sum_x.2
  41.9 0.2 collective-permute-start.6
  42.1 0.9 collective-permute-start.5
  43.0 2.2 %collective-permute-start.4 = (bf16[128,256]{1,0:T(8,128)(2,1)S(1)}, bf16[128,256]{1,0:T(8,128)(2,1)S(1)}, u32[]{:S(2)}, u32[]{:S(2)}) collective-permute-start(bf16[128,256]{1,0:T(8,128)(2,1)S(1)} %get-tuple-element.27), channel_id=1, source_target_pairs={{0,2},{1,3},{2,0},{3,1},{4,6},{5,7},{6,4},{7,5},{8,10},{9,11},{10,... | collective-permute-start | bytes 196616 | tf_op jit(solution)/shard_map/step1/ppermute | solution.py:306
  45.2 1.2 %collective-permute-done.5.far_ref = bf16[128,256]{1,0:T(8,128)(2,1)S(1)} collective-permute-done((bf16[128,256]{1,0:T(8,128)(2,1)S(1)}, bf16[128,256]{1,0:T(8,128)(2,1)S(1)}, u32[]{:S(2)}, u32[]{:S(2)}) %collective-permute-start.5) | collective-permute-done | bytes 65568 | tf_op jit(solution)/shard_map/step1/ppermute | solution.py:314
  46.4 1.2 %collective-permute-done.4.arrived_ref = bf16[128,256]{1,0:T(8,128)(2,1)S(1)} collective-permute-done((bf16[128,256]{1,0:T(8,128)(2,1)S(1)}, bf16[128,256]{1,0:T(8,128)(2,1)S(1)}, u32[]{:S(2)}, u32[]{:S(2)}) %collective-permute-start.4) | collective-permute-done | bytes 65568 | tf_op jit(solution)/shard_map/step1/ppermute | solution.py:306
  47.7 0.5 collective-permute-start.9
  48.2 1.9 %collective-permute-start.8 = (bf16[256,256]{1,0:T(8,128)(2,1)S(1)}, bf16[256,256]{1,0:T(8,128)(2,1)S(1)}, u32[]{:S(2)}, u32[]{:S(2)}) collective-permute-start(bf16[256,256]{1,0:T(8,128)(2,1)S(1)} %next.2.refs_1_.refs_4_), channel_id=1, source_target_pairs={{0,96},{16,112},{32,0},{48,16},{64,32},{80,48},{96,64},{112,80},{1... | collective-permute-start | bytes 393224 | tf_op jit(solution)/shard_map/step1/ppermute | solution.py:300
  50.2 0.0 collective-permute-start.7
  50.2 3.1 %fetch.6 = (bf16[2,512,1024]{2,1,0:T(8,128)(2,1)S(1)}, bf16[2,512,1024]{2,1,0:T(8,128)(2,1)}) custom-call(bf16[16,512,1024]{2,1,0:T(8,128)(2,1)} %merge_blocks.1.tile_ref, bf16[256,256]{1,0:T(8,128)(2,1)S(1)} %get-tuple-element.21.refs_0_.a_ref), custom_call_target="tpu_custom_call" | custom-call | bytes 4325376 | tf_op jit(solution)/shard_map/step1/fetch/pallas_call | solution.py:36
  53.3 0.0 collective-permute-done.9.refs_4_
  53.3 3.3 %collective-permute-done.7.refs_2_ = bf16[256,256]{1,0:T(8,128)(2,1)S(1)} collective-permute-done((bf16[256,256]{1,0:T(8,128)(2,1)S(1)}, bf16[256,256]{1,0:T(8,128)(2,1)S(1)}, u32[]{:S(2)}, u32[]{:S(2)}) %collective-permute-start.7) | collective-permute-done | bytes 131104 | tf_op jit(solution)/shard_map/step1/ppermute | solution.py:300
  56.6 0.8 step_send.1
  57.4 2.7 %collective-permute-start.10 = (bf16[1024,256]{1,0:T(8,128)(2,1)S(1)}, bf16[1024,256]{1,0:T(8,128)(2,1)S(1)}, u32[]{:S(2)}, u32[]{:S(2)}) collective-permute-start(bf16[1024,256]{1,0:T(8,128)(2,1)S(1)} %step_send.1), channel_id=1, source_target_pairs={{0,1},{1,0},{2,3},{3,2},{4,5},{5,4},{6,7},{7,6},{8,9},{9,8},{10,11... | collective-permute-start | bytes 1572872 | tf_op jit(solution)/shard_map/step2/ppermute | solution.py:294
  60.1 0.8 step_keep.1.a_ref
  60.9 0.8 collective-permute-done.10.b_ref
  61.6 0.1 add.4
  61.8 1.3 %collective-permute-start.11 = (bf16[256,256]{1,0:T(8,128)(2,1)S(1)}, bf16[256,256]{1,0:T(8,128)(2,1)S(1)}, u32[]{:S(2)}, u32[]{:S(2)}) collective-permute-start(bf16[256,256]{1,0:T(8,128)(2,1)S(1)} %get-tuple-element.31), channel_id=1, source_target_pairs={{0,8},{1,9},{2,10},{3,11},{4,12},{5,13},{6,14},{7,15},{8,0},{9,1},... | collective-permute-start | bytes 393224 | tf_op jit(solution)/shard_map/step2/ppermute | solution.py:297
  63.0 0.0 collective-permute-start.12
  63.0 2.7 %collective-permute-start.13 = (bf16[256,256]{1,0:T(8,128)(2,1)S(1)}, bf16[256,256]{1,0:T(8,128)(2,1)S(1)}, u32[]{:S(2)}, u32[]{:S(2)}) collective-permute-start(bf16[256,256]{1,0:T(8,128)(2,1)S(1)} %get-tuple-element.33), channel_id=1, source_target_pairs={{0,12},{1,13},{2,14},{3,15},{4,0},{5,1},{6,2},{7,3},{8,4},{9,5},{1... | collective-permute-start | bytes 393224 | tf_op jit(solution)/shard_map/step2/ppermute | solution.py:297
  65.7 2.4 %collective-permute-done.11.b_ref = bf16[256,256]{1,0:T(8,128)(2,1)S(1)} collective-permute-done((bf16[256,256]{1,0:T(8,128)(2,1)S(1)}, bf16[256,256]{1,0:T(8,128)(2,1)S(1)}, u32[]{:S(2)}, u32[]{:S(2)}) %collective-permute-start.11) | collective-permute-done | bytes 131104 | tf_op jit(solution)/shard_map/step2/ppermute | solution.py:297
  68.0 3.5 %collective-permute-done.12.c_ref = bf16[256,256]{1,0:T(8,128)(2,1)S(1)} collective-permute-done((bf16[256,256]{1,0:T(8,128)(2,1)S(1)}, bf16[256,256]{1,0:T(8,128)(2,1)S(1)}, u32[]{:S(2)}, u32[]{:S(2)}) %collective-permute-start.12) | collective-permute-done | bytes 131104 | tf_op jit(solution)/shard_map/step2/ppermute | solution.py:297
  71.6 0.1 sum_x.3
  71.6 0.4 collective-permute-start.16
  72.0 2.4 %collective-permute-start.15 = (bf16[128,256]{1,0:T(8,128)(2,1)S(1)}, bf16[128,256]{1,0:T(8,128)(2,1)S(1)}, u32[]{:S(2)}, u32[]{:S(2)}) collective-permute-start(bf16[128,256]{1,0:T(8,128)(2,1)S(1)} %get-tuple-element.35), channel_id=1, source_target_pairs={{0,18},{1,19},{2,16},{3,17},{4,22},{5,23},{6,20},{7,21},{8,26},{9,... | collective-permute-start | bytes 196616 | tf_op jit(solution)/shard_map/step2/ppermute | solution.py:314
  74.4 0.7 collective-permute-start.14
  75.0 1.3 %collective-permute-done.15.far_ref = bf16[128,256]{1,0:T(8,128)(2,1)S(1)} collective-permute-done((bf16[128,256]{1,0:T(8,128)(2,1)S(1)}, bf16[128,256]{1,0:T(8,128)(2,1)S(1)}, u32[]{:S(2)}, u32[]{:S(2)}) %collective-permute-start.15) | collective-permute-done | bytes 65568 | tf_op jit(solution)/shard_map/step2/ppermute | solution.py:314
  76.3 2.6 %collective-permute-done.14.arrived_ref = bf16[128,256]{1,0:T(8,128)(2,1)S(1)} collective-permute-done((bf16[128,256]{1,0:T(8,128)(2,1)S(1)}, bf16[128,256]{1,0:T(8,128)(2,1)S(1)}, u32[]{:S(2)}, u32[]{:S(2)}) %collective-permute-start.14) | collective-permute-done | bytes 65568 | tf_op jit(solution)/shard_map/step2/ppermute | solution.py:306
  79.0 0.1 next.3.refs_0_
  79.0 0.1 collective-permute-start.19
  79.1 1.0 collective-permute-start.18
  80.1 0.6 collective-permute-start.17
  80.7 3.1 %fetch.7 = (bf16[2,512,1024]{2,1,0:T(8,128)(2,1)S(1)}, bf16[2,512,1024]{2,1,0:T(8,128)(2,1)}) custom-call(bf16[16,512,1024]{2,1,0:T(8,128)(2,1)} %merge_blocks.1.tile_ref, bf16[256,256]{1,0:T(8,128)(2,1)S(1)} %get-tuple-element.29.refs_0_.a_ref), custom_call_target="tpu_custom_call" | custom-call | bytes 4325376 | tf_op jit(solution)/shard_map/step2/fetch/pallas_call | solution.py:36
  83.8 0.7 collective-permute-done.19.refs_3_
  84.5 1.7 %collective-permute-done.17.refs_1_ = bf16[256,256]{1,0:T(8,128)(2,1)S(1)} collective-permute-done((bf16[256,256]{1,0:T(8,128)(2,1)S(1)}, bf16[256,256]{1,0:T(8,128)(2,1)S(1)}, u32[]{:S(2)}, u32[]{:S(2)}) %collective-permute-start.17) | collective-permute-done | bytes 131104 | tf_op jit(solution)/shard_map/step2/ppermute | solution.py:300
  86.2 0.8 last_send.1
  87.0 3.2 %collective-permute-start.20 = (bf16[1024,256]{1,0:T(8,128)(2,1)S(1)}, bf16[1024,256]{1,0:T(8,128)(2,1)S(1)}, u32[]{:S(2)}, u32[]{:S(2)}) collective-permute-start(bf16[1024,256]{1,0:T(8,128)(2,1)S(1)} %last_send.1), channel_id=1, source_target_pairs={{0,1},{1,0},{2,3},{3,2},{4,5},{5,4},{6,7},{7,6},{8,9},{9,8},{10,11... | collective-permute-start | bytes 1572872 | tf_op jit(solution)/shard_map/step3/ppermute | solution.py:294
  90.3 0.8 last_keep.1.a_ref
  91.0 0.8 collective-permute-done.20.b_ref
  91.8 0.1 add.5
  91.9 12.7 %all_to_all.15 = bf16[8,128,256]{2,1,0:T(8,128)(2,1)S(1)} all-to-all(bf16[8,128,256]{2,1,0:T(8,128)(2,1)S(1)} %bitcast.12), channel_id=1, replica_groups={{0,2,4,6,8,10,12,14},{1,3,5,7,9,11,13,15},{16,18,20,22,24,26,28,30},{17..., dimensions={0} | all-to-all | bytes 1048576 | tf_op jit(solution)/shard_map/step3/all_to_all | solution.py:289
  104.6 0.1 convert_reduce_fusion
  104.7 0.0 copy-start.2
  104.7 0.2 fusion
  104.9 0.1 reshape.19
  105.0 15.4 %all_to_all.16 = bf16[128,2,256]{2,1,0:T(2,128)(2,1)S(1)} all-to-all(bf16[128,2,256]{2,1,0:T(2,128)(2,1)S(1)} %reshape.19), channel_id=1, replica_groups=mesh['row'=8,'col'=16] {'row','col'}, dimensions={0} | all-to-all | bytes 262144 | tf_op jit(solution)/shard_map/gram/all_to_all | solution.py:289
  120.3 0.7 convert_reduce_fusion.1
  (12 shorter events, 0.1 us)
Async XLA Ops:
  2.4 25.0 %all-to-all-start = ((bf16[128,8,256]{2,1,0:T(8,128)(2,1)}), bf16[128,8,256]{2,1,0:T(8,128)(2,1)S(1)}, u32[]{:S(2)}, u32[]{:S(2)}) async-start(bf16[128,8,256]{2,1,0:T(8,128)(2,1)} %bitcast.14), calls=%async_computation | async-start | bytes 1048576 | tf_op jit(solution)/shard_map/deal/all_to_all | solution.py:289
  28.2 3.6 %collective-permute-start = (bf16[1024,256]{1,0:T(8,128)(2,1)S(1)}, bf16[1024,256]{1,0:T(8,128)(2,1)S(1)}, u32[]{:S(2)}, u32[]{:S(2)}) collective-permute-start(bf16[1024,256]{1,0:T(8,128)(2,1)S(1)} %get-tuple-element.20), channel_id=1, source_target_pairs={{0,1},{1,0},{2,3},{3,2},{4,5},{5,4},{6,7},{7,6},{8,9},{9,8},{10,11... | collective-permute-start | bytes 1572872 | tf_op jit(solution)/shard_map/step1/ppermute | solution.py:294
  32.0 6.7 %collective-permute-start.1 = (bf16[256,256]{1,0:T(8,128)(2,1)S(1)}, bf16[256,256]{1,0:T(8,128)(2,1)S(1)}, u32[]{:S(2)}, u32[]{:S(2)}) collective-permute-start(bf16[256,256]{1,0:T(8,128)(2,1)S(1)} %get-tuple-element.23), channel_id=1, source_target_pairs={{0,8},{1,9},{2,10},{3,11},{4,12},{5,13},{6,14},{7,15},{8,0},{9,1},... | collective-permute-start | bytes 393224 | tf_op jit(solution)/shard_map/step1/ppermute | solution.py:297
  33.1 8.7 %collective-permute-start.2 = (bf16[256,256]{1,0:T(8,128)(2,1)S(1)}, bf16[256,256]{1,0:T(8,128)(2,1)S(1)}, u32[]{:S(2)}, u32[]{:S(2)}) collective-permute-start(bf16[256,256]{1,0:T(8,128)(2,1)S(1)} %get-tuple-element.24), channel_id=1, source_target_pairs={{0,4},{1,5},{2,6},{3,7},{4,8},{5,9},{6,10},{7,11},{8,12},{9,13},{1... | collective-permute-start | bytes 393224 | tf_op jit(solution)/shard_map/step1/ppermute | solution.py:297
  33.5 8.3 %collective-permute-start.3 = (bf16[256,256]{1,0:T(8,128)(2,1)S(1)}, bf16[256,256]{1,0:T(8,128)(2,1)S(1)}, u32[]{:S(2)}, u32[]{:S(2)}) collective-permute-start(bf16[256,256]{1,0:T(8,128)(2,1)S(1)} %get-tuple-element.25), channel_id=1, source_target_pairs={{0,12},{1,13},{2,14},{3,15},{4,0},{5,1},{6,2},{7,3},{8,4},{9,5},{1... | collective-permute-start | bytes 393224 | tf_op jit(solution)/shard_map/step1/ppermute | solution.py:297
  41.9 3.3 %collective-permute-start.6 = (bf16[128,256]{1,0:T(8,128)(2,1)S(1)}, bf16[128,256]{1,0:T(8,128)(2,1)S(1)}, u32[]{:S(2)}, u32[]{:S(2)}) collective-permute-start(bf16[128,256]{1,0:T(8,128)(2,1)S(1)} %get-tuple-element.26.own_ref), channel_id=1, source_target_pairs={{0,16},{16,0},{32,48},{48,32},{64,80},{80,64},{96,112},{112,96},{1... | collective-permute-start | bytes 196616 | tf_op jit(solution)/shard_map/step1/ppermute | solution.py:303
  42.1 4.3 %collective-permute-start.5 = (bf16[128,256]{1,0:T(8,128)(2,1)S(1)}, bf16[128,256]{1,0:T(8,128)(2,1)S(1)}, u32[]{:S(2)}, u32[]{:S(2)}) collective-permute-start(bf16[128,256]{1,0:T(8,128)(2,1)S(1)} %get-tuple-element.27), channel_id=1, source_target_pairs={{0,18},{1,19},{2,16},{3,17},{4,22},{5,23},{6,20},{7,21},{8,26},{9,... | collective-permute-start | bytes 196616 | tf_op jit(solution)/shard_map/step1/ppermute | solution.py:314
  43.0 4.7 %collective-permute-start.4 = (bf16[128,256]{1,0:T(8,128)(2,1)S(1)}, bf16[128,256]{1,0:T(8,128)(2,1)S(1)}, u32[]{:S(2)}, u32[]{:S(2)}) collective-permute-start(bf16[128,256]{1,0:T(8,128)(2,1)S(1)} %get-tuple-element.27), channel_id=1, source_target_pairs={{0,2},{1,3},{2,0},{3,1},{4,6},{5,7},{6,4},{7,5},{8,10},{9,11},{10,... | collective-permute-start | bytes 196616 | tf_op jit(solution)/shard_map/step1/ppermute | solution.py:306
  47.7 5.6 %collective-permute-start.9 = (bf16[256,256]{1,0:T(8,128)(2,1)S(1)}, bf16[256,256]{1,0:T(8,128)(2,1)S(1)}, u32[]{:S(2)}, u32[]{:S(2)}) collective-permute-start(bf16[256,256]{1,0:T(8,128)(2,1)S(1)} %next.2.refs_1_.refs_4_), channel_id=1, source_target_pairs={{0,64},{16,80},{32,96},{48,112},{64,0},{80,16},{96,32},{112,48},{1... | collective-permute-start | bytes 393224 | tf_op jit(solution)/shard_map/step1/ppermute | solution.py:300
  48.2 5.1 %collective-permute-start.8 = (bf16[256,256]{1,0:T(8,128)(2,1)S(1)}, bf16[256,256]{1,0:T(8,128)(2,1)S(1)}, u32[]{:S(2)}, u32[]{:S(2)}) collective-permute-start(bf16[256,256]{1,0:T(8,128)(2,1)S(1)} %next.2.refs_1_.refs_4_), channel_id=1, source_target_pairs={{0,96},{16,112},{32,0},{48,16},{64,32},{80,48},{96,64},{112,80},{1... | collective-permute-start | bytes 393224 | tf_op jit(solution)/shard_map/step1/ppermute | solution.py:300
  50.2 6.4 %collective-permute-start.7 = (bf16[256,256]{1,0:T(8,128)(2,1)S(1)}, bf16[256,256]{1,0:T(8,128)(2,1)S(1)}, u32[]{:S(2)}, u32[]{:S(2)}) collective-permute-start(bf16[256,256]{1,0:T(8,128)(2,1)S(1)} %next.2.refs_1_.refs_4_), channel_id=1, source_target_pairs={{0,32},{16,48},{32,64},{48,80},{64,96},{80,112},{96,0},{112,16},{1... | collective-permute-start | bytes 393224 | tf_op jit(solution)/shard_map/step1/ppermute | solution.py:300
  53.3 6.8 %copy-start = (bf16[2,512,1024]{2,1,0:T(8,128)(2,1)S(1)}, bf16[2,512,1024]{2,1,0:T(8,128)(2,1)}, u32[]{:S(2)}) copy-start(bf16[2,512,1024]{2,1,0:T(8,128)(2,1)} %get-tuple-element.22.refs_0_) | copy-start | bytes 6291460
  57.4 4.2 %collective-permute-start.10 = (bf16[1024,256]{1,0:T(8,128)(2,1)S(1)}, bf16[1024,256]{1,0:T(8,128)(2,1)S(1)}, u32[]{:S(2)}, u32[]{:S(2)}) collective-permute-start(bf16[1024,256]{1,0:T(8,128)(2,1)S(1)} %step_send.1), channel_id=1, source_target_pairs={{0,1},{1,0},{2,3},{3,2},{4,5},{5,4},{6,7},{7,6},{8,9},{9,8},{10,11... | collective-permute-start | bytes 1572872 | tf_op jit(solution)/shard_map/step2/ppermute | solution.py:294
  61.8 6.3 %collective-permute-start.11 = (bf16[256,256]{1,0:T(8,128)(2,1)S(1)}, bf16[256,256]{1,0:T(8,128)(2,1)S(1)}, u32[]{:S(2)}, u32[]{:S(2)}) collective-permute-start(bf16[256,256]{1,0:T(8,128)(2,1)S(1)} %get-tuple-element.31), channel_id=1, source_target_pairs={{0,8},{1,9},{2,10},{3,11},{4,12},{5,13},{6,14},{7,15},{8,0},{9,1},... | collective-permute-start | bytes 393224 | tf_op jit(solution)/shard_map/step2/ppermute | solution.py:297
  63.0 8.6 %collective-permute-start.12 = (bf16[256,256]{1,0:T(8,128)(2,1)S(1)}, bf16[256,256]{1,0:T(8,128)(2,1)S(1)}, u32[]{:S(2)}, u32[]{:S(2)}) collective-permute-start(bf16[256,256]{1,0:T(8,128)(2,1)S(1)} %get-tuple-element.32), channel_id=1, source_target_pairs={{0,4},{1,5},{2,6},{3,7},{4,8},{5,9},{6,10},{7,11},{8,12},{9,13},{1... | collective-permute-start | bytes 393224 | tf_op jit(solution)/shard_map/step2/ppermute | solution.py:297
  63.0 8.6 %collective-permute-start.13 = (bf16[256,256]{1,0:T(8,128)(2,1)S(1)}, bf16[256,256]{1,0:T(8,128)(2,1)S(1)}, u32[]{:S(2)}, u32[]{:S(2)}) collective-permute-start(bf16[256,256]{1,0:T(8,128)(2,1)S(1)} %get-tuple-element.33), channel_id=1, source_target_pairs={{0,12},{1,13},{2,14},{3,15},{4,0},{5,1},{6,2},{7,3},{8,4},{9,5},{1... | collective-permute-start | bytes 393224 | tf_op jit(solution)/shard_map/step2/ppermute | solution.py:297
  71.6 3.4 %collective-permute-start.16 = (bf16[128,256]{1,0:T(8,128)(2,1)S(1)}, bf16[128,256]{1,0:T(8,128)(2,1)S(1)}, u32[]{:S(2)}, u32[]{:S(2)}) collective-permute-start(bf16[128,256]{1,0:T(8,128)(2,1)S(1)} %get-tuple-element.34.own_ref), channel_id=1, source_target_pairs={{0,16},{16,0},{32,48},{48,32},{64,80},{80,64},{96,112},{112,96},{1... | collective-permute-start | bytes 196616 | tf_op jit(solution)/shard_map/step2/ppermute | solution.py:303
  72.0 4.3 %collective-permute-start.15 = (bf16[128,256]{1,0:T(8,128)(2,1)S(1)}, bf16[128,256]{1,0:T(8,128)(2,1)S(1)}, u32[]{:S(2)}, u32[]{:S(2)}) collective-permute-start(bf16[128,256]{1,0:T(8,128)(2,1)S(1)} %get-tuple-element.35), channel_id=1, source_target_pairs={{0,18},{1,19},{2,16},{3,17},{4,22},{5,23},{6,20},{7,21},{8,26},{9,... | collective-permute-start | bytes 196616 | tf_op jit(solution)/shard_map/step2/ppermute | solution.py:314
  74.4 4.6 %collective-permute-start.14 = (bf16[128,256]{1,0:T(8,128)(2,1)S(1)}, bf16[128,256]{1,0:T(8,128)(2,1)S(1)}, u32[]{:S(2)}, u32[]{:S(2)}) collective-permute-start(bf16[128,256]{1,0:T(8,128)(2,1)S(1)} %get-tuple-element.35), channel_id=1, source_target_pairs={{0,2},{1,3},{2,0},{3,1},{4,6},{5,7},{6,4},{7,5},{8,10},{9,11},{10,... | collective-permute-start | bytes 196616 | tf_op jit(solution)/shard_map/step2/ppermute | solution.py:306
  79.0 5.5 %collective-permute-start.19 = (bf16[256,256]{1,0:T(8,128)(2,1)S(1)}, bf16[256,256]{1,0:T(8,128)(2,1)S(1)}, u32[]{:S(2)}, u32[]{:S(2)}) collective-permute-start(bf16[256,256]{1,0:T(8,128)(2,1)S(1)} %next.3.refs_0_), channel_id=1, source_target_pairs={{0,64},{16,80},{32,96},{48,112},{64,0},{80,16},{96,32},{112,48},{1... | collective-permute-start | bytes 393224 | tf_op jit(solution)/shard_map/step2/ppermute | solution.py:300
  79.1 5.4 %collective-permute-start.18 = (bf16[256,256]{1,0:T(8,128)(2,1)S(1)}, bf16[256,256]{1,0:T(8,128)(2,1)S(1)}, u32[]{:S(2)}, u32[]{:S(2)}) collective-permute-start(bf16[256,256]{1,0:T(8,128)(2,1)S(1)} %next.3.refs_0_), channel_id=1, source_target_pairs={{0,96},{16,112},{32,0},{48,16},{64,32},{80,48},{96,64},{112,80},{1... | collective-permute-start | bytes 393224 | tf_op jit(solution)/shard_map/step2/ppermute | solution.py:300
  80.1 6.2 %collective-permute-start.17 = (bf16[256,256]{1,0:T(8,128)(2,1)S(1)}, bf16[256,256]{1,0:T(8,128)(2,1)S(1)}, u32[]{:S(2)}, u32[]{:S(2)}) collective-permute-start(bf16[256,256]{1,0:T(8,128)(2,1)S(1)} %next.3.refs_0_), channel_id=1, source_target_pairs={{0,32},{16,48},{32,64},{48,80},{64,96},{80,112},{96,0},{112,16},{1... | collective-permute-start | bytes 393224 | tf_op jit(solution)/shard_map/step2/ppermute | solution.py:300
  83.8 6.5 %copy-start.1 = (bf16[2,512,1024]{2,1,0:T(8,128)(2,1)S(1)}, bf16[2,512,1024]{2,1,0:T(8,128)(2,1)}, u32[]{:S(2)}) copy-start(bf16[2,512,1024]{2,1,0:T(8,128)(2,1)} %get-tuple-element.30.tile_ref) | copy-start | bytes 6291460
  87.0 4.8 %collective-permute-start.20 = (bf16[1024,256]{1,0:T(8,128)(2,1)S(1)}, bf16[1024,256]{1,0:T(8,128)(2,1)S(1)}, u32[]{:S(2)}, u32[]{:S(2)}) collective-permute-start(bf16[1024,256]{1,0:T(8,128)(2,1)S(1)} %last_send.1), channel_id=1, source_target_pairs={{0,1},{1,0},{2,3},{3,2},{4,5},{5,4},{6,7},{7,6},{8,9},{9,8},{10,11... | collective-permute-start | bytes 1572872 | tf_op jit(solution)/shard_map/step3/ppermute | solution.py:294
  104.7 16.4 %copy-start.2 = (bf16[128,256]{1,0:T(8,128)(2,1)}, bf16[128,256]{1,0:T(8,128)(2,1)S(1)}, u32[]{:S(2)}) copy-start(bf16[128,256]{1,0:T(8,128)(2,1)S(1)} %multiply_convert_fusion) | copy-start | bytes 196612
